TPU v7x, 32 devices: a whole 2x2x4 slice. The times are simulated.
32 devices in a mesh: dp: 4 (over x, core), tensor: 8 (over z, y).
Axes of the slice: x: 2, y: 2, z: 4, core: 2. Of those that a mesh axis runs over, the one named last changes fastest.
Arguments:
- queries: bfloat16 [4, 4, 64, 8192], P('dp', None, None, 'tensor'), may hold values from -64 to 64
- slot_keys_values: bfloat16 [4, 4, 2, 64, 1024], P('dp'), may hold values from -8 to 8
- segment_ids: int32 [4, 4, 64], P('dp'), may hold values from 0 to 3, never falling along the last dimension, each value on 1 to 32 neighbouring positions
- residual_in: bfloat16 [4, 4, 64, 4224], P('dp', None, None, 'tensor'), may hold values from -6 to 6
- cotangent: bfloat16 [4, 4, 64, 4224], P('dp', None, None, 'tensor'), may hold values from -32 to 32
- out_weight: bfloat16 [8192, 4224], P('tensor', 'dp'), may hold values from -0.0625 to 0.0625
- live_mask: int32 [4], replicated, may hold values 0 or 1
- micro_counts: int32 [4], replicated, may hold values from 1 to 4
Outputs:
- block_residual: bfloat16 [4, 4, 64, 4224], P('dp', None, None, 'tensor')
- query_gradient: bfloat16 [4, 4, 64, 8192], P('dp', None, None, 'tensor')
- key_value_grad: bfloat16 [4, 4, 2, 64, 1024], P('dp')
- projection_weight_gradient: float32 [8192, 4224], P('tensor', 'dp')
All inputs are finite; a program needn't handle non-finite values.
Results may differ from a plain program's by a relative error of at most 0.014.
Values may be sent and summed in bfloat16 or wider, within the bound.
No kernel may reach another device: no remote copies, remote signals or barrier semaphores. Data moves between devices by JAX's collectives and lax.ppermute only.
A program may use at most 128 MiB of HBM per device.

v0:
```python
import math

import jax
import jax.numpy as jnp
from jax import lax
from jax.sharding import PartitionSpec as P

HEAD_SIZE = 128
QUERY_HEADS = 64
KEY_VALUE_HEADS = 8


def attention_backward(query_f, key_f, value_f, probs, rounded, grad_heads):
    prob_grad = jnp.einsum("mhqd,mhkd->mhqk", grad_heads, value_f, precision=lax.Precision.HIGHEST)
    delta = jnp.sum(prob_grad * probs, axis=-1, keepdims=True)
    score_grad = probs * (prob_grad - delta)
    query_gradient = jnp.einsum(
        "mhqk,mhkd->mhqd", score_grad, key_f, precision=lax.Precision.HIGHEST
    ) / math.sqrt(HEAD_SIZE)
    key_term = jnp.einsum(
        "mhqk,mhqd->mhkd", score_grad, query_f, precision=lax.Precision.HIGHEST
    ) / math.sqrt(HEAD_SIZE)
    value_term = jnp.einsum("mhqk,mhqd->mhkd", rounded, grad_heads, precision=lax.Precision.HIGHEST)
    return (query_gradient, key_term, value_term)


def per_device(
    queries,
    slot_keys_values,
    segment_ids,
    residual_in,
    cotangent,
    out_weight,
    live_mask,
    micro_counts,
):
    tensor_size = lax.axis_size("tensor")
    heads_here = QUERY_HEADS // tensor_size
    heads_per_group = QUERY_HEADS // KEY_VALUE_HEADS
    tensor_idx = lax.axis_index("tensor")
    replica_idx = lax.axis_index("dp")
    query_here = queries[0]
    slot_total_count = query_here.shape[0]
    sequence_length = query_here.shape[1]
    local_feats = residual_in.shape[3]
    key_value_local = slot_keys_values[0].reshape(
        slot_total_count, 2, sequence_length, KEY_VALUE_HEADS, HEAD_SIZE
    )
    segments = segment_ids[0]
    head_ids = tensor_idx * heads_here + jnp.arange(heads_here)
    key_value_head_rows = head_ids // heads_per_group
    query_heads = query_here.reshape(
        slot_total_count, sequence_length, heads_here, HEAD_SIZE
    ).transpose(0, 2, 1, 3)
    key_head_rows = jnp.take(key_value_local[:, 0], key_value_head_rows, axis=2).transpose(
        0, 2, 1, 3
    )
    value_heads = jnp.take(key_value_local[:, 1], key_value_head_rows, axis=2).transpose(0, 2, 1, 3)
    positions = jnp.arange(sequence_length)
    allowed = (positions[None, :] <= positions[:, None])[None] & (
        segments[:, :, None] == segments[:, None, :]
    )
    allowed = allowed[:, None]
    scores = jnp.einsum(
        "mhqd,mhkd->mhqk", query_heads, key_head_rows, preferred_element_type=jnp.float32
    ) / math.sqrt(HEAD_SIZE)
    masked = jnp.where(allowed, scores, -jnp.inf)
    top_score = jnp.max(masked, axis=-1, keepdims=True)
    expo = jnp.where(allowed, jnp.exp(masked - top_score), 0.0)
    probs = expo / jnp.sum(expo, axis=-1, keepdims=True)
    probs_low = probs.astype(jnp.bfloat16)
    context = jnp.einsum(
        "mhqk,mhkd->mqhd", probs_low, value_heads, preferred_element_type=jnp.float32
    )
    context = context.astype(jnp.bfloat16).reshape(
        slot_total_count, sequence_length, heads_here * HEAD_SIZE
    )
    context_rows = context.reshape(slot_total_count * sequence_length, heads_here * HEAD_SIZE)
    weight_rows = lax.all_gather(out_weight, "dp", axis=1, tiled=True)
    reduced_total = lax.psum_scatter(
        jnp.einsum(
            "hd,nh->dn", weight_rows, context_rows, preferred_element_type=jnp.float32
        ).astype(jnp.bfloat16),
        "tensor",
        scatter_dimension=0,
        tiled=True,
    ).astype(jnp.float32)
    reduced_total = reduced_total.transpose(1, 0).reshape(
        slot_total_count, sequence_length, local_feats
    )
    block_residual = (residual_in[0].astype(jnp.float32) + reduced_total).astype(jnp.bfloat16)[None]
    replica_pick = jnp.arange(live_mask.shape[0]) == replica_idx
    my_live = jnp.sum(jnp.where(replica_pick, live_mask, 0))
    my_count = jnp.sum(jnp.where(replica_pick, micro_counts, 0))
    live_total = jnp.maximum(jnp.sum(live_mask * micro_counts), 1)
    slot_live = (jnp.arange(slot_total_count) < my_count) & (my_live > 0)
    slot_weight = slot_live.astype(jnp.float32) / live_total.astype(jnp.float32)
    scaled_cot = (cotangent[0].astype(jnp.float32) * slot_weight[:, None, None]).astype(
        jnp.bfloat16
    )
    weight_back = lax.all_gather(out_weight, "dp", axis=1, tiled=True)
    shard_piece = lax.all_gather(scaled_cot, "tensor", axis=2, tiled=True)
    grad_piece = jnp.einsum("msh,msd->hd", context, shard_piece, preferred_element_type=jnp.float32)
    grad_rows = grad_piece
    context_grad = jnp.einsum(
        "msd,hd->msh", shard_piece, weight_back, preferred_element_type=jnp.float32
    )
    grad_rows, context_grad = (grad_rows, context_grad)
    projection_weight_gradient = lax.psum_scatter(
        grad_rows.astype(jnp.bfloat16), "dp", scatter_dimension=1, tiled=True
    ).astype(jnp.float32)
    grad_heads = context_grad.reshape(
        slot_total_count, sequence_length, heads_here, HEAD_SIZE
    ).transpose(0, 2, 1, 3)
    query_f = query_heads.astype(jnp.float32)
    key_f = key_head_rows.astype(jnp.float32)
    value_f = value_heads.astype(jnp.float32)
    rounded = probs_low.astype(jnp.float32)
    query_gradient, key_term, value_term = attention_backward(
        query_f, key_f, value_f, probs, rounded, grad_heads
    )
    query_out = (
        query_gradient.transpose(0, 2, 1, 3)
        .reshape(slot_total_count, sequence_length, heads_here * HEAD_SIZE)
        .astype(jnp.bfloat16)[None]
    )
    addend_terms = (
        jnp.stack([key_term, value_term], axis=1).astype(jnp.bfloat16).astype(jnp.float32)
    )
    head_choice = (key_value_head_rows[:, None] == jnp.arange(KEY_VALUE_HEADS)[None, :]).astype(
        jnp.float32
    )
    positioned = jnp.einsum(
        "mchsd,hk->mcskd", addend_terms, head_choice, precision=lax.Precision.HIGHEST
    )
    positioned = positioned.reshape(
        slot_total_count, 2, sequence_length, KEY_VALUE_HEADS * HEAD_SIZE
    )
    keyval_sum = lax.psum(positioned.astype(jnp.bfloat16), "tensor")
    key_value_gradient = keyval_sum[None]
    return (block_residual, query_out, key_value_gradient, projection_weight_gradient)


def solution(mesh):
    placed = (
        P("dp", None, None, "tensor"),
        P("dp", None, None, None, None),
        P("dp", None, None),
        P("dp", None, None, "tensor"),
        P("dp", None, None, "tensor"),
        P("tensor", "dp"),
        P(),
        P(),
    )
    return jax.shard_map(
        per_device,
        mesh=mesh,
        in_specs=placed,
        out_specs=(
            P("dp", None, None, "tensor"),
            P("dp", None, None, "tensor"),
            P("dp", None, None, None, None),
            P("tensor", "dp"),
        ),
        check_vma=False,
    )
```

profile of v0, /device:TPU:0, one launch (start us, length us, event | category | flops | bytes accessed | tf_op | source)
XLA Modules:
  0.0 385.1 jit_solution(2700345857586108065)
XLA Ops:
  7.2 0.0 copy-start.12
  7.2 0.0 copy-start.13
  7.2 0.0 copy-start.10
  7.2 0.0 all-gather.3.cloned.1.call-start
  7.3 0.7 all-gather.3.cloned.1.call-update
  7.9 0.0 copy-start
  8.0 0.0 all-gather.5.cloned.1.call-start
  8.0 0.7 fusion.40
  9.4 0.3 copy.50
  10.4 0.7 and_select_fusion
  11.0 1.1 fusion.18
  12.2 0.0 all-gather.5.cloned.1.call-update
  12.2 0.0 reduce-scatter.7.cloned.1.call-start
  12.2 0.0 copy-done.6
  12.2 0.1 copy.70
  12.4 0.3 copy.69
  12.7 0.1 fusion.42
  12.8 0.0 copy-start.11
  12.8 0.3 copy_bitcast_fusion
  13.0 0.7 gather_fusion.1
  13.7 0.6 gather_fusion
  14.4 0.1 compare_and_fusion
  14.5 0.2 select_bitcast_fusion
  14.7 0.0 copy-start.2
  14.7 0.4 fusion.12
  15.1 1.3 fusion.43
  16.4 0.5 convolution_convert_fusion.2
  16.9 0.0 copy-done.4
  16.9 0.3 copy.49
  17.2 54.9 %all-gather.3.cloned.1.call-done = bf16[1024,4224]{0,1:T(8,128)(2,1)} async-done(((bf16[1024,1056]{0,1:T(8,128)(2,1)}), bf16[1024,4224]{0,1:T(8,128)(2,1)}) %all-gather.3.cloned.1.call-update) | async-done | bytes 8650768 | tf_op jit(solution)/shard_map/all_gather | solution.py:79
  72.1 6.0 %fusion.3 = bf16[4224,256]{0,1:T(8,128)(2,1)S(1)} fusion(bf16[1024,4224]{0,1:T(8,128)(2,1)} %all-gather.3.cloned.1.call-done, bf16[32,8,8,128]{3,2,1,0:T(8,128)(2,1)S(1)} %bitcast.104), kind=kOutput, calls=%fused_computation.7 | convolution fusion | flops 2215673856 | bytes 11337728 | tf_op jit(solution)/shard_map/hd,nh->dn/dot_general | solution.py:81
  78.1 2.4 copy.63
  80.5 0.0 reduce-scatter.7.cloned.1.call-update
  80.5 0.0 reduce-scatter.5.cloned.1.call-start
  80.6 68.8 %all-gather.5.cloned.1.call-done = bf16[4,64,4224]{1,0,2:T(4,128)(2,1)} async-done(((bf16[4,64,528]{1,0,2:T(4,128)(2,1)}), bf16[4,64,4224]{1,0,2:T(4,128)(2,1)}) %all-gather.5.cloned.1.call-update) | async-done | bytes 2162704 | tf_op jit(solution)/shard_map/all_gather | solution.py:102
  149.4 6.6 %copy.51 = bf16[4,64,4224]{2,1,0:T(8,128)(2,1)S(1)} copy(bf16[4,64,4224]{1,0,2:T(4,128)(2,1)} %all-gather.5.cloned.1.call-done) | data formatting | bytes 4325376 | tf_op jit(solution)/shard_map/all_gather | solution.py:102
  156.0 5.8 %bitcast_convert_fusion = bf16[1024,4224]{0,1:T(8,128)(2,1)} fusion(bf16[4,64,4224]{2,1,0:T(8,128)(2,1)S(1)} %copy.51, bf16[4,8,128,64]{2,3,1,0:T(8,128)(2,1)S(1)} %convolution_convert_fusion.2), kind=kOutput, calls=%fused_computation.3 | convolution fusion | flops 2218917888 | bytes 11337728 | tf_op jit(solution)/shard_map/msh,msd->hd/dot_general | solution.py:103
  161.7 0.0 reduce-scatter.5.cloned.1.call-update
  161.8 0.0 copy-start.1
  161.8 0.2 all-reduce.2.cloned.1.call-start
  162.0 6.0 %fusion.8 = f32[4,8,8,8,128]{4,3,2,1,0:T(8,128)S(1)} fusion(bf16[4,64,4224]{2,1,0:T(8,128)(2,1)S(1)} %copy.51, bf16[1024,4224]{0,1:T(8,128)(2,1)} %all-gather.3.cloned.1.call-done), kind=kOutput, calls=%fused_computation.13 | convolution fusion | flops 2214592512 | bytes 11862016 | tf_op jit(solution)/shard_map/msd,hd->msh/dot_general | solution.py:105
  168.1 0.7 fusion.15
  168.7 0.3 copy-done.5
  169.1 1.0 multiply_reduce_fusion
  170.1 0.0 copy-start.14
  170.1 0.0 copy-done.8
  170.1 0.8 fusion.16
  170.9 0.1 copy-done.14
  171.1 0.1 pad_maximum_fusion
  171.2 0.0 copy-start.3
  171.2 0.7 fusion.5
  171.9 1.3 broadcast_in_dim.51
  173.2 0.0 all-reduce.2.cloned.1.call-update
  173.2 2.2 fusion.17
  175.4 0.0 copy-start.9
  175.5 0.3 copy.56
  175.8 1.0 convert_element_type.89
  176.8 43.0 %reduce-scatter.7.cloned.1.call-done = bf16[528,256]{1,0:T(8,128)(2,1)} async-done(((bf16[4224,256]{1,0:T(8,128)(2,1)}), bf16[528,256]{1,0:T(8,128)(2,1)}) %reduce-scatter.7.cloned.1.call-update) | async-done | bytes 270352
  219.8 1.2 copy.64
  221.0 0.8 add_convert_fusion
  221.8 72.9 %reduce-scatter.5.cloned.1.call-done = bf16[1024,1056]{0,1:T(8,128)(2,1)} async-done(((bf16[1024,4224]{0,1:T(8,128)(2,1)}), bf16[1024,1056]{0,1:T(8,128)(2,1)}) %reduce-scatter.5.cloned.1.call-update) | async-done | bytes 2162704 | tf_op jit(solution)/shard_map/reduce_scatter | solution.py:109
  294.7 4.1 %convert_element_type.94 = f32[1024,1056]{0,1:T(8,128)} convert(bf16[1024,1056]{0,1:T(8,128)(2,1)} %reduce-scatter.5.cloned.1.call-done) | non-fusion elementwise | flops 1081344 | bytes 6488064 | tf_op jit(solution)/shard_map/convert_element_type | solution.py:111
  298.9 77.4 %all-reduce.2.cloned.1.call-done = bf16[1,4,2,64,1024]{4,3,2,1,0:T(8,128)(2,1)} async-done(((bf16[1,4,2,64,1024]{4,3,2,1,0:T(8,128)(2,1)}), bf16[1,4,2,64,1024]{4,3,2,1,0:T(8,128)(2,1)}) %all-reduce.2.cloned.1.call-update) | async-done | bytes 1048592 | tf_op jit(solution)/shard_map/psum | solution.py:139
  376.3 2.3 copy.113
  (20 shorter events, 0.1 us)
Async XLA Ops:
  7.2 0.8 copy-start.12
  7.2 0.8 copy-start.13
  7.2 2.2 copy-start.10
  7.2 5.0 %copy-start.6 = (bf16[1,4,64,1024]{3,2,1,0:T(8,128)(2,1)S(1)}, bf16[1,4,64,1024]{3,2,1,0:T(8,128)(2,1)}, u32[]{:S(2)}) copy-start(bf16[1,4,64,1024]{3,2,1,0:T(8,128)(2,1)} %param.10) | copy-start | bytes 1572868
  7.2 64.9 %all-gather.3.cloned.1.call-start = ((), (), s32[]{:S(2)}) async-start(), calls=%async_computation.2 | async-start | bytes 10813440 | tf_op jit(solution)/shard_map/all_gather | solution.py:79
  7.9 4.4 %copy-start = (bf16[1,4,2,64,1024]{4,3,2,1,0:T(8,128)(2,1)S(1)}, bf16[1,4,2,64,1024]{4,3,2,1,0:T(8,128)(2,1)}, u32[]{:S(2)}) copy-start(bf16[1,4,2,64,1024]{4,3,2,1,0:T(8,128)(2,1)} %param.11) | copy-start | bytes 3145732
  8.0 141.4 %all-gather.5.cloned.1.call-start = ((), (), s32[]{:S(2)}) async-start(), calls=%async_computation.3 | async-start | bytes 4866048 | tf_op jit(solution)/shard_map/all_gather | solution.py:102
  12.2 207.6 %reduce-scatter.7.cloned.1.call-start = ((), (), s32[]{:S(2)}) async-start(), calls=%async_computation.6 | async-start | bytes 2433024
  12.3 2.4 copy-start.7
  12.8 1.6 copy-start.11
  14.7 1.7 copy-start.2
  14.7 2.2 copy-start.4
  80.5 214.2 %reduce-scatter.5.cloned.1.call-start = ((), (), s32[]{:S(2)}) async-start(), calls=%async_computation.5 | async-start | bytes 10813440 | tf_op jit(solution)/shard_map/reduce_scatter | solution.py:109
  161.8 6.3 %copy-start.1 = (f32[4,8,64,64]{2,3,1,0:T(8,128)S(1)}, f32[4,8,64,64]{2,3,1,0:T(8,128)}, u32[]{:S(2)}) copy-start(f32[4,8,64,64]{2,3,1,0:T(8,128)} %get-tuple-element.13) | copy-start | bytes 1572868
  161.8 214.5 %all-reduce.2.cloned.1.call-start = ((), (), s32[]{:S(2)}) async-start(), calls=%async_computation.4 | async-start | bytes 2097152 | tf_op jit(solution)/shard_map/psum | solution.py:139
  168.0 1.0 copy-start.5
  169.1 1.0 copy-start.8
  170.1 1.0 copy-start.14
  171.2 2.0 copy-start.3
  175.4 45.6 %copy-start.9 = (bf16[1,4,64,528]{3,2,1,0:T(8,128)(2,1)S(1)}, bf16[1,4,64,528]{3,2,1,0:T(8,128)(2,1)}, u32[]{:S(2)}) copy-start(bf16[1,4,64,528]{3,2,1,0:T(8,128)(2,1)} %param.13) | copy-start | bytes 811012
Sparse Core Ops, SparseCore 0:
  9.6 62.4 all-gather.2
  74.3 75.0 all-gather.4
  153.4 66.3 reduce-scatter.6
  222.3 72.3 reduce-scatter.4
  298.1 78.1 all-reduce.1
where the time goes:
time: 386 us; the launch traced here: 385 us
  waiting for transfers between devices  318 us (82%)
  matrix products  24.1 us (6%)
  local copies, waits for them, and re-layouts  18.3 us (5%)
  between operations  15.5 us (4%)
  other arithmetic  9.08 us (2%)
    psum x1, waiting for transfers between devices, per_device(): keyval_sum = lax.psum(positioned.astype(jnp.bfloat16), 'tensor')  77.4 us
    reduce_scatter x1, waiting for transfers between devices, per_device(): lax.psum_scatter(grad_rows.astype(jnp.bfloat16), 'dp', scatter_dimension=...  72.9 us
    all_gather x1, waiting for transfers between devices, per_device(): shard_piece = lax.all_gather(scaled_cot, 'tensor', axis=2, tiled=True)  68.8 us
    all_gather x1, waiting for transfers between devices, per_device(): weight_rows = lax.all_gather(out_weight, 'dp', axis=1, tiled=True)  54.9 us
    unnamed x6, waiting for transfers between devices  43.7 us
  transfers between devices with their start and end apart: 5, of which 5 were waited for; matrix products, arithmetic and copies ran while one was open for 13% of the time, Pallas kernels for 0%

commit v1 on v0

--- a/solution.py
+++ b/solution.py
@@ -1,13 +1,345 @@
+import functools
 import math
 
 import jax
 import jax.numpy as jnp
 from jax import lax
+from jax.experimental import pallas as pl
+from jax.experimental.pallas import tpu as pltpu
 from jax.sharding import PartitionSpec as P
 
 HEAD_SIZE = 128
 QUERY_HEADS = 64
 KEY_VALUE_HEADS = 8
+BF = jnp.bfloat16
+F32 = jnp.float32
+VMEM = pl.BlockSpec(memory_space=pltpu.VMEM)
+SMEM = pl.BlockSpec(memory_space=pltpu.SMEM)
+NT = (((1,), (1,)), ((), ()))
+TN = (((0,), (0,)), ((), ()))
+NN = (((1,), (0,)), ((), ()))
+LIMIT = 48 * 1024 * 1024
+
+
+def dot(a, b, dims=NN):
+    return lax.dot_general(a, b, dims, preferred_element_type=F32)
+
+
+def call(kernel, out_shape, in_specs, flops, moved, scratch=(), **grid):
+    return pl.pallas_call(
+        kernel,
+        out_shape=out_shape,
+        in_specs=in_specs,
+        scratch_shapes=scratch,
+        cost_estimate=pl.CostEstimate(flops=flops, bytes_accessed=moved, transcendentals=0),
+        compiler_params=pltpu.CompilerParams(vmem_limit_bytes=LIMIT),
+        **grid,
+    )
+
+
+def stack_heads(rows, heads):
+    return jnp.concatenate(
+        [rows[:, h * HEAD_SIZE : (h + 1) * HEAD_SIZE] for h in range(heads)], axis=0
+    )
+
+
+def forward_kernel(heads, q_ref, key_value_ref, seg_ref, context_ref, probs_ref):
+    slots, length = q_ref.shape[:2]
+    row = lax.broadcasted_iota(jnp.int32, (length, length), 0)
+    col = lax.broadcasted_iota(jnp.int32, (length, length), 1)
+    for m in range(slots):
+        seg = jnp.broadcast_to(seg_ref[m : m + 1, :].astype(F32), (length, length))
+        allowed = (col <= row) & (seg == seg.T)
+        q = stack_heads(q_ref[m], heads)
+        scores = dot(q, key_value_ref[m, 0], NT) * (1.0 / math.sqrt(HEAD_SIZE))
+        scores = scores.reshape(heads, length, length)
+        masked = jnp.where(allowed[None], scores, -jnp.inf)
+        expo = jnp.exp(masked - jnp.max(masked, axis=-1, keepdims=True))
+        probs = expo / jnp.sum(expo, axis=-1, keepdims=True)
+        probs = probs.reshape(heads * length, length)
+        probs_ref[m] = probs
+        context = dot(probs.astype(BF), key_value_ref[m, 1]).astype(BF)
+        for h in range(heads):
+            context_ref[m * length : (m + 1) * length, h * HEAD_SIZE : (h + 1) * HEAD_SIZE] = (
+                context[h * length : (h + 1) * length]
+            )
+
+
+def backward_kernel(
+    heads, own_ref, got_ref, q_ref, key_value_ref, probs_ref, query_grad_ref, key_value_grad_ref
+):
+    slots, length = q_ref.shape[:2]
+    scale = 1.0 / math.sqrt(HEAD_SIZE)
+    for m in range(slots):
+        rows = slice(m * length, (m + 1) * length)
+        grad = (own_ref[rows, :] + got_ref[rows, :].astype(F32)).astype(BF)
+        grad = stack_heads(grad, heads)
+        q = stack_heads(q_ref[m], heads)
+        key, value = key_value_ref[m, 0], key_value_ref[m, 1]
+        probs = probs_ref[m]
+        prob_grad = dot(grad, value, NT)
+        delta = jnp.sum(prob_grad * probs, axis=-1, keepdims=True)
+        score_grad = probs * (prob_grad - delta)
+        high = score_grad.astype(BF)
+        low = (score_grad - high.astype(F32)).astype(BF)
+        query_grad = ((dot(high, key) + dot(low, key)) * scale).astype(BF)
+        for h in range(heads):
+            query_grad_ref[m, :, h * HEAD_SIZE : (h + 1) * HEAD_SIZE] = query_grad[
+                h * length : (h + 1) * length
+            ]
+        key_grad = (dot(high, q, TN) + dot(low, q, TN)) * scale
+        key_value_grad_ref[m, 0] = key_grad.astype(BF)
+        key_value_grad_ref[m, 1] = dot(probs.astype(BF), grad, TN).astype(BF)
+
+
+def project_kernel(parts, split, half_ref, block_ref, own_ref, other_ref, weight_ref, *refs):
+    outs, context = refs[:-1], refs[-1]
+    tokens = own_ref.shape[0]
+    features = outs[0].shape[0] + outs[1].shape[0]
+    context[:tokens, :] = own_ref[...]
+    context[tokens:, :] = other_ref[...]
+    for k in range(parts):
+        at = pl.multiple_of(block_ref[k] * features, 16)
+        rows = pl.multiple_of(half_ref[k] * tokens, 16)
+        block = dot(weight_ref[pl.ds(at, features), :], context[pl.ds(rows, tokens), :], NT)
+        block = block.astype(BF)
+        outs[2 * k][...] = block[:split]
+        outs[2 * k + 1][...] = block[split:]
+
+
+def context_grad_kernel(half_ref, block_ref, *refs):
+    shards, (weight_ref, own_ref, other_ref, total) = refs[:-4], refs[-4:]
+    total[...] = jnp.zeros_like(total)
+    tokens = own_ref.shape[0]
+    for k in range(len(shards) // 2):
+        base = block_ref[k] * (shards[0].shape[0] + shards[1].shape[0])
+        rows = pl.ds(pl.multiple_of(half_ref[k] * tokens, 16), tokens)
+        term = None
+        for shard in shards[2 * k : 2 * k + 2]:
+            at = pl.multiple_of(base, 16)
+            part = dot(shard[...], weight_ref[pl.ds(at, shard.shape[0]), :], TN)
+            term = part if term is None else term + part
+            base = base + shard.shape[0]
+        total[rows, :] += term
+    own_ref[...] = total[:tokens, :]
+    other_ref[...] = total[tokens:, :].astype(BF)
+
+
+def weight_grad_kernel(half_ref, block_ref, *refs):
+    shards = refs[:-6]
+    context_own, context_other, own_ref, other_ref, total, context = refs[-6:]
+    tokens = context_own.shape[0]
+    context[:tokens, :] = context_own[...]
+    context[tokens:, :] = context_other[...]
+    total[...] = jnp.zeros_like(total)
+    for k in range(len(shards) // 2):
+        base = block_ref[k] * (shards[0].shape[0] + shards[1].shape[0])
+        rows = pl.ds(pl.multiple_of(half_ref[k] * tokens, 16), tokens)
+        for shard in shards[2 * k : 2 * k + 2]:
+            at = pl.ds(pl.multiple_of(base, 16), shard.shape[0])
+            total[at, :] += dot(shard[...], context[rows, :])
+            base = base + shard.shape[0]
+    own = own_ref.shape[0]
+    own_ref[...] = total[:own, :]
+    other_ref[...] = total[own:, :].astype(BF)
+
+
+def place_kernel(col_ref, *refs):
+    shards, out_ref = refs[:-1], refs[-1]
+    for k, shard in enumerate(shards):
+        at = pl.multiple_of(col_ref[k] * HEAD_SIZE, HEAD_SIZE)
+        out_ref[:, pl.ds(at, HEAD_SIZE)] = shard[...]
+
+
+class Ring:
+    def __init__(self, axis, size):
+        self.axis, self.size = axis, size
+        self.order = list(range(0, size, 2)) + list(range(1, size, 2))[::-1]
+        self.up = [(self.order[i], self.order[(i + 1) % size]) for i in range(size)]
+        self.down = [(b, a) for a, b in self.up]
+        place = [self.order.index(t) for t in range(size)]
+        table = [[self.order[(place[t] + k) % size] for k in range(size)] for t in range(size)]
+        self.table = jnp.array(table, jnp.int32)
+
+    def ids(self):
+        return self.table[lax.axis_index(self.axis)]
+
+    def send(self, arrays, way):
+        return [lax.ppermute(a, self.axis, way) for a in arrays]
+
+    def gather(self, pair):
+        n = self.size
+        out = [None] * n
+        out[0] = a = b = list(pair)
+        for step in range(1, n // 2):
+            a, b = self.send(a, self.up), self.send(b, self.down)
+            out[n - step], out[step] = a, b
+        out[n // 2] = self.send(a[:1], self.up) + self.send(b[1:], self.down)
+        return out
+
+    def scatter_sum(self, pairs):
+        n = self.size
+        far = pairs[n // 2]
+        a = [far[0], None]
+        b = [None, far[1]]
+        for step in range(n // 2 - 1, -1, -1):
+            a = [None if v is None else lax.ppermute(v, self.axis, self.up) for v in a]
+            b = [None if v is None else lax.ppermute(v, self.axis, self.down) for v in b]
+            if step:
+                add = lambda mine, got: mine if got is None else mine + got
+                a = [add(m, g) for m, g in zip(pairs[step], a)]
+                b = [add(m, g) for m, g in zip(pairs[n - step], b)]
+        return [
+            p.astype(F32) + u.astype(F32) + d.astype(F32) for p, u, d in zip(pairs[0], a, b)
+        ]
+
+
+def slot_weights(live_mask, micro_counts, slots):
+    replica = lax.axis_index("dp")
+    pick = jnp.arange(live_mask.shape[0]) == replica
+    my_live = jnp.sum(jnp.where(pick, live_mask, 0))
+    my_count = jnp.sum(jnp.where(pick, micro_counts, 0))
+    live_total = jnp.maximum(jnp.sum(live_mask * micro_counts), 1)
+    slot_live = (jnp.arange(slots) < my_count) & (my_live > 0)
+    return slot_live.astype(F32) / live_total.astype(F32)
+
+
+def by_activations(
+    dp_size,
+    tensor_size,
+    queries,
+    slot_keys_values,
+    segment_ids,
+    residual_in,
+    cotangent,
+    out_weight,
+    live_mask,
+    micro_counts,
+):
+    pairs = dp_size // 2
+    inner = tensor_size // pairs
+    _, slots, length, width = queries.shape
+    features = residual_in.shape[3]
+    heads = width // HEAD_SIZE
+    tokens = slots * length
+    dp_idx, tensor_idx = lax.axis_index("dp"), lax.axis_index("tensor")
+    pair_idx, core = dp_idx // 2, dp_idx % 2
+    both = ("dp", "tensor")
+
+    def device(x, c, t):
+        return (2 * x + c) * tensor_size + t
+
+    every = [(x, c, t) for x in range(pairs) for c in range(2) for t in range(tensor_size)]
+    swap_cores = [(2 * x + c, 2 * x + 1 - c) for x in range(pairs) for c in range(2)]
+    swap_pairs = [(2 * x + c, 2 * (1 - x) + c) for x in range(pairs) for c in range(2)]
+    turn = [
+        (device(x, c, t), device(t // inner, c, x * inner + t % inner)) for x, c, t in every
+    ]
+    ring = Ring("tensor", tensor_size)
+    ids = ring.ids()
+    half_ids = (ids // inner) ^ pair_idx
+    in_block = ids % inner
+    per_core = inner // 2
+    block_ids = ((in_block // per_core) ^ core) * per_core + in_block % per_core
+    split = (features // 2 + 15) // 16 * 16
+
+    weight = slot_weights(live_mask, micro_counts, slots)
+    scaled = (cotangent[0].astype(F32) * weight[:, None, None]).astype(BF)
+    scaled = scaled.reshape(tokens, features).T
+    scaled = lax.ppermute(scaled, both, turn)
+    shards = ring.gather([scaled[:split], scaled[split:]])
+
+    weight_own = out_weight.T
+    weight_rows = jnp.concatenate([weight_own, lax.ppermute(weight_own, "dp", swap_cores)], axis=0)
+
+    key_value = lax.dynamic_slice_in_dim(
+        slot_keys_values[0], tensor_idx * HEAD_SIZE, HEAD_SIZE, axis=3
+    )
+    context, probs = call(
+        functools.partial(forward_kernel, heads),
+        (
+            jax.ShapeDtypeStruct((tokens, width), BF),
+            jax.ShapeDtypeStruct((slots, heads * length, length), F32),
+        ),
+        [VMEM] * 3,
+        4 * tokens * width * length,
+        4 * tokens * width * 2,
+    )(queries[0], key_value, segment_ids[0])
+    context_other = lax.ppermute(context, "dp", swap_pairs)
+
+    piece = [
+        jax.ShapeDtypeStruct((split, tokens), BF),
+        jax.ShapeDtypeStruct((features - split, tokens), BF),
+    ]
+    big = 2 * 2 * tokens * width * inner * features
+    partial = call(
+        functools.partial(project_kernel, tensor_size, split),
+        piece * tensor_size,
+        [SMEM, SMEM, VMEM, VMEM, VMEM],
+        big,
+        2 * inner * features * width,
+        [pltpu.VMEM((2 * tokens, width), BF)],
+    )(half_ids, block_ids, context, context_other, weight_rows)
+    summed = ring.scatter_sum([partial[2 * k : 2 * k + 2] for k in range(tensor_size)])
+    summed = jnp.concatenate([s.astype(BF) for s in summed], axis=0)
+    summed = lax.ppermute(summed, both, turn)
+    block_residual = (
+        residual_in[0].astype(F32) + summed.T.reshape(slots, length, features).astype(F32)
+    ).astype(BF)[None]
+
+    flat = [piece for pair in shards for piece in pair]
+    grad_own, grad_other = call(
+        context_grad_kernel,
+        (jax.ShapeDtypeStruct((tokens, width), F32), jax.ShapeDtypeStruct((tokens, width), BF)),
+        [SMEM, SMEM] + [VMEM] * (len(flat) + 1),
+        big,
+        2 * inner * features * width,
+        [pltpu.VMEM((2 * tokens, width), F32)],
+    )(half_ids, block_ids, *flat, weight_rows)
+    grad_got = lax.ppermute(grad_other, "dp", swap_pairs)
+    query_gradient, key_value_part = call(
+        functools.partial(backward_kernel, heads),
+        (
+            jax.ShapeDtypeStruct((slots, length, width), BF),
+            jax.ShapeDtypeStruct((slots, 2, length, HEAD_SIZE), BF),
+        ),
+        [VMEM] * 5,
+        14 * tokens * width * length,
+        8 * tokens * width * 2,
+    )(grad_own, grad_got, queries[0], key_value, probs)
+
+    own_rows = weight_own.shape[0]
+    weight_grad, weight_grad_other = call(
+        weight_grad_kernel,
+        (
+            jax.ShapeDtypeStruct((own_rows, width), F32),
+            jax.ShapeDtypeStruct((own_rows, width), BF),
+        ),
+        [SMEM, SMEM] + [VMEM] * (len(flat) + 2),
+        big,
+        6 * own_rows * width,
+        [pltpu.VMEM((2 * own_rows, width), F32), pltpu.VMEM((2 * tokens, width), BF)],
+    )(half_ids, block_ids, *flat, context, context_other)
+    weight_grad_got = lax.ppermute(weight_grad_other, "dp", swap_cores)
+    weight_grad = (weight_grad + weight_grad_got.astype(F32)).T
+
+    rows = slots * 2 * length
+    part = key_value_part.reshape(rows, HEAD_SIZE)
+    parts = ring.gather([part[: rows // 2], part[rows // 2 :]])
+    top, bottom = [
+        call(
+            place_kernel,
+            jax.ShapeDtypeStruct((rows // 2, KEY_VALUE_HEADS * HEAD_SIZE), BF),
+            [SMEM] + [VMEM] * tensor_size,
+            0,
+            2 * rows * KEY_VALUE_HEADS * HEAD_SIZE,
+        )(ids, *[pair[i] for pair in parts])
+        for i in range(2)
+    ]
+    key_value_gradient = jnp.concatenate([top, bottom], axis=0).reshape(
+        1, slots, 2, length, KEY_VALUE_HEADS * HEAD_SIZE
+    )
+    return block_residual, query_gradient[None], key_value_gradient, weight_grad
 
 
 def attention_backward(query_f, key_f, value_f, probs, rounded, grad_heads):
@@ -24,7 +356,7 @@
     return (query_gradient, key_term, value_term)
 
 
-def per_device(
+def by_weights(
     queries,
     slot_keys_values,
     segment_ids,
@@ -142,6 +474,12 @@
 
 
 def solution(mesh):
+    dp_size, tensor_size = mesh.shape["dp"], mesh.shape["tensor"]
+    regular = dp_size == 4 and tensor_size % dp_size == 0
+    regular = regular and tensor_size == KEY_VALUE_HEADS
+    per_device = (
+        functools.partial(by_activations, dp_size, tensor_size) if regular else by_weights
+    )
     placed = (
         P("dp", None, None, "tensor"),
         P("dp", None, None, None, None),

time: 386 us -> 152 us (0.39)
  the two profiles are of different devices: /device:TPU:0 before, /device:TPU:8 now
where the time goes in v1:
time: 152 us
  starting transfers between devices  63.4 us (42%)
  waiting for transfers between devices  30.9 us (20%)
  Pallas kernels  23.7 us (16%)
  other arithmetic  17.1 us (11%)
  local copies, waits for them, and re-layouts  14.3 us (9%)
  between operations  2.35 us (2%)
    ppermute x28, starting transfers between devices, send(): return [lax.ppermute(a, self.axis, way) for a in arrays]  41.2 us
    ppermute x28, waiting for transfers between devices, send(): return [lax.ppermute(a, self.axis, way) for a in arrays]  20.6 us
    unnamed x48, local copies, waits for them, and re-layouts  11.1 us
    ppermute x7, starting transfers between devices, scatter_sum(): a = [None if v is None else lax.ppermute(v, self.axis, self.up) for v in a]  9.27 us
    ppermute x7, waiting for transfers between devices, scatter_sum(): lax.ppermute(v, self.axis, self.down)  8.42 us
    pallas_call x1, Pallas kernels, by_activations(): call(weight_grad_kernel, (jax.ShapeDtypeStruct((own_rows, width), F32), j...  7.57 us
    pallas_call x1, Pallas kernels, by_activations(): call(context_grad_kernel, (jax.ShapeDtypeStruct((tokens, width), F32), ja...  6.33 us
    transpose x1, other arithmetic, by_activations(): weight_grad = (weight_grad + weight_grad_got.astype(F32)).T  6.09 us
  transfers between devices with their start and end apart: 48, of which 18 were waited for; matrix products, arithmetic and copies ran while one was open for 9% of the time, Pallas kernels for 16%

profile of v1, /device:TPU:8, one launch (start us, length us, event | category | flops | bytes accessed | tf_op | source)
XLA Modules:
  0.0 151.7 jit_solution(4671108266316693917)
XLA Ops:
  0.7 1.4 fusion.2
  4.3 1.0 bitcast_convert_fusion
  5.5 0.7 fusion
  6.3 3.7 %collective-permute-start.17 = (bf16[528,256]{1,0:T(8,128)(2,1)}, bf16[528,256]{1,0:T(8,128)(2,1)}, u32[]{:S(2)}, u32[]{:S(2)}) collective-permute-start(bf16[528,256]{1,0:T(8,128)(2,1)} %fusion), channel_id=1, source_target_pairs={{0,0},{1,1},{2,2},{3,3},{4,16},{5,17},{6,18},{7,19},{8,8},{9,9},{1... | collective-permute-start | bytes 811016 | tf_op jit(solution)/shard_map/ppermute | solution.py:249
  10.0 1.0 copy-done.1
  11.7 1.2 shard_map.120
  12.9 2.4 %collective-permute-start = (bf16[256,1024]{1,0:T(8,128)(2,1)S(1)}, bf16[256,1024]{1,0:T(8,128)(2,1)S(1)}, u32[]{:S(2)}, u32[]{:S(2)}) collective-permute-start(bf16[256,1024]{1,0:T(8,128)(2,1)S(1)} %get-tuple-element.28.own_ref.refs_16_), channel_id=1, source_target_pairs={{0,16},{8,24},{16,0},{24,8},{1,17},{9,25},{17,1},{25,9},{2,18},{10... | collective-permute-start | bytes 1572872 | tf_op jit(solution)/shard_map/ppermute | solution.py:268
  15.3 0.9 slice.24.refs_0_
  16.2 8.2 %collective-permute-start.24 = (bf16[272,256]{1,0:T(8,128)(2,1)S(1)}, bf16[272,256]{1,0:T(8,128)(2,1)S(1)}, u32[]{:S(2)}, u32[]{:S(2)}) collective-permute-start(bf16[272,256]{1,0:T(8,128)(2,1)S(1)} %slice.24.refs_0_), channel_id=1, source_target_pairs={{0,2},{2,4},{4,6},{6,7},{7,5},{5,3},{3,1},{1,0},{8,10},{10,12},{12... | collective-permute-start | bytes 417800 | tf_op jit(solution)/shard_map/ppermute | solution.py:168
  24.4 0.9 slice.25.refs_1_
  25.3 4.7 %collective-permute-start.29 = (bf16[256,256]{1,0:T(8,128)(2,1)S(1)}, bf16[256,256]{1,0:T(8,128)(2,1)S(1)}, u32[]{:S(2)}, u32[]{:S(2)}) collective-permute-start(bf16[256,256]{1,0:T(8,128)(2,1)S(1)} %slice.25.refs_1_), channel_id=1, source_target_pairs={{0,2},{2,4},{4,6},{6,7},{7,5},{5,3},{3,1},{1,0},{8,10},{10,12},{12... | collective-permute-start | bytes 393224 | tf_op jit(solution)/shard_map/ppermute | solution.py:168
  30.0 2.6 %collective-permute-done.29.refs_15_ = bf16[256,256]{1,0:T(8,128)(2,1)S(1)} collective-permute-done((bf16[256,256]{1,0:T(8,128)(2,1)S(1)}, bf16[256,256]{1,0:T(8,128)(2,1)S(1)}, u32[]{:S(2)}, u32[]{:S(2)}) %collective-permute-start.29) | collective-permute-done | bytes 131104 | tf_op jit(solution)/shard_map/ppermute | solution.py:168
  32.6 2.5 %collective-permute-start.25 = (bf16[272,256]{1,0:T(8,128)(2,1)S(1)}, bf16[272,256]{1,0:T(8,128)(2,1)S(1)}, u32[]{:S(2)}, u32[]{:S(2)}) collective-permute-start(bf16[272,256]{1,0:T(8,128)(2,1)S(1)} %collective-permute-done.24.refs_14_), channel_id=1, source_target_pairs={{0,2},{2,4},{4,6},{6,7},{7,5},{5,3},{3,1},{1,0},{8,10},{10,12},{12... | collective-permute-start | bytes 417800 | tf_op jit(solution)/shard_map/ppermute | solution.py:168
  36.7 1.6 %collective-permute-done.18.refs_2_ = bf16[272,256]{1,0:T(8,128)(2,1)S(1)} collective-permute-done((bf16[272,256]{1,0:T(8,128)(2,1)S(1)}, bf16[272,256]{1,0:T(8,128)(2,1)S(1)}, u32[]{:S(2)}, u32[]{:S(2)}) %collective-permute-start.18) | collective-permute-done | bytes 139296 | tf_op jit(solution)/shard_map/ppermute | solution.py:168
  39.3 2.8 %collective-permute-start.26 = (bf16[272,256]{1,0:T(8,128)(2,1)S(1)}, bf16[272,256]{1,0:T(8,128)(2,1)}, u32[]{:S(2)}, u32[]{:S(2)}) collective-permute-start(bf16[272,256]{1,0:T(8,128)(2,1)S(1)} %collective-permute-done.25.refs_12_), channel_id=1, source_target_pairs={{0,2},{2,4},{4,6},{6,7},{7,5},{5,3},{3,1},{1,0},{8,10},{10,12},{12... | collective-permute-start | bytes 417800 | tf_op jit(solution)/shard_map/ppermute | solution.py:168
  42.8 2.1 %collective-permute-start.30 = (bf16[256,256]{1,0:T(8,128)(2,1)S(1)}, bf16[256,256]{1,0:T(8,128)(2,1)}, u32[]{:S(2)}, u32[]{:S(2)}) collective-permute-start(bf16[256,256]{1,0:T(8,128)(2,1)S(1)} %collective-permute-done.29.refs_15_), channel_id=1, source_target_pairs={{0,2},{2,4},{4,6},{6,7},{7,5},{5,3},{3,1},{1,0},{8,10},{10,12},{12... | collective-permute-start | bytes 393224 | tf_op jit(solution)/shard_map/ppermute | solution.py:168
  46.2 2.1 %collective-permute-start.27 = (bf16[272,256]{1,0:T(8,128)(2,1)}, bf16[272,256]{1,0:T(8,128)(2,1)}, u32[]{:S(2)}, u32[]{:S(2)}) collective-permute-start(bf16[272,256]{1,0:T(8,128)(2,1)} %collective-permute-done.26.refs_10_), channel_id=1, source_target_pairs={{0,2},{2,4},{4,6},{6,7},{7,5},{5,3},{3,1},{1,0},{8,10},{10,12},{12... | collective-permute-start | bytes 417800 | tf_op jit(solution)/shard_map/ppermute | solution.py:168
  48.3 0.7 collective-permute-done.30.refs_13_
  49.0 2.4 %collective-permute-start.31 = (bf16[256,256]{1,0:T(8,128)(2,1)}, bf16[256,256]{1,0:T(8,128)(2,1)}, u32[]{:S(2)}, u32[]{:S(2)}) collective-permute-start(bf16[256,256]{1,0:T(8,128)(2,1)} %collective-permute-done.30.refs_13_), channel_id=1, source_target_pairs={{0,2},{2,4},{4,6},{6,7},{7,5},{5,3},{3,1},{1,0},{8,10},{10,12},{12... | collective-permute-start | bytes 393224 | tf_op jit(solution)/shard_map/ppermute | solution.py:168
  51.7 0.7 fusion.1
  52.4 1.9 %collective-permute-done.31.refs_11_ = bf16[256,256]{1,0:T(8,128)(2,1)} collective-permute-done((bf16[256,256]{1,0:T(8,128)(2,1)}, bf16[256,256]{1,0:T(8,128)(2,1)}, u32[]{:S(2)}, u32[]{:S(2)}) %collective-permute-start.31) | collective-permute-done | bytes 131104 | tf_op jit(solution)/shard_map/ppermute | solution.py:168
  54.3 2.9 %collective-permute-done.28.refs_9_ = bf16[256,256]{1,0:T(8,128)(2,1)} collective-permute-done((bf16[256,256]{1,0:T(8,128)(2,1)}, bf16[256,256]{1,0:T(8,128)(2,1)}, u32[]{:S(2)}, u32[]{:S(2)}) %collective-permute-start.28) | collective-permute-done | bytes 131104 | tf_op jit(solution)/shard_map/ppermute | solution.py:168
  57.2 0.9 copy-done.5
  58.1 0.9 copy-done.8
  59.0 0.9 copy-done.11
  59.9 0.9 copy-done.14
  60.8 0.9 copy-done.17
  61.7 0.9 copy-done.20
  62.6 7.6 %shard_map.126 = (f32[1056,1024]{1,0:T(8,128)}, bf16[1056,1024]{1,0:T(8,128)(2,1)}) custom-call(s32[8]{0:T(128)S(1)} %get-tuple-element.58.half_ref, s32[8]{0:T(128)S(1)} %get-tuple-element.57.block_ref, bf16[272,256]{1,0:T(8,128)(2,1)S(1)} %slice.24.refs_0_, bf16[256,256]{1,0:T(8,128)(2,1)S(1)} %slice.25.refs_1_, bf16[272,256]{1,0:T(8,128)(2,1)S(1)} %copy-done.8, ...), custom_call_target="tpu_custom_call" | custom-call | flops 2214592512 | bytes 6488064 | tf_op jit(solution)/shard_map/pallas_call | solution.py:312
  70.2 4.1 %pad_maximum_fusion.weight_ref.refs_16_ = bf16[2112,1024]{1,0:T(8,128)(2,1)} fusion(bf16[1056,1024]{1,0:T(8,128)(2,1)} %collective-permute-done.1, bf16[1056,1024]{1,0:T(8,128)(2,1)S(1)} %bitcast.40), kind=kLoop, calls=%fused_computation | loop fusion | flops 8650752 | bytes 8650752 | tf_op jit(solution)/shard_map/concatenate | solution.py:253
  74.4 4.8 %shard_map.121 = (bf16[272,256]{1,0:T(8,128)(2,1)S(1)}, bf16[256,256]{1,0:T(8,128)(2,1)S(1)}, bf16[272,256]{1,0:T(8,128)(2,1)S(1)}, bf16[256,256]{1,0:T(8,128)(2...) custom-call(s32[8]{0:T(128)S(1)} %get-tuple-element.58.half_ref, ...), custom_call_target="tpu_custom_call" | custom-call | flops 2214592512 | bytes 4325376 | tf_op jit(solution)/shard_map/pallas_call | solution.py:275
  79.2 2.3 %collective-permute-start.2 = (bf16[272,256]{1,0:T(8,128)(2,1)S(1)}, bf16[272,256]{1,0:T(8,128)(2,1)S(1)}, u32[]{:S(2)}, u32[]{:S(2)}) collective-permute-start(bf16[272,256]{1,0:T(8,128)(2,1)S(1)} %get-tuple-element.33), channel_id=1, source_target_pairs={{0,2},{2,4},{4,6},{6,7},{7,5},{5,3},{3,1},{1,0},{8,10},{10,12},{12... | collective-permute-start | bytes 417800 | tf_op jit(solution)/shard_map/ppermute | solution.py:186
  81.5 6.3 %shard_map.122 = (f32[256,1024]{1,0:T(8,128)S(1)}, bf16[256,1024]{1,0:T(8,128)(2,1)S(1)}) custom-call(s32[8]{0:T(128)S(1)} %get-tuple-element.58.half_ref, s32[8]{0:T(128)S(1)} %get-tuple-element.57.block_ref, bf16[272,256]{1,0:T(8,128)(2,1)S(1)} %slice.24.refs_0_, bf16[256,256]{1,0:T(8,128)(2,1)S(1)} %slice.25.refs_1_, bf16[272,256]{1,0:T(8,128)(2,1)S(1)} %copy-done.9, ...), custom_call_target="tpu_custom_call" | custom-call | flops 2214592512 | bytes 4325376 | tf_op jit(solution)/shard_map/pallas_call | solution.py:291
  88.0 1.8 %collective-permute-start.6 = (bf16[272,256]{1,0:T(8,128)(2,1)S(1)}, bf16[272,256]{1,0:T(8,128)(2,1)S(1)}, u32[]{:S(2)}, u32[]{:S(2)}) collective-permute-start(bf16[272,256]{1,0:T(8,128)(2,1)S(1)} %get-tuple-element.36), channel_id=1, source_target_pairs={{2,0},{4,2},{6,4},{7,6},{5,7},{3,5},{1,3},{0,1},{10,8},{12,10},{14... | collective-permute-start | bytes 417800 | tf_op jit(solution)/shard_map/ppermute | solution.py:187
  90.1 4.2 %collective-permute-done.12 = bf16[256,256]{1,0:T(8,128)(2,1)S(1)} collective-permute-done((bf16[256,256]{1,0:T(8,128)(2,1)S(1)}, bf16[256,256]{1,0:T(8,128)(2,1)S(1)}, u32[]{:S(2)}, u32[]{:S(2)}) %collective-permute-start.12) | collective-permute-done | bytes 131104 | tf_op jit(solution)/shard_map/ppermute | solution.py:187
  94.3 1.7 %collective-permute-start.3 = (bf16[272,256]{1,0:T(8,128)(2,1)S(1)}, bf16[272,256]{1,0:T(8,128)(2,1)S(1)}, u32[]{:S(2)}, u32[]{:S(2)}) collective-permute-start(bf16[272,256]{1,0:T(8,128)(2,1)S(1)} %add.81), channel_id=1, source_target_pairs={{0,2},{2,4},{4,6},{6,7},{7,5},{5,3},{3,1},{1,0},{8,10},{10,12},{12... | collective-permute-start | bytes 417800 | tf_op jit(solution)/shard_map/ppermute | solution.py:186
  96.6 2.4 %collective-permute-start.10 = (bf16[256,256]{1,0:T(8,128)(2,1)S(1)}, bf16[256,256]{1,0:T(8,128)(2,1)S(1)}, u32[]{:S(2)}, u32[]{:S(2)}) collective-permute-start(bf16[256,256]{1,0:T(8,128)(2,1)S(1)} %add.88), channel_id=1, source_target_pairs={{0,2},{2,4},{4,6},{6,7},{7,5},{5,3},{3,1},{1,0},{8,10},{10,12},{12... | collective-permute-start | bytes 393224 | tf_op jit(solution)/shard_map/ppermute | solution.py:186
  99.0 1.2 collective-permute-done.3
  100.3 1.9 %collective-permute-done.13 = bf16[256,256]{1,0:T(8,128)(2,1)S(1)} collective-permute-done((bf16[256,256]{1,0:T(8,128)(2,1)S(1)}, bf16[256,256]{1,0:T(8,128)(2,1)S(1)}, u32[]{:S(2)}, u32[]{:S(2)}) %collective-permute-start.13) | collective-permute-done | bytes 131104 | tf_op jit(solution)/shard_map/ppermute | solution.py:187
  103.0 1.4 collective-permute-start.14
  104.5 2.1 %collective-permute-done.7 = bf16[272,256]{1,0:T(8,128)(2,1)S(1)} collective-permute-done((bf16[272,256]{1,0:T(8,128)(2,1)S(1)}, bf16[272,256]{1,0:T(8,128)(2,1)S(1)}, u32[]{:S(2)}, u32[]{:S(2)}) %collective-permute-start.7) | collective-permute-done | bytes 139296 | tf_op jit(solution)/shard_map/ppermute | solution.py:187
  106.6 1.5 collective-permute-start.11
  108.3 1.1 collective-permute-start.8
  109.5 1.3 collective-permute-start.15
  110.8 0.9 collective-permute-start.5
  111.7 2.4 %shard_map.123 = (bf16[4,64,1024]{2,1,0:T(8,128)(2,1)}, bf16[4,2,64,128]{3,2,1,0:T(8,128)(2,1)S(1)}) custom-call(f32[256,1024]{1,0:T(8,128)S(1)} %get-tuple-element.45.own_ref, bf16[256,1024]{1,0:T(8,128)(2,1)S(1)} %collective-permute-done.32.got_ref, bf16[4,64,1024]{2,1,0:T(8,128)(2,1)S(1)} %bitcast.30, ...), custom_call_target="tpu_custom_call" | custom-call | flops 234881024 | bytes 4194304 | tf_op jit(solution)/shard_map/pallas_call | solution.py:300
  114.1 1.0 collective-permute-start.44
  115.1 1.1 collective-permute-start.40
  116.2 1.3 collective-permute-start.36
  117.5 0.8 collective-permute-start.33
  118.4 1.2 collective-permute-start.45
  119.6 1.2 collective-permute-start.41
  120.8 1.5 collective-permute-start.37
  123.0 1.5 collective-permute-start.46
  125.1 1.5 collective-permute-start.38
  127.8 1.6 %collective-permute-start.35 = (bf16[256,128]{1,0:T(8,128)(2,1)S(1)}, bf16[256,128]{1,0:T(8,128)(2,1)S(1)}, u32[]{:S(2)}, u32[]{:S(2)}) collective-permute-start(bf16[256,128]{1,0:T(8,128)(2,1)S(1)} %collective-permute-done.34.refs_2_), channel_id=1, source_target_pairs={{2,0},{4,2},{6,4},{7,6},{5,7},{3,5},{1,3},{0,1},{10,8},{12,10},{14... | collective-permute-start | bytes 196616 | tf_op jit(solution)/shard_map/ppermute | solution.py:168
  129.4 2.8 %collective-permute-done.42.refs_3_ = bf16[256,128]{1,0:T(8,128)(2,1)S(1)} collective-permute-done((bf16[256,128]{1,0:T(8,128)(2,1)S(1)}, bf16[256,128]{1,0:T(8,128)(2,1)S(1)}, u32[]{:S(2)}, u32[]{:S(2)}) %collective-permute-start.42) | collective-permute-done | bytes 65568 | tf_op jit(solution)/shard_map/ppermute | solution.py:168
  132.3 2.0 %collective-permute-start.39 = (bf16[256,128]{1,0:T(8,128)(2,1)S(1)}, bf16[256,128]{1,0:T(8,128)(2,1)S(1)}, u32[]{:S(2)}, u32[]{:S(2)}) collective-permute-start(bf16[256,128]{1,0:T(8,128)(2,1)S(1)} %collective-permute-done.38.refs_5_), channel_id=1, source_target_pairs={{0,2},{2,4},{4,6},{6,7},{7,5},{5,3},{3,1},{1,0},{8,10},{10,12},{12... | collective-permute-start | bytes 196616 | tf_op jit(solution)/shard_map/ppermute | solution.py:168
  134.3 0.7 dynamic-slice_bitcast_fusion.1.col_ref
  135.0 7.1 %collective-permute-done.43.refs_4_ = bf16[256,128]{1,0:T(8,128)(2,1)S(1)} collective-permute-done((bf16[256,128]{1,0:T(8,128)(2,1)S(1)}, bf16[256,128]{1,0:T(8,128)(2,1)S(1)}, u32[]{:S(2)}, u32[]{:S(2)}) %collective-permute-start.43) | collective-permute-done | bytes 65568 | tf_op jit(solution)/shard_map/ppermute | solution.py:168
  142.8 0.7 shard_map.124
  143.5 1.0 pad_maximum_fusion.1
  144.8 0.8 add_convert_fusion
  145.6 6.1 %add_bitcast_fusion = f32[1024,1056]{0,1:T(8,128)} fusion(f32[1056,1024]{1,0:T(8,128)} %get-tuple-element.50, bf16[1056,1024]{1,0:T(8,128)(2,1)} %collective-permute-done.47), kind=kLoop, calls=%fused_computation.1 | loop fusion | flops 2162688 | bytes 10813440 | tf_op jit(solution)/shard_map/transpose | solution.py:324
  (119 shorter events, 12.7 us)
Async XLA Ops:
  0.6 9.3 %copy-start = (bf16[1,4,2,64,1024]{4,3,2,1,0:T(8,128)(2,1)S(1)}, bf16[1,4,2,64,1024]{4,3,2,1,0:T(8,128)(2,1)}, u32[]{:S(2)}) copy-start(bf16[1,4,2,64,1024]{4,3,2,1,0:T(8,128)(2,1)} %param.10) | copy-start | bytes 3145732
  0.6 69.5 %collective-permute-start.1 = (bf16[1056,1024]{1,0:T(8,128)(2,1)}, bf16[1056,1024]{1,0:T(8,128)(2,1)}, u32[]{:S(2)}, u32[]{:S(2)}) collective-permute-start(bf16[1056,1024]{1,0:T(8,128)(2,1)} %bitcast.39), channel_id=1, source_target_pairs={{0,8},{8,0},{16,24},{24,16},{1,9},{9,1},{17,25},{25,17},{2,10},{10... | collective-permute-start | bytes 6488072 | tf_op jit(solution)/shard_map/ppermute | solution.py:253
  6.3 9.0 %collective-permute-start.17 = (bf16[528,256]{1,0:T(8,128)(2,1)}, bf16[528,256]{1,0:T(8,128)(2,1)}, u32[]{:S(2)}, u32[]{:S(2)}) collective-permute-start(bf16[528,256]{1,0:T(8,128)(2,1)} %fusion), channel_id=1, source_target_pairs={{0,0},{1,1},{2,2},{3,3},{4,16},{5,17},{6,18},{7,19},{8,8},{9,9},{1... | collective-permute-start | bytes 811016 | tf_op jit(solution)/shard_map/ppermute | solution.py:249
  10.0 1.0 copy-start.1
  12.9 29.8 %collective-permute-start = (bf16[256,1024]{1,0:T(8,128)(2,1)S(1)}, bf16[256,1024]{1,0:T(8,128)(2,1)S(1)}, u32[]{:S(2)}, u32[]{:S(2)}) collective-permute-start(bf16[256,1024]{1,0:T(8,128)(2,1)S(1)} %get-tuple-element.28.own_ref.refs_16_), channel_id=1, source_target_pairs={{0,16},{8,24},{16,0},{24,8},{1,17},{9,25},{17,1},{25,9},{2,18},{10... | collective-permute-start | bytes 1572872 | tf_op jit(solution)/shard_map/ppermute | solution.py:268
  16.2 16.4 %collective-permute-start.24 = (bf16[272,256]{1,0:T(8,128)(2,1)S(1)}, bf16[272,256]{1,0:T(8,128)(2,1)S(1)}, u32[]{:S(2)}, u32[]{:S(2)}) collective-permute-start(bf16[272,256]{1,0:T(8,128)(2,1)S(1)} %slice.24.refs_0_), channel_id=1, source_target_pairs={{0,2},{2,4},{4,6},{6,7},{7,5},{5,3},{3,1},{1,0},{8,10},{10,12},{12... | collective-permute-start | bytes 417800 | tf_op jit(solution)/shard_map/ppermute | solution.py:168
  25.3 7.3 %collective-permute-start.29 = (bf16[256,256]{1,0:T(8,128)(2,1)S(1)}, bf16[256,256]{1,0:T(8,128)(2,1)S(1)}, u32[]{:S(2)}, u32[]{:S(2)}) collective-permute-start(bf16[256,256]{1,0:T(8,128)(2,1)S(1)} %slice.25.refs_1_), channel_id=1, source_target_pairs={{0,2},{2,4},{4,6},{6,7},{7,5},{5,3},{3,1},{1,0},{8,10},{10,12},{12... | collective-permute-start | bytes 393224 | tf_op jit(solution)/shard_map/ppermute | solution.py:168
  30.0 5.7 %collective-permute-start.19 = (bf16[256,256]{1,0:T(8,128)(2,1)S(1)}, bf16[256,256]{1,0:T(8,128)(2,1)S(1)}, u32[]{:S(2)}, u32[]{:S(2)}) collective-permute-start(bf16[256,256]{1,0:T(8,128)(2,1)S(1)} %slice.25.refs_1_), channel_id=1, source_target_pairs={{2,0},{4,2},{6,4},{7,6},{5,7},{3,5},{1,3},{0,1},{10,8},{12,10},{14... | collective-permute-start | bytes 393224 | tf_op jit(solution)/shard_map/ppermute | solution.py:168
  32.6 5.7 %collective-permute-start.18 = (bf16[272,256]{1,0:T(8,128)(2,1)S(1)}, bf16[272,256]{1,0:T(8,128)(2,1)S(1)}, u32[]{:S(2)}, u32[]{:S(2)}) collective-permute-start(bf16[272,256]{1,0:T(8,128)(2,1)S(1)} %slice.24.refs_0_), channel_id=1, source_target_pairs={{2,0},{4,2},{6,4},{7,6},{5,7},{3,5},{1,3},{0,1},{10,8},{12,10},{14... | collective-permute-start | bytes 417800 | tf_op jit(solution)/shard_map/ppermute | solution.py:168
  32.6 6.7 %collective-permute-start.25 = (bf16[272,256]{1,0:T(8,128)(2,1)S(1)}, bf16[272,256]{1,0:T(8,128)(2,1)S(1)}, u32[]{:S(2)}, u32[]{:S(2)}) collective-permute-start(bf16[272,256]{1,0:T(8,128)(2,1)S(1)} %collective-permute-done.24.refs_14_), channel_id=1, source_target_pairs={{0,2},{2,4},{4,6},{6,7},{7,5},{5,3},{3,1},{1,0},{8,10},{10,12},{12... | collective-permute-start | bytes 417800 | tf_op jit(solution)/shard_map/ppermute | solution.py:168
  35.8 9.8 %collective-permute-start.21 = (bf16[256,256]{1,0:T(8,128)(2,1)S(1)}, bf16[256,256]{1,0:T(8,128)(2,1)S(1)}, u32[]{:S(2)}, u32[]{:S(2)}) collective-permute-start(bf16[256,256]{1,0:T(8,128)(2,1)S(1)} %collective-permute-done.19.refs_3_), channel_id=1, source_target_pairs={{2,0},{4,2},{6,4},{7,6},{5,7},{3,5},{1,3},{0,1},{10,8},{12,10},{14... | collective-permute-start | bytes 393224 | tf_op jit(solution)/shard_map/ppermute | solution.py:168
  38.3 7.9 %collective-permute-start.20 = (bf16[272,256]{1,0:T(8,128)(2,1)S(1)}, bf16[272,256]{1,0:T(8,128)(2,1)}, u32[]{:S(2)}, u32[]{:S(2)}) collective-permute-start(bf16[272,256]{1,0:T(8,128)(2,1)S(1)} %collective-permute-done.18.refs_2_), channel_id=1, source_target_pairs={{2,0},{4,2},{6,4},{7,6},{5,7},{3,5},{1,3},{0,1},{10,8},{12,10},{14... | collective-permute-start | bytes 417800 | tf_op jit(solution)/shard_map/ppermute | solution.py:168
  39.3 6.9 %collective-permute-start.26 = (bf16[272,256]{1,0:T(8,128)(2,1)S(1)}, bf16[272,256]{1,0:T(8,128)(2,1)}, u32[]{:S(2)}, u32[]{:S(2)}) collective-permute-start(bf16[272,256]{1,0:T(8,128)(2,1)S(1)} %collective-permute-done.25.refs_12_), channel_id=1, source_target_pairs={{0,2},{2,4},{4,6},{6,7},{7,5},{5,3},{3,1},{1,0},{8,10},{10,12},{12... | collective-permute-start | bytes 417800 | tf_op jit(solution)/shard_map/ppermute | solution.py:168
  42.8 6.2 %collective-permute-start.30 = (bf16[256,256]{1,0:T(8,128)(2,1)S(1)}, bf16[256,256]{1,0:T(8,128)(2,1)}, u32[]{:S(2)}, u32[]{:S(2)}) collective-permute-start(bf16[256,256]{1,0:T(8,128)(2,1)S(1)} %collective-permute-done.29.refs_15_), channel_id=1, source_target_pairs={{0,2},{2,4},{4,6},{6,7},{7,5},{5,3},{3,1},{1,0},{8,10},{10,12},{12... | collective-permute-start | bytes 393224 | tf_op jit(solution)/shard_map/ppermute | solution.py:168
  45.5 6.1 %collective-permute-start.23 = (bf16[256,256]{1,0:T(8,128)(2,1)S(1)}, bf16[256,256]{1,0:T(8,128)(2,1)}, u32[]{:S(2)}, u32[]{:S(2)}) collective-permute-start(bf16[256,256]{1,0:T(8,128)(2,1)S(1)} %collective-permute-done.21.refs_5_), channel_id=1, source_target_pairs={{2,0},{4,2},{6,4},{7,6},{5,7},{3,5},{1,3},{0,1},{10,8},{12,10},{14... | collective-permute-start | bytes 393224 | tf_op jit(solution)/shard_map/ppermute | solution.py:168
  46.2 8.1 %collective-permute-start.22 = (bf16[272,256]{1,0:T(8,128)(2,1)}, bf16[272,256]{1,0:T(8,128)(2,1)}, u32[]{:S(2)}, u32[]{:S(2)}) collective-permute-start(bf16[272,256]{1,0:T(8,128)(2,1)} %collective-permute-done.20.refs_4_), channel_id=1, source_target_pairs={{2,0},{4,2},{6,4},{7,6},{5,7},{3,5},{1,3},{0,1},{10,8},{12,10},{14... | collective-permute-start | bytes 417800 | tf_op jit(solution)/shard_map/ppermute | solution.py:168
  46.2 11.0 %collective-permute-start.27 = (bf16[272,256]{1,0:T(8,128)(2,1)}, bf16[272,256]{1,0:T(8,128)(2,1)}, u32[]{:S(2)}, u32[]{:S(2)}) collective-permute-start(bf16[272,256]{1,0:T(8,128)(2,1)} %collective-permute-done.26.refs_10_), channel_id=1, source_target_pairs={{0,2},{2,4},{4,6},{6,7},{7,5},{5,3},{3,1},{1,0},{8,10},{10,12},{12... | collective-permute-start | bytes 417800 | tf_op jit(solution)/shard_map/ppermute | solution.py:168
  49.0 5.3 %collective-permute-start.31 = (bf16[256,256]{1,0:T(8,128)(2,1)}, bf16[256,256]{1,0:T(8,128)(2,1)}, u32[]{:S(2)}, u32[]{:S(2)}) collective-permute-start(bf16[256,256]{1,0:T(8,128)(2,1)} %collective-permute-done.30.refs_13_), channel_id=1, source_target_pairs={{0,2},{2,4},{4,6},{6,7},{7,5},{5,3},{3,1},{1,0},{8,10},{10,12},{12... | collective-permute-start | bytes 393224 | tf_op jit(solution)/shard_map/ppermute | solution.py:168
  51.7 5.5 %collective-permute-start.28 = (bf16[256,256]{1,0:T(8,128)(2,1)}, bf16[256,256]{1,0:T(8,128)(2,1)}, u32[]{:S(2)}, u32[]{:S(2)}) collective-permute-start(bf16[256,256]{1,0:T(8,128)(2,1)} %collective-permute-done.23.refs_7_), channel_id=1, source_target_pairs={{2,0},{4,2},{6,4},{7,6},{5,7},{3,5},{1,3},{0,1},{10,8},{12,10},{14... | collective-permute-start | bytes 393224 | tf_op jit(solution)/shard_map/ppermute | solution.py:168
  57.2 0.9 copy-start.5
  58.1 0.9 copy-start.8
  59.0 0.9 copy-start.11
  60.8 0.9 copy-start.17
  61.7 0.9 copy-start.20
  62.6 7.6 %copy-start.22 = (bf16[1024,1056]{0,1:T(8,128)(2,1)S(1)}, bf16[1024,1056]{0,1:T(8,128)(2,1)}, u32[]{:S(2)}) copy-start(bf16[1024,1056]{0,1:T(8,128)(2,1)} %param.14) | copy-start | bytes 6488068
  70.2 75.4 %collective-permute-start.47 = (bf16[1056,1024]{1,0:T(8,128)(2,1)}, bf16[1056,1024]{1,0:T(8,128)(2,1)}, u32[]{:S(2)}, u32[]{:S(2)}) collective-permute-start(bf16[1056,1024]{1,0:T(8,128)(2,1)} %get-tuple-element.51), channel_id=1, source_target_pairs={{0,8},{8,0},{16,24},{24,16},{1,9},{9,1},{17,25},{25,17},{2,10},{10... | collective-permute-start | bytes 6488072 | tf_op jit(solution)/shard_map/ppermute | solution.py:323
  74.3 7.1 %copy-start.6 = (bf16[272,256]{1,0:T(8,128)(2,1)S(1)}, bf16[272,256]{1,0:T(8,128)(2,1)}, u32[]{:S(2)}) copy-start(bf16[272,256]{1,0:T(8,128)(2,1)} %copy-done.4) | copy-start | bytes 417796
  74.3 7.1 %copy-start.9 = (bf16[272,256]{1,0:T(8,128)(2,1)S(1)}, bf16[272,256]{1,0:T(8,128)(2,1)}, u32[]{:S(2)}) copy-start(bf16[272,256]{1,0:T(8,128)(2,1)} %copy-done.7) | copy-start | bytes 417796
  74.3 7.1 %copy-start.12 = (bf16[272,256]{1,0:T(8,128)(2,1)S(1)}, bf16[272,256]{1,0:T(8,128)(2,1)}, u32[]{:S(2)}) copy-start(bf16[272,256]{1,0:T(8,128)(2,1)} %copy-done.10) | copy-start | bytes 417796
  74.3 7.1 %copy-start.15 = (bf16[256,256]{1,0:T(8,128)(2,1)S(1)}, bf16[256,256]{1,0:T(8,128)(2,1)}, u32[]{:S(2)}) copy-start(bf16[256,256]{1,0:T(8,128)(2,1)} %copy-done.13) | copy-start | bytes 393220
  74.3 7.1 %copy-start.18 = (bf16[256,256]{1,0:T(8,128)(2,1)S(1)}, bf16[256,256]{1,0:T(8,128)(2,1)}, u32[]{:S(2)}) copy-start(bf16[256,256]{1,0:T(8,128)(2,1)} %copy-done.16) | copy-start | bytes 393220
  74.4 7.1 %copy-start.21 = (bf16[256,256]{1,0:T(8,128)(2,1)S(1)}, bf16[256,256]{1,0:T(8,128)(2,1)}, u32[]{:S(2)}) copy-start(bf16[256,256]{1,0:T(8,128)(2,1)} %copy-done.19) | copy-start | bytes 393220
  79.2 32.5 %copy-start.2 = (bf16[1,4,64,1024]{3,2,1,0:T(8,128)(2,1)S(1)}, bf16[1,4,64,1024]{3,2,1,0:T(8,128)(2,1)}, u32[]{:S(2)}) copy-start(bf16[1,4,64,1024]{3,2,1,0:T(8,128)(2,1)} %param.9) | copy-start | bytes 1572868
  79.2 10.6 %collective-permute-start.2 = (bf16[272,256]{1,0:T(8,128)(2,1)S(1)}, bf16[272,256]{1,0:T(8,128)(2,1)S(1)}, u32[]{:S(2)}, u32[]{:S(2)}) collective-permute-start(bf16[272,256]{1,0:T(8,128)(2,1)S(1)} %get-tuple-element.33), channel_id=1, source_target_pairs={{0,2},{2,4},{4,6},{6,7},{7,5},{5,3},{3,1},{1,0},{8,10},{10,12},{12... | collective-permute-start | bytes 417800 | tf_op jit(solution)/shard_map/ppermute | solution.py:186
  87.8 22.9 %collective-permute-start.32 = (bf16[256,1024]{1,0:T(8,128)(2,1)S(1)}, bf16[256,1024]{1,0:T(8,128)(2,1)S(1)}, u32[]{:S(2)}, u32[]{:S(2)}) collective-permute-start(bf16[256,1024]{1,0:T(8,128)(2,1)S(1)} %get-tuple-element.46), channel_id=1, source_target_pairs={{0,16},{8,24},{16,0},{24,8},{1,17},{9,25},{17,1},{25,9},{2,18},{10... | collective-permute-start | bytes 1572872 | tf_op jit(solution)/shard_map/ppermute | solution.py:299
  87.9 6.4 %collective-permute-start.12 = (bf16[256,256]{1,0:T(8,128)(2,1)S(1)}, bf16[256,256]{1,0:T(8,128)(2,1)S(1)}, u32[]{:S(2)}, u32[]{:S(2)}) collective-permute-start(bf16[256,256]{1,0:T(8,128)(2,1)S(1)} %get-tuple-element.44), channel_id=1, source_target_pairs={{2,0},{4,2},{6,4},{7,6},{5,7},{3,5},{1,3},{0,1},{10,8},{12,10},{14... | collective-permute-start | bytes 393224 | tf_op jit(solution)/shard_map/ppermute | solution.py:187
  88.0 8.6 %collective-permute-start.6 = (bf16[272,256]{1,0:T(8,128)(2,1)S(1)}, bf16[272,256]{1,0:T(8,128)(2,1)S(1)}, u32[]{:S(2)}, u32[]{:S(2)}) collective-permute-start(bf16[272,256]{1,0:T(8,128)(2,1)S(1)} %get-tuple-element.36), channel_id=1, source_target_pairs={{2,0},{4,2},{6,4},{7,6},{5,7},{3,5},{1,3},{0,1},{10,8},{12,10},{14... | collective-permute-start | bytes 417800 | tf_op jit(solution)/shard_map/ppermute | solution.py:187
  89.8 6.3 %collective-permute-start.9 = (bf16[256,256]{1,0:T(8,128)(2,1)S(1)}, bf16[256,256]{1,0:T(8,128)(2,1)S(1)}, u32[]{:S(2)}, u32[]{:S(2)}) collective-permute-start(bf16[256,256]{1,0:T(8,128)(2,1)S(1)} %get-tuple-element.40), channel_id=1, source_target_pairs={{0,2},{2,4},{4,6},{6,7},{7,5},{5,3},{3,1},{1,0},{8,10},{10,12},{12... | collective-permute-start | bytes 393224 | tf_op jit(solution)/shard_map/ppermute | solution.py:186
  94.3 5.9 %collective-permute-start.3 = (bf16[272,256]{1,0:T(8,128)(2,1)S(1)}, bf16[272,256]{1,0:T(8,128)(2,1)S(1)}, u32[]{:S(2)}, u32[]{:S(2)}) collective-permute-start(bf16[272,256]{1,0:T(8,128)(2,1)S(1)} %add.81), channel_id=1, source_target_pairs={{0,2},{2,4},{4,6},{6,7},{7,5},{5,3},{3,1},{1,0},{8,10},{10,12},{12... | collective-permute-start | bytes 417800 | tf_op jit(solution)/shard_map/ppermute | solution.py:186
  96.1 6.1 %collective-permute-start.13 = (bf16[256,256]{1,0:T(8,128)(2,1)S(1)}, bf16[256,256]{1,0:T(8,128)(2,1)S(1)}, u32[]{:S(2)}, u32[]{:S(2)}) collective-permute-start(bf16[256,256]{1,0:T(8,128)(2,1)S(1)} %add.91), channel_id=1, source_target_pairs={{2,0},{4,2},{6,4},{7,6},{5,7},{3,5},{1,3},{0,1},{10,8},{12,10},{14... | collective-permute-start | bytes 393224 | tf_op jit(solution)/shard_map/ppermute | solution.py:187
  96.6 6.5 %collective-permute-start.10 = (bf16[256,256]{1,0:T(8,128)(2,1)S(1)}, bf16[256,256]{1,0:T(8,128)(2,1)S(1)}, u32[]{:S(2)}, u32[]{:S(2)}) collective-permute-start(bf16[256,256]{1,0:T(8,128)(2,1)S(1)} %add.88), channel_id=1, source_target_pairs={{0,2},{2,4},{4,6},{6,7},{7,5},{5,3},{3,1},{1,0},{8,10},{10,12},{12... | collective-permute-start | bytes 393224 | tf_op jit(solution)/shard_map/ppermute | solution.py:186
  100.2 6.3 %collective-permute-start.7 = (bf16[272,256]{1,0:T(8,128)(2,1)S(1)}, bf16[272,256]{1,0:T(8,128)(2,1)S(1)}, u32[]{:S(2)}, u32[]{:S(2)}) collective-permute-start(bf16[272,256]{1,0:T(8,128)(2,1)S(1)} %add.85), channel_id=1, source_target_pairs={{2,0},{4,2},{6,4},{7,6},{5,7},{3,5},{1,3},{0,1},{10,8},{12,10},{14... | collective-permute-start | bytes 417800 | tf_op jit(solution)/shard_map/ppermute | solution.py:187
  102.1 7.3 %collective-permute-start.4 = (bf16[272,256]{1,0:T(8,128)(2,1)S(1)}, bf16[272,256]{1,0:T(8,128)(2,1)S(1)}, u32[]{:S(2)}, u32[]{:S(2)}) collective-permute-start(bf16[272,256]{1,0:T(8,128)(2,1)S(1)} %add.82), channel_id=1, source_target_pairs={{0,2},{2,4},{4,6},{6,7},{7,5},{5,3},{3,1},{1,0},{8,10},{10,12},{12... | collective-permute-start | bytes 417800 | tf_op jit(solution)/shard_map/ppermute | solution.py:186
  103.0 5.3 %collective-permute-start.14 = (bf16[256,256]{1,0:T(8,128)(2,1)S(1)}, bf16[256,256]{1,0:T(8,128)(2,1)S(1)}, u32[]{:S(2)}, u32[]{:S(2)}) collective-permute-start(bf16[256,256]{1,0:T(8,128)(2,1)S(1)} %add.92), channel_id=1, source_target_pairs={{2,0},{4,2},{6,4},{7,6},{5,7},{3,5},{1,3},{0,1},{10,8},{12,10},{14... | collective-permute-start | bytes 393224 | tf_op jit(solution)/shard_map/ppermute | solution.py:187
  106.6 7.5 %collective-permute-start.11 = (bf16[256,256]{1,0:T(8,128)(2,1)S(1)}, bf16[256,256]{1,0:T(8,128)(2,1)S(1)}, u32[]{:S(2)}, u32[]{:S(2)}) collective-permute-start(bf16[256,256]{1,0:T(8,128)(2,1)S(1)} %add.89), channel_id=1, source_target_pairs={{0,2},{2,4},{4,6},{6,7},{7,5},{5,3},{3,1},{1,0},{8,10},{10,12},{12... | collective-permute-start | bytes 393224 | tf_op jit(solution)/shard_map/ppermute | solution.py:186
  108.3 6.8 %collective-permute-start.8 = (bf16[272,256]{1,0:T(8,128)(2,1)S(1)}, bf16[272,256]{1,0:T(8,128)(2,1)S(1)}, u32[]{:S(2)}, u32[]{:S(2)}) collective-permute-start(bf16[272,256]{1,0:T(8,128)(2,1)S(1)} %add.86), channel_id=1, source_target_pairs={{2,0},{4,2},{6,4},{7,6},{5,7},{3,5},{1,3},{0,1},{10,8},{12,10},{14... | collective-permute-start | bytes 417800 | tf_op jit(solution)/shard_map/ppermute | solution.py:187
  109.5 6.7 %collective-permute-start.15 = (bf16[256,256]{1,0:T(8,128)(2,1)S(1)}, bf16[256,256]{1,0:T(8,128)(2,1)S(1)}, u32[]{:S(2)}, u32[]{:S(2)}) collective-permute-start(bf16[256,256]{1,0:T(8,128)(2,1)S(1)} %add.93), channel_id=1, source_target_pairs={{2,0},{4,2},{6,4},{7,6},{5,7},{3,5},{1,3},{0,1},{10,8},{12,10},{14... | collective-permute-start | bytes 393224 | tf_op jit(solution)/shard_map/ppermute | solution.py:187
  110.8 6.8 %collective-permute-start.5 = (bf16[272,256]{1,0:T(8,128)(2,1)S(1)}, bf16[272,256]{1,0:T(8,128)(2,1)S(1)}, u32[]{:S(2)}, u32[]{:S(2)}) collective-permute-start(bf16[272,256]{1,0:T(8,128)(2,1)S(1)} %add.83), channel_id=1, source_target_pairs={{0,2},{2,4},{4,6},{6,7},{7,5},{5,3},{3,1},{1,0},{8,10},{10,12},{12... | collective-permute-start | bytes 417800 | tf_op jit(solution)/shard_map/ppermute | solution.py:186
  114.1 30.7 %copy-start.23 = (bf16[1,4,64,528]{3,2,1,0:T(8,128)(2,1)S(1)}, bf16[1,4,64,528]{3,2,1,0:T(8,128)(2,1)}, u32[]{:S(2)}) copy-start(bf16[1,4,64,528]{3,2,1,0:T(8,128)(2,1)} %param.12) | copy-start | bytes 811012
  114.1 4.3 %collective-permute-start.44 = (bf16[256,128]{1,0:T(8,128)(2,1)S(1)}, bf16[256,128]{1,0:T(8,128)(2,1)S(1)}, u32[]{:S(2)}, u32[]{:S(2)}) collective-permute-start(bf16[256,128]{1,0:T(8,128)(2,1)S(1)} %bitcast.34), channel_id=1, source_target_pairs={{0,2},{2,4},{4,6},{6,7},{7,5},{5,3},{3,1},{1,0},{8,10},{10,12},{12... | collective-permute-start | bytes 196616 | tf_op jit(solution)/shard_map/ppermute | solution.py:168
  115.1 4.5 %collective-permute-start.40 = (bf16[256,128]{1,0:T(8,128)(2,1)S(1)}, bf16[256,128]{1,0:T(8,128)(2,1)S(1)}, u32[]{:S(2)}, u32[]{:S(2)}) collective-permute-start(bf16[256,128]{1,0:T(8,128)(2,1)S(1)} %bitcast.35), channel_id=1, source_target_pairs={{2,0},{4,2},{6,4},{7,6},{5,7},{3,5},{1,3},{0,1},{10,8},{12,10},{14... | collective-permute-start | bytes 196616 | tf_op jit(solution)/shard_map/ppermute | solution.py:168
  116.2 4.7 %collective-permute-start.36 = (bf16[256,128]{1,0:T(8,128)(2,1)S(1)}, bf16[256,128]{1,0:T(8,128)(2,1)S(1)}, u32[]{:S(2)}, u32[]{:S(2)}) collective-permute-start(bf16[256,128]{1,0:T(8,128)(2,1)S(1)} %bitcast.31), channel_id=1, source_target_pairs={{0,2},{2,4},{4,6},{6,7},{7,5},{5,3},{3,1},{1,0},{8,10},{10,12},{12... | collective-permute-start | bytes 196616 | tf_op jit(solution)/shard_map/ppermute | solution.py:168
  117.5 4.8 %collective-permute-start.33 = (bf16[256,128]{1,0:T(8,128)(2,1)S(1)}, bf16[256,128]{1,0:T(8,128)(2,1)S(1)}, u32[]{:S(2)}, u32[]{:S(2)}) collective-permute-start(bf16[256,128]{1,0:T(8,128)(2,1)S(1)} %bitcast.32), channel_id=1, source_target_pairs={{2,0},{4,2},{6,4},{7,6},{5,7},{3,5},{1,3},{0,1},{10,8},{12,10},{14... | collective-permute-start | bytes 196616 | tf_op jit(solution)/shard_map/ppermute | solution.py:168
  118.4 4.6 %collective-permute-start.45 = (bf16[256,128]{1,0:T(8,128)(2,1)S(1)}, bf16[256,128]{1,0:T(8,128)(2,1)S(1)}, u32[]{:S(2)}, u32[]{:S(2)}) collective-permute-start(bf16[256,128]{1,0:T(8,128)(2,1)S(1)} %collective-permute-done.44.refs_7_), channel_id=1, source_target_pairs={{0,2},{2,4},{4,6},{6,7},{7,5},{5,3},{3,1},{1,0},{8,10},{10,12},{12... | collective-permute-start | bytes 196616 | tf_op jit(solution)/shard_map/ppermute | solution.py:168
  119.6 4.8 %collective-permute-start.41 = (bf16[256,128]{1,0:T(8,128)(2,1)S(1)}, bf16[256,128]{1,0:T(8,128)(2,1)S(1)}, u32[]{:S(2)}, u32[]{:S(2)}) collective-permute-start(bf16[256,128]{1,0:T(8,128)(2,1)S(1)} %collective-permute-done.40.refs_1_), channel_id=1, source_target_pairs={{2,0},{4,2},{6,4},{7,6},{5,7},{3,5},{1,3},{0,1},{10,8},{12,10},{14... | collective-permute-start | bytes 196616 | tf_op jit(solution)/shard_map/ppermute | solution.py:168
  120.8 4.3 %collective-permute-start.37 = (bf16[256,128]{1,0:T(8,128)(2,1)S(1)}, bf16[256,128]{1,0:T(8,128)(2,1)S(1)}, u32[]{:S(2)}, u32[]{:S(2)}) collective-permute-start(bf16[256,128]{1,0:T(8,128)(2,1)S(1)} %collective-permute-done.36.refs_7_), channel_id=1, source_target_pairs={{0,2},{2,4},{4,6},{6,7},{7,5},{5,3},{3,1},{1,0},{8,10},{10,12},{12... | collective-permute-start | bytes 196616 | tf_op jit(solution)/shard_map/ppermute | solution.py:168
  122.4 4.3 %collective-permute-start.34 = (bf16[256,128]{1,0:T(8,128)(2,1)S(1)}, bf16[256,128]{1,0:T(8,128)(2,1)S(1)}, u32[]{:S(2)}, u32[]{:S(2)}) collective-permute-start(bf16[256,128]{1,0:T(8,128)(2,1)S(1)} %collective-permute-done.33.refs_1_), channel_id=1, source_target_pairs={{2,0},{4,2},{6,4},{7,6},{5,7},{3,5},{1,3},{0,1},{10,8},{12,10},{14... | collective-permute-start | bytes 196616 | tf_op jit(solution)/shard_map/ppermute | solution.py:168
  123.0 4.8 %collective-permute-start.46 = (bf16[256,128]{1,0:T(8,128)(2,1)S(1)}, bf16[256,128]{1,0:T(8,128)(2,1)S(1)}, u32[]{:S(2)}, u32[]{:S(2)}) collective-permute-start(bf16[256,128]{1,0:T(8,128)(2,1)S(1)} %collective-permute-done.45.refs_6_), channel_id=1, source_target_pairs={{0,2},{2,4},{4,6},{6,7},{7,5},{5,3},{3,1},{1,0},{8,10},{10,12},{12... | collective-permute-start | bytes 196616 | tf_op jit(solution)/shard_map/ppermute | solution.py:168
  124.5 7.8 %collective-permute-start.42 = (bf16[256,128]{1,0:T(8,128)(2,1)S(1)}, bf16[256,128]{1,0:T(8,128)(2,1)S(1)}, u32[]{:S(2)}, u32[]{:S(2)}) collective-permute-start(bf16[256,128]{1,0:T(8,128)(2,1)S(1)} %collective-permute-done.41.refs_2_), channel_id=1, source_target_pairs={{2,0},{4,2},{6,4},{7,6},{5,7},{3,5},{1,3},{0,1},{10,8},{12,10},{14... | collective-permute-start | bytes 196616 | tf_op jit(solution)/shard_map/ppermute | solution.py:168
  125.1 7.1 %collective-permute-start.38 = (bf16[256,128]{1,0:T(8,128)(2,1)S(1)}, bf16[256,128]{1,0:T(8,128)(2,1)S(1)}, u32[]{:S(2)}, u32[]{:S(2)}) collective-permute-start(bf16[256,128]{1,0:T(8,128)(2,1)S(1)} %collective-permute-done.37.refs_6_), channel_id=1, source_target_pairs={{0,2},{2,4},{4,6},{6,7},{7,5},{5,3},{3,1},{1,0},{8,10},{10,12},{12... | collective-permute-start | bytes 196616 | tf_op jit(solution)/shard_map/ppermute | solution.py:168
  126.7 17.8 %collective-permute-start.16 = (bf16[528,256]{1,0:T(8,128)(2,1)S(1)}, bf16[528,256]{1,0:T(8,128)(2,1)S(1)}, u32[]{:S(2)}, u32[]{:S(2)}) collective-permute-start(bf16[528,256]{1,0:T(8,128)(2,1)S(1)} %pad_maximum_fusion.2), channel_id=1, source_target_pairs={{0,0},{1,1},{2,2},{3,3},{4,16},{5,17},{6,18},{7,19},{8,8},{9,9},{1... | collective-permute-start | bytes 811016 | tf_op jit(solution)/shard_map/ppermute | solution.py:285
  127.8 15.0 %collective-permute-start.35 = (bf16[256,128]{1,0:T(8,128)(2,1)S(1)}, bf16[256,128]{1,0:T(8,128)(2,1)S(1)}, u32[]{:S(2)}, u32[]{:S(2)}) collective-permute-start(bf16[256,128]{1,0:T(8,128)(2,1)S(1)} %collective-permute-done.34.refs_2_), channel_id=1, source_target_pairs={{2,0},{4,2},{6,4},{7,6},{5,7},{3,5},{1,3},{0,1},{10,8},{12,10},{14... | collective-permute-start | bytes 196616 | tf_op jit(solution)/shard_map/ppermute | solution.py:168
  132.2 9.8 %collective-permute-start.43 = (bf16[256,128]{1,0:T(8,128)(2,1)S(1)}, bf16[256,128]{1,0:T(8,128)(2,1)S(1)}, u32[]{:S(2)}, u32[]{:S(2)}) collective-permute-start(bf16[256,128]{1,0:T(8,128)(2,1)S(1)} %collective-permute-done.42.refs_3_), channel_id=1, source_target_pairs={{2,0},{4,2},{6,4},{7,6},{5,7},{3,5},{1,3},{0,1},{10,8},{12,10},{14... | collective-permute-start | bytes 196616 | tf_op jit(solution)/shard_map/ppermute | solution.py:168
  132.3 10.5 %collective-permute-start.39 = (bf16[256,128]{1,0:T(8,128)(2,1)S(1)}, bf16[256,128]{1,0:T(8,128)(2,1)S(1)}, u32[]{:S(2)}, u32[]{:S(2)}) collective-permute-start(bf16[256,128]{1,0:T(8,128)(2,1)S(1)} %collective-permute-done.38.refs_5_), channel_id=1, source_target_pairs={{0,2},{2,4},{4,6},{6,7},{7,5},{5,3},{3,1},{1,0},{8,10},{10,12},{12... | collective-permute-start | bytes 196616 | tf_op jit(solution)/shard_map/ppermute | solution.py:168
  (8 other events, 5.5 us)

commit v2 on v0

--- a/solution.py
+++ b/solution.py
@@ -1,13 +1,406 @@
+import functools
 import math
 
 import jax
 import jax.numpy as jnp
 from jax import lax
+from jax.experimental import pallas as pl
+from jax.experimental.pallas import tpu as pltpu
 from jax.sharding import PartitionSpec as P
 
 HEAD_SIZE = 128
 QUERY_HEADS = 64
 KEY_VALUE_HEADS = 8
+BF = jnp.bfloat16
+F32 = jnp.float32
+VMEM = pl.BlockSpec(memory_space=pltpu.VMEM)
+SMEM = pl.BlockSpec(memory_space=pltpu.SMEM)
+NT = (((1,), (1,)), ((), ()))
+TN = (((0,), (0,)), ((), ()))
+NN = (((1,), (0,)), ((), ()))
+LIMIT = 28 * 1024 * 1024
+
+
+def dot(a, b, dims=NN):
+    return lax.dot_general(a, b, dims, preferred_element_type=F32)
+
+
+def call(kernel, out_shape, in_specs, flops, moved, scratch=(), **grid):
+    return pl.pallas_call(
+        kernel,
+        out_shape=out_shape,
+        in_specs=in_specs,
+        scratch_shapes=scratch,
+        cost_estimate=pl.CostEstimate(flops=flops, bytes_accessed=moved, transcendentals=0),
+        compiler_params=pltpu.CompilerParams(vmem_limit_bytes=LIMIT),
+        **grid,
+    )
+
+
+def stack_heads(rows, heads):
+    return jnp.concatenate(
+        [rows[:, h * HEAD_SIZE : (h + 1) * HEAD_SIZE] for h in range(heads)], axis=0
+    )
+
+
+def forward_kernel(heads, q_ref, key_value_ref, seg_ref, context_ref, probs_ref):
+    slots, length = q_ref.shape[:2]
+    row = lax.broadcasted_iota(jnp.int32, (length, length), 0)
+    col = lax.broadcasted_iota(jnp.int32, (length, length), 1)
+    for m in range(slots):
+        seg = jnp.broadcast_to(seg_ref[m : m + 1, :].astype(F32), (length, length))
+        allowed = (col <= row) & (seg == seg.T)
+        q = stack_heads(q_ref[m], heads)
+        scores = dot(q, key_value_ref[m, 0], NT) * (1.0 / math.sqrt(HEAD_SIZE))
+        scores = scores.reshape(heads, length, length)
+        masked = jnp.where(allowed[None], scores, -jnp.inf)
+        expo = jnp.exp(masked - jnp.max(masked, axis=-1, keepdims=True))
+        probs = expo / jnp.sum(expo, axis=-1, keepdims=True)
+        probs = probs.reshape(heads * length, length)
+        probs_ref[m] = probs
+        context = dot(probs.astype(BF), key_value_ref[m, 1]).astype(BF)
+        for h in range(heads):
+            context_ref[m * length : (m + 1) * length, h * HEAD_SIZE : (h + 1) * HEAD_SIZE] = (
+                context[h * length : (h + 1) * length]
+            )
+
+
+def backward_kernel(
+    heads, own_ref, got_ref, q_ref, key_value_ref, probs_ref, query_grad_ref, key_value_grad_ref
+):
+    slots, length = q_ref.shape[:2]
+    scale = 1.0 / math.sqrt(HEAD_SIZE)
+    for m in range(slots):
+        rows = slice(m * length, (m + 1) * length)
+        grad = (own_ref[rows, :] + got_ref[rows, :].astype(F32)).astype(BF)
+        grad = stack_heads(grad, heads)
+        q = stack_heads(q_ref[m], heads)
+        key, value = key_value_ref[m, 0], key_value_ref[m, 1]
+        probs = probs_ref[m]
+        prob_grad = dot(grad, value, NT)
+        delta = jnp.sum(prob_grad * probs, axis=-1, keepdims=True)
+        score_grad = probs * (prob_grad - delta)
+        high = score_grad.astype(BF)
+        low = (score_grad - high.astype(F32)).astype(BF)
+        query_grad = ((dot(high, key) + dot(low, key)) * scale).astype(BF)
+        for h in range(heads):
+            query_grad_ref[m, :, h * HEAD_SIZE : (h + 1) * HEAD_SIZE] = query_grad[
+                h * length : (h + 1) * length
+            ]
+        key_grad = (dot(high, q, TN) + dot(low, q, TN)) * scale
+        key_value_grad_ref[m, 0] = key_grad.astype(BF)
+        key_value_grad_ref[m, 1] = dot(probs.astype(BF), grad, TN).astype(BF)
+
+
+def prepare_kernel(info_ref, cot_ref, out_ref, padded):
+    slots, length, features = cot_ref.shape
+    replicas = (info_ref.shape[0] - 2) // 2
+    total = 0
+    for r in range(2, 2 + replicas):
+        total += info_ref[r] * info_ref[r + replicas]
+    live = info_ref[2 + info_ref[0]]
+    count = jnp.where(live > 0, info_ref[2 + replicas + info_ref[0]], 0)
+    total = jnp.full((length, features), jnp.maximum(total, 1), jnp.int32).astype(F32)
+    padded[:, features:] = jnp.zeros((slots * length, padded.shape[1] - features), F32)
+    for m in range(slots):
+        weight = jnp.where(jnp.full((length, features), m < count), 1.0, 0.0) / total
+        padded[m * length : (m + 1) * length, :features] = cot_ref[m].astype(F32) * weight
+    out_ref[...] = padded[...].T[:features].astype(BF)
+
+
+def finish_kernel(kept_ref, got_ref, residual_ref, out_ref, padded):
+    slots, length, features = residual_ref.shape
+    padded[:features, :] = kept_ref[...].astype(F32) + got_ref[...].astype(F32)
+    padded[features:, :] = jnp.zeros((padded.shape[0] - features, padded.shape[1]), F32)
+    rows = padded[...].T
+    for m in range(slots):
+        out_ref[m] = (
+            residual_ref[m].astype(F32) + rows[m * length : (m + 1) * length, :features]
+        ).astype(BF)
+
+
+def local_block(place_ref, mask, inner):
+    core = place_ref[0] % 2
+    index = (place_ref[1] % inner) ^ mask
+    return ((index // (inner // 2)) ^ core) * (inner // 2) + index % (inner // 2)
+
+
+def project_kernel(inner, place_ref, own_w, other_w, context_own, context_other, *refs):
+    outs, total, turned = refs[:-2], refs[-2], refs[-1]
+    step = pl.program_id(0)
+    tokens = context_own.shape[0]
+    features = own_w.shape[0]
+
+    @pl.when(step == 0)
+    def _():
+        turned[:, :tokens] = context_own[...].T
+        turned[:, tokens:] = context_other[...].T
+
+    def rows(weight):
+        at = pl.ds(pl.multiple_of(step * features, 16), features)
+        total[at, :] = dot(weight, turned[...]).astype(BF)
+
+    @pl.when(step < inner // 2)
+    def _():
+        rows(own_w[...])
+
+    @pl.when(step >= inner // 2)
+    def _():
+        rows(other_w[...])
+
+    @pl.when(step == inner - 1)
+    def _():
+        for mask in range(inner):
+            at = pl.multiple_of(local_block(place_ref, mask, inner) * features, 16)
+            block = total[pl.ds(at, features), :]
+            outs[2 * mask][...] = block[:, :tokens]
+            outs[2 * mask + 1][...] = block[:, tokens:]
+
+
+def load_shards(inner, place_ref, shards, cot, first, sems):
+    features, tokens = shards[0].shape
+    copies = []
+    for mask, shard in enumerate(shards):
+        at = pl.multiple_of(local_block(place_ref, mask, inner) * features, 16)
+        to = cot.at[pl.ds(at, features), pl.ds(first, tokens)]
+        copies.append(pltpu.make_async_copy(shard, to, sems.at[first // tokens, mask]))
+        copies[-1].start()
+    return copies
+
+
+def context_grad_kernel(inner, place_ref, own_w, other_w, *refs):
+    shards, (out_ref, cot, turned, sems) = refs[:inner], refs[-4:]
+    own_rows = own_w.shape[0]
+
+    @pl.when(pl.program_id(0) == 0)
+    def _():
+        for copy in load_shards(inner, place_ref, shards, cot, 0, sems):
+            copy.wait()
+        turned[0] = cot[:own_rows, :].T
+        turned[1] = cot[own_rows:, :].T
+
+    total = dot(turned[0], own_w[...]) + dot(turned[1], other_w[...])
+    out_ref[...] = total.astype(out_ref.dtype)
+
+
+def weight_grad_kernel(inner, place_ref, context_own, context_other, *refs):
+    shards, (own_ref, other_ref, cot, sems) = refs[: 2 * inner], refs[-4:]
+    own_rows = own_ref.shape[0]
+    tokens = context_own.shape[0]
+
+    @pl.when(pl.program_id(0) == 0)
+    def _():
+        copies = load_shards(inner, place_ref, shards[:inner], cot, 0, sems)
+        copies += load_shards(inner, place_ref, shards[inner:], cot, tokens, sems)
+        for copy in copies:
+            copy.wait()
+
+    def rows(start):
+        return dot(cot[start : start + own_rows, :tokens], context_own[...]) + dot(
+            cot[start : start + own_rows, tokens:], context_other[...]
+        )
+
+    own_ref[...] = rows(0)
+    other_ref[...] = rows(own_rows).astype(BF)
+
+
+def place_kernel(place_ref, *refs):
+    shards, (out_ref, sems) = refs[:-2], refs[-2:]
+    copies = []
+    for mask, shard in enumerate(shards):
+        at = pl.multiple_of((place_ref[1] ^ mask) * HEAD_SIZE, HEAD_SIZE)
+        copies.append(
+            pltpu.make_async_copy(shard, out_ref.at[:, pl.ds(at, HEAD_SIZE)], sems.at[mask])
+        )
+    for copy in copies:
+        copy.start()
+    for copy in copies:
+        copy.wait()
+
+
+def by_activations(
+    tensor_size,
+    queries,
+    slot_keys_values,
+    segment_ids,
+    residual_in,
+    cotangent,
+    out_weight,
+    live_mask,
+    micro_counts,
+):
+    inner = tensor_size // 2
+    _, slots, length, width = queries.shape
+    features = residual_in.shape[3]
+    heads = width // HEAD_SIZE
+    tokens = slots * length
+    dp_idx, tensor_idx = lax.axis_index("dp"), lax.axis_index("tensor")
+    place = jnp.stack([dp_idx, tensor_idx]).astype(jnp.int32)
+    info = jnp.concatenate([place, live_mask, micro_counts])
+    home = (dp_idx // 2) == (tensor_idx // inner)
+
+    def swap(array, mask):
+        return lax.ppermute(array, "tensor", [(t, t ^ mask) for t in range(tensor_size)])
+
+    def swap_x(array):
+        return lax.ppermute(array, "dp", [(d, d ^ 2) for d in range(4)])
+
+    def swap_core(array):
+        return lax.ppermute(array, "dp", [(d, d ^ 1) for d in range(4)])
+
+    shape = jax.ShapeDtypeStruct
+    wide = (features + 127) // 128 * 128
+
+    scaled = call(
+        prepare_kernel,
+        shape((features, tokens), BF),
+        [SMEM, pl.BlockSpec(cotangent.shape[1:])],
+        0,
+        4 * tokens * features,
+        [pltpu.VMEM((tokens, wide), F32)],
+    )(info, cotangent[0])
+    across = swap(scaled, inner)
+
+    weight_own = out_weight.T
+    weight_other = swap_core(weight_own)
+    own_rows = weight_own.shape[0]
+
+    key_value = lax.dynamic_slice_in_dim(
+        slot_keys_values[0], tensor_idx * HEAD_SIZE, HEAD_SIZE, axis=3
+    )
+    context, probs = call(
+        functools.partial(forward_kernel, heads),
+        (
+            shape((tokens, width), BF),
+            shape((slots, heads * length, length), F32),
+        ),
+        [pl.BlockSpec((slots, length, width)), pl.BlockSpec((slots, 2, length, HEAD_SIZE)), pl.BlockSpec((slots, length))],
+        4 * tokens * width * length,
+        4 * tokens * width * 2,
+    )(queries[0], key_value, segment_ids[0])
+    context_other = swap_x(context)
+    across, context = lax.optimization_barrier((across, context))
+    cot_own = jnp.where(home, scaled, across)
+    cot_other = swap_x(jnp.where(home, across, scaled))
+    shards_own = [swap(cot_own, mask) if mask else cot_own for mask in range(inner)]
+
+
+    big = 2 * tokens * width * 2 * own_rows
+    whole = lambda *dims: pl.BlockSpec(dims, lambda i: (0,) * len(dims))
+    anywhere = pl.BlockSpec(memory_space=pl.ANY)
+    half = inner // 2
+    partial = call(
+        functools.partial(project_kernel, inner),
+        [shape((features, tokens), BF)] * (2 * inner),
+        [
+            SMEM,
+            pl.BlockSpec((features, width), lambda i: (jnp.minimum(i, half - 1), 0)),
+            pl.BlockSpec((features, width), lambda i: (jnp.maximum(i - half, 0), 0)),
+            whole(tokens, width),
+            whole(tokens, width),
+        ],
+        2 * big,
+        4 * own_rows * width,
+        [pltpu.VMEM((2 * own_rows, 2 * tokens), BF), pltpu.VMEM((width, 2 * tokens), BF)],
+        out_specs=[whole(features, tokens)] * (2 * inner),
+        grid=(inner,),
+    )(place, weight_own, weight_other, context, context_other)
+    cot_other, partial = lax.optimization_barrier((cot_other, partial))
+    shards_other = [swap(cot_other, mask) if mask else cot_other for mask in range(inner)]
+    near, far = list(partial[::2]), partial[1::2]
+    far = [swap(far[mask], mask) if mask else far[mask] for mask in range(inner)]
+
+    tile = min(256, width)
+    column = lambda rows: pl.BlockSpec((rows, tile), lambda i: (0, i))
+
+    def context_grad(shards, dtype):
+        return call(
+            functools.partial(context_grad_kernel, inner),
+            shape((tokens, width), dtype),
+            [SMEM, column(own_rows), column(own_rows)] + [anywhere] * len(shards),
+            big,
+            4 * own_rows * width,
+            [
+                pltpu.VMEM((2 * own_rows, tokens), BF),
+                pltpu.VMEM((2, tokens, own_rows), BF),
+                pltpu.SemaphoreType.DMA((1, inner)),
+            ],
+            out_specs=column(tokens),
+            grid=(width // tile,),
+        )(place, weight_own, weight_other, *shards)
+
+    grad_own = context_grad(shards_own, F32)
+    grad_other = context_grad(shards_other + [grad_own], BF)
+    grad_got = swap_x(grad_other)
+
+    *near, _ = lax.optimization_barrier((*near, grad_other))
+    near = [swap(near[mask], mask) if mask else near[mask] for mask in range(inner)]
+    add = lambda blocks: sum(block.astype(F32) for block in blocks).astype(BF)
+    near_sum, far_sum = add(near), add(far)
+    far_got = swap_x(far_sum)
+
+    far_sum, context_late = lax.optimization_barrier((far_sum, context))
+    weight_grad, weight_grad_other = call(
+        functools.partial(weight_grad_kernel, inner),
+        (
+            shape((own_rows, width), F32),
+            shape((own_rows, width), BF),
+        ),
+        [SMEM, column(tokens), column(tokens)] + [anywhere] * (2 * inner + 1),
+        2 * big,
+        6 * own_rows * width,
+        [
+            pltpu.VMEM((2 * own_rows, 2 * tokens), BF),
+            pltpu.SemaphoreType.DMA((2, inner)),
+        ],
+        out_specs=(column(own_rows), column(own_rows)),
+        grid=(width // tile,),
+    )(place, context_late, context_other, *shards_own, *shards_other, grad_other)
+    grad_got, weight_grad_other, near_sum = lax.optimization_barrier(
+        (grad_got, weight_grad_other, near_sum)
+    )
+    query_gradient, key_value_part = call(
+        functools.partial(backward_kernel, heads),
+        (
+            shape((slots, length, width), BF),
+            shape((slots, 2, length, HEAD_SIZE), BF),
+        ),
+        [VMEM] * 5,
+        14 * tokens * width * length,
+        8 * tokens * width * 2,
+    )(grad_own, grad_got, queries[0], key_value, probs)
+    weight_grad = (weight_grad + swap_core(weight_grad_other).astype(F32)).T
+
+    rows = slots * 2 * length
+    part = key_value_part.reshape(rows, HEAD_SIZE)
+    parts = [swap(part, mask) if mask else part for mask in range(inner)]
+    far_got, _ = lax.optimization_barrier((far_got, part))
+    part = swap(part, inner)
+    kept = jnp.where(home, near_sum, far_got)
+    got = swap(jnp.where(home, far_got, near_sum), inner)
+    part, weight_grad = lax.optimization_barrier((part, weight_grad))
+    parts += [swap(part, mask) if mask else part for mask in range(inner)]
+    block_residual = call(
+        finish_kernel,
+        shape((slots, length, features), BF),
+        [VMEM] * 3,
+        0,
+        8 * tokens * features,
+        [pltpu.VMEM((wide, tokens), F32)],
+    )(kept, got, residual_in[0])[None]
+    key_value_gradient = call(
+        place_kernel,
+        shape((rows, KEY_VALUE_HEADS * HEAD_SIZE), BF),
+        [SMEM] + [pl.BlockSpec(memory_space=pl.ANY)] * tensor_size,
+        0,
+        2 * rows * KEY_VALUE_HEADS * HEAD_SIZE,
+        [pltpu.SemaphoreType.DMA((tensor_size,))],
+        out_specs=pl.BlockSpec(memory_space=pl.ANY),
+    )(place, *parts)
+    key_value_gradient = key_value_gradient.reshape(
+        1, slots, 2, length, KEY_VALUE_HEADS * HEAD_SIZE
+    )
+    return block_residual, query_gradient[None], key_value_gradient, weight_grad
 
 
 def attention_backward(query_f, key_f, value_f, probs, rounded, grad_heads):
@@ -24,7 +417,7 @@
     return (query_gradient, key_term, value_term)
 
 
-def per_device(
+def by_weights(
     queries,
     slot_keys_values,
     segment_ids,
@@ -142,6 +535,10 @@
 
 
 def solution(mesh):
+    dp_size, tensor_size = mesh.shape["dp"], mesh.shape["tensor"]
+    regular = dp_size == 4 and tensor_size % 4 == 0 and tensor_size & (tensor_size - 1) == 0
+    regular = regular and tensor_size == KEY_VALUE_HEADS
+    per_device = functools.partial(by_activations, tensor_size) if regular else by_weights
     placed = (
         P("dp", None, None, "tensor"),
         P("dp", None, None, None, None),

time: 386 us -> 106 us (0.27)
  waiting for transfers between devices: 318 us -> 33.6 us
  starting transfers between devices: 0.38 us -> 34.7 us
  Pallas kernels: 0 us -> 25.6 us
  matrix products: 24.1 us -> 0 us
  between operations: 15.5 us -> 0.78 us
  local copies, waits for them, and re-layouts: 18.3 us -> 5.33 us
  other arithmetic: 9.08 us -> 5.13 us
    all_gather x2 -> x0, waiting for transfers between devices: 124 us -> none  [the longest x1 68.8 us: per_device(): shard_piece = lax.all_gather(scaled_cot, 'tensor', axis=2, tiled=True)]
    psum x1 -> x0, waiting for transfers between devices: 77.4 us -> none  [per_device(): keyval_sum = lax.psum(positioned.astype(jnp.bfloat16), 'tensor')]
    reduce_scatter x1 -> x0, waiting for transfers between devices: 72.9 us -> none  [per_device(): lax.psum_scatter(grad_rows.astype(jnp.bfloat16), 'dp', scatter_dimension=...]
    unnamed x6 -> x0, waiting for transfers between devices: 43.7 us -> none
    ppermute x0 -> x27, starting transfers between devices: none -> 34.7 us  [the longest x21 29.1 us: swap(): lax.ppermute(array, 'tensor', [(t, t ^ mask) for t in range(tensor_size)])]
    ppermute x0 -> x27, waiting for transfers between devices: none -> 33.6 us  [the longest x21 32.3 us: swap(): lax.ppermute(array, 'tensor', [(t, t ^ mask) for t in range(tensor_size)])]
    pallas_call x0 -> x9, Pallas kernels: none -> 25.6 us  [the longest x2 7.29 us: context_grad(): call(functools.partial(context_grad_kernel, inner), shape((tokens, width)...]
    dot_general x10 -> x0, matrix products: 24.1 us -> none  [the longest x1 6.02 us: per_device(): jnp.einsum('msd,hd->msh', shard_piece, weight_back, preferred_element_typ...]
  transfers between devices with their start and end apart: 5 -> 27, of which waited for: 5 -> 14; matrix products, arithmetic and copies ran while one was open for 13% -> 5% of each run, Pallas kernels for 0% -> 23%
where the time goes in v2:
time: 106 us; the launch traced here: 105 us
  starting transfers between devices  34.7 us (33%)
  waiting for transfers between devices  33.6 us (32%)
  Pallas kernels  25.6 us (24%)
  local copies, waits for them, and re-layouts  5.33 us (5%)
  other arithmetic  5.13 us (5%)
    ppermute x21, waiting for transfers between devices, swap(): lax.ppermute(array, 'tensor', [(t, t ^ mask) for t in range(tensor_size)])  32.3 us
    ppermute x21, starting transfers between devices, swap(): lax.ppermute(array, 'tensor', [(t, t ^ mask) for t in range(tensor_size)])  29.1 us
    pallas_call x2, Pallas kernels, context_grad(): call(functools.partial(context_grad_kernel, inner), shape((tokens, width)...  7.29 us
    unnamed x20, local copies, waits for them, and re-layouts  5.3 us
    pallas_call x1, Pallas kernels, by_activations(): call(functools.partial(weight_grad_kernel, inner), (shape((own_rows, widt...  5.13 us
    ppermute x4, starting transfers between devices, swap_x(): return lax.ppermute(array, 'dp', [(d, d ^ 2) for d in range(4)])  5.05 us
    pallas_call x1, Pallas kernels, by_activations(): call(functools.partial(project_kernel, inner), [shape((features, tokens),...  4.88 us
    transpose x1, other arithmetic, by_activations(): weight_grad = (weight_grad + swap_core(weight_grad_other).astype(F32)).T  2.89 us
  transfers between devices with their start and end apart: 27, of which 14 were waited for; matrix products, arithmetic and copies ran while one was open for 5% of the time, Pallas kernels for 23%

profile of v2, /device:TPU:0, one launch (start us, length us, event | category | flops | bytes accessed | tf_op | source)
XLA Modules:
  0.0 105.2 jit_solution(1014562307474794748)
XLA Ops:
  0.6 0.0 copy-start
  0.6 0.5 collective-permute-start
  1.2 0.7 pad_add_fusion.1.info_ref
  1.9 1.0 copy-done.8
  2.9 1.4 %shard_map.111 = bf16[528,256]{1,0:T(8,128)(2,1)} custom-call(s32[10]{0:T(128)S(1)} %pad_add_fusion.1.info_ref, bf16[4,64,528]{2,1,0:T(8,128)(2,1)S(1)} %bitcast.22), custom_call_target="tpu_custom_call" | custom-call | bytes 540672 | tf_op jit(solution)/shard_map/pallas_call | solution.py:254
  4.3 3.7 %collective-permute-start.1 = (bf16[528,256]{1,0:T(8,128)(2,1)}, bf16[528,256]{1,0:T(8,128)(2,1)}, u32[]{:S(2)}, u32[]{:S(2)}) collective-permute-start(bf16[528,256]{1,0:T(8,128)(2,1)} %shard_map.111), channel_id=1, source_target_pairs={{0,4},{1,5},{2,6},{3,7},{4,0},{5,1},{6,2},{7,3},{8,12},{9,13},{10,... | collective-permute-start | bytes 811016 | tf_op jit(solution)/shard_map/ppermute | solution.py:243
  8.1 0.0 copy-start.3
  8.1 1.0 copy-done.3
  9.1 0.7 copy-done.9
  9.8 1.9 %shard_map.112 = (bf16[256,1024]{1,0:T(8,128)(2,1)}, f32[4,512,64]{2,1,0:T(8,128)S(1)}) custom-call(bf16[4,64,1024]{2,1,0:T(8,128)(2,1)S(1)} %bitcast.19, bf16[4,2,64,128]{3,2,1,0:T(8,128)(2,1)S(1)} %dynamic-slice_bitcast_fusion.key_value_ref, s32[4,64]{1,0:T(4,128)S(1)} %bitcast.28), custom_call_target="tpu_custom_call" | custom-call | flops 67108864 | bytes 2097152 | tf_op jit(solution)/shard_map/pallas_call | solution.py:271
  11.7 1.0 copy-done.5
  12.7 1.5 %collective-permute-start.3 = (bf16[256,1024]{1,0:T(8,128)(2,1)}, bf16[256,1024]{1,0:T(8,128)(2,1)}, u32[]{:S(2)}, u32[]{:S(2)}) collective-permute-start(bf16[256,1024]{1,0:T(8,128)(2,1)} %get-tuple-element.56.context_own), channel_id=1, source_target_pairs={{0,16},{8,24},{16,0},{24,8},{1,17},{9,25},{17,1},{25,9},{2,18},{10... | collective-permute-start | bytes 1572872 | tf_op jit(solution)/shard_map/ppermute | solution.py:246
  14.2 7.0 %collective-permute-done.1 = bf16[528,256]{1,0:T(8,128)(2,1)} collective-permute-done((bf16[528,256]{1,0:T(8,128)(2,1)}, bf16[528,256]{1,0:T(8,128)(2,1)}, u32[]{:S(2)}, u32[]{:S(2)}) %collective-permute-start.1) | collective-permute-done | bytes 270368 | tf_op jit(solution)/shard_map/ppermute | solution.py:243
  21.2 1.1 %broadcast_select_fusion.2 = (bf16[528,256]{1,0:T(8,128)(2,1)S(1)}, bf16[528,256]{1,0:T(8,128)(2,1)S(1)}) fusion(bf16[528,256]{1,0:T(8,128)(2,1)} %shard_map.111, bf16[528,256]{1,0:T(8,128)(2,1)} %collective-permute-done.1, pred[]{:T(512)S(6)} %eq.3), kind=kLoop, calls=%fused_computation.5 | loop fusion | flops 270336 | bytes 1081345 | tf_op jit(solution)/shard_map/jit(_where)/select_n | solution.py:283
  22.3 1.6 %collective-permute-start.2 = (bf16[528,256]{1,0:T(8,128)(2,1)S(1)}, bf16[528,256]{1,0:T(8,128)(2,1)S(1)}, u32[]{:S(2)}, u32[]{:S(2)}) collective-permute-start(bf16[528,256]{1,0:T(8,128)(2,1)S(1)} %get-tuple-element.79), channel_id=1, source_target_pairs={{0,16},{8,24},{16,0},{24,8},{1,17},{9,25},{17,1},{25,9},{2,18},{10... | collective-permute-start | bytes 811016 | tf_op jit(solution)/shard_map/ppermute | solution.py:246
  23.9 0.1 pad_add_fusion.place_ref
  24.0 1.6 %collective-permute-start.9 = (bf16[528,256]{1,0:T(8,128)(2,1)S(1)}, bf16[528,256]{1,0:T(8,128)(2,1)S(1)}, u32[]{:S(2)}, u32[]{:S(2)}) collective-permute-start(bf16[528,256]{1,0:T(8,128)(2,1)S(1)} %get-tuple-element.78.refs_0_), channel_id=1, source_target_pairs={{0,3},{1,2},{2,1},{3,0},{4,7},{5,6},{6,5},{7,4},{8,11},{9,10},{10,... | collective-permute-start | bytes 811016 | tf_op jit(solution)/shard_map/ppermute | solution.py:243
  25.6 1.4 %collective-permute-start.8 = (bf16[528,256]{1,0:T(8,128)(2,1)S(1)}, bf16[528,256]{1,0:T(8,128)(2,1)S(1)}, u32[]{:S(2)}, u32[]{:S(2)}) collective-permute-start(bf16[528,256]{1,0:T(8,128)(2,1)S(1)} %get-tuple-element.78.refs_0_), channel_id=1, source_target_pairs={{0,2},{1,3},{2,0},{3,1},{4,6},{5,7},{6,4},{7,5},{8,10},{9,11},{10,... | collective-permute-start | bytes 811016 | tf_op jit(solution)/shard_map/ppermute | solution.py:243
  26.9 0.8 collective-permute-done.3.context_other
  27.8 1.5 %collective-permute-start.7 = (bf16[528,256]{1,0:T(8,128)(2,1)S(1)}, bf16[528,256]{1,0:T(8,128)(2,1)S(1)}, u32[]{:S(2)}, u32[]{:S(2)}) collective-permute-start(bf16[528,256]{1,0:T(8,128)(2,1)S(1)} %get-tuple-element.78.refs_0_), channel_id=1, source_target_pairs={{0,1},{1,0},{2,3},{3,2},{4,5},{5,4},{6,7},{7,6},{8,9},{9,8},{10,11... | collective-permute-start | bytes 811016 | tf_op jit(solution)/shard_map/ppermute | solution.py:243
  29.3 1.6 %copy-done.1 = bf16[1024,1056]{0,1:T(8,128)(2,1)S(1)} copy-done((bf16[1024,1056]{0,1:T(8,128)(2,1)S(1)}, bf16[1024,1056]{0,1:T(8,128)(2,1)}, u32[]{:S(2)}) %copy-start.1) | copy-done | bytes 2162712
  30.9 4.9 %shard_map.113 = (bf16[528,256]{1,0:T(8,128)(2,1)S(1)}, bf16[528,256]{1,0:T(8,128)(2,1)S(1)}, bf16[528,256]{1,0:T(8,128)(2,1)S(1)}, bf16[528,256]{1,0:T(8,128)(2...) custom-call(s32[2]{0:T(128)S(1)} %pad_add_fusion.place_ref, ...), custom_call_target="tpu_custom_call" | custom-call | flops 2214592512 | bytes 4325376 | tf_op jit(solution)/shard_map/pallas_call | solution.py:292
  35.8 0.0 collective-permute-done.2.refs_0_.refs_4_
  35.8 1.6 %collective-permute-start.6 = (bf16[528,256]{1,0:T(8,128)(2,1)S(1)}, bf16[528,256]{1,0:T(8,128)(2,1)S(1)}, u32[]{:S(2)}, u32[]{:S(2)}) collective-permute-start(bf16[528,256]{1,0:T(8,128)(2,1)S(1)} %collective-permute-done.2.refs_0_.refs_4_), channel_id=1, source_target_pairs={{0,3},{1,2},{2,1},{3,0},{4,7},{5,6},{6,5},{7,4},{8,11},{9,10},{10,... | collective-permute-start | bytes 811016 | tf_op jit(solution)/shard_map/ppermute | solution.py:243
  37.4 0.4 collective-permute-start.5
  37.8 0.0 collective-permute-done.9.refs_3_
  37.8 1.5 %collective-permute-start.4 = (bf16[528,256]{1,0:T(8,128)(2,1)S(1)}, bf16[528,256]{1,0:T(8,128)(2,1)S(1)}, u32[]{:S(2)}, u32[]{:S(2)}) collective-permute-start(bf16[528,256]{1,0:T(8,128)(2,1)S(1)} %collective-permute-done.2.refs_0_.refs_4_), channel_id=1, source_target_pairs={{0,1},{1,0},{2,3},{3,2},{4,5},{5,4},{6,7},{7,6},{8,9},{9,8},{10,11... | collective-permute-start | bytes 811016 | tf_op jit(solution)/shard_map/ppermute | solution.py:243
  39.4 0.8 collective-permute-done.8.refs_2_
  40.2 2.5 %collective-permute-done.7.refs_1_ = bf16[528,256]{1,0:T(8,128)(2,1)S(1)} collective-permute-done((bf16[528,256]{1,0:T(8,128)(2,1)S(1)}, bf16[528,256]{1,0:T(8,128)(2,1)S(1)}, u32[]{:S(2)}, u32[]{:S(2)}) %collective-permute-start.7) | collective-permute-done | bytes 270368 | tf_op jit(solution)/shard_map/ppermute | solution.py:243
  42.6 0.0 collective-permute-start.12
  42.6 3.6 %collective-permute-done.6.refs_3_.refs_7_ = bf16[528,256]{1,0:T(8,128)(2,1)S(1)} collective-permute-done((bf16[528,256]{1,0:T(8,128)(2,1)S(1)}, bf16[528,256]{1,0:T(8,128)(2,1)S(1)}, u32[]{:S(2)}, u32[]{:S(2)}) %collective-permute-start.6) | collective-permute-done | bytes 270368 | tf_op jit(solution)/shard_map/ppermute | solution.py:243
  46.2 1.6 %collective-permute-start.13 = (bf16[528,256]{1,0:T(8,128)(2,1)S(1)}, bf16[528,256]{1,0:T(8,128)(2,1)S(1)}, u32[]{:S(2)}, u32[]{:S(2)}) collective-permute-start(bf16[528,256]{1,0:T(8,128)(2,1)S(1)} %get-tuple-element.55), channel_id=1, source_target_pairs={{0,3},{1,2},{2,1},{3,0},{4,7},{5,6},{6,5},{7,4},{8,11},{9,10},{10,... | collective-permute-start | bytes 811016 | tf_op jit(solution)/shard_map/ppermute | solution.py:243
  47.8 3.6 %shard_map.114.refs_4_.own_ref = f32[256,1024]{1,0:T(8,128)S(1)} custom-call(s32[2]{0:T(128)S(1)} %pad_add_fusion.place_ref, bf16[1056,1024]{1,0:T(8,128)(2,1)S(1)} %bitcast.17, bf16[1056,1024]{1,0:T(8,128)(2,1)S(1)} %collective-permute-done.other_w, bf16[528,256]{1,0:T(8,128)(2,1)S(1)} %get-tuple-element.78.refs_0_, ...), custom_call_target="tpu_custom_call" | custom-call | flops 1107296256 | bytes 4325376 | tf_op jit(solution)/shard_map/pallas_call | solution.py:317
  51.4 0.4 collective-permute-done.5.refs_2_.refs_6_
  51.8 0.0 collective-permute-done.4.refs_1_.refs_5_
  51.8 3.7 %shard_map.115.refs_8_ = bf16[256,1024]{1,0:T(8,128)(2,1)S(1)} custom-call(s32[2]{0:T(128)S(1)} %pad_add_fusion.place_ref, bf16[1056,1024]{1,0:T(8,128)(2,1)S(1)} %bitcast.18, bf16[1056,1024]{1,0:T(8,128)(2,1)S(1)} %collective-permute-done.other_w, bf16[528,256]{1,0:T(8,128)(2,1)S(1)} %collective-permute-done.2.refs_0_.refs_4_, ...), custom_call_target="tpu_custom_call" | custom-call | flops 1107296256 | bytes 4325376 | tf_op jit(solution)/shard_map/pallas_call | solution.py:317
  55.5 1.2 %collective-permute-start.10 = (bf16[256,1024]{1,0:T(8,128)(2,1)S(1)}, bf16[256,1024]{1,0:T(8,128)(2,1)S(1)}, u32[]{:S(2)}, u32[]{:S(2)}) collective-permute-start(bf16[256,1024]{1,0:T(8,128)(2,1)S(1)} %shard_map.115.refs_8_), channel_id=1, source_target_pairs={{0,16},{8,24},{16,0},{24,8},{1,17},{9,25},{17,1},{25,9},{2,18},{10... | collective-permute-start | bytes 1572872 | tf_op jit(solution)/shard_map/ppermute | solution.py:246
  56.7 1.5 %collective-permute-start.14 = (bf16[528,256]{1,0:T(8,128)(2,1)S(1)}, bf16[528,256]{1,0:T(8,128)(2,1)S(1)}, u32[]{:S(2)}, u32[]{:S(2)}) collective-permute-start(bf16[528,256]{1,0:T(8,128)(2,1)S(1)} %get-tuple-element.63), channel_id=1, source_target_pairs={{0,1},{1,0},{2,3},{3,2},{4,5},{5,4},{6,7},{7,6},{8,9},{9,8},{10,11... | collective-permute-start | bytes 811016 | tf_op jit(solution)/shard_map/ppermute | solution.py:243
  58.1 2.7 %collective-permute-done.11 = bf16[528,256]{1,0:T(8,128)(2,1)S(1)} collective-permute-done((bf16[528,256]{1,0:T(8,128)(2,1)S(1)}, bf16[528,256]{1,0:T(8,128)(2,1)S(1)}, u32[]{:S(2)}, u32[]{:S(2)}) %collective-permute-start.11) | collective-permute-done | bytes 270368 | tf_op jit(solution)/shard_map/ppermute | solution.py:243
  60.8 2.4 %collective-permute-start.16 = (bf16[528,256]{1,0:T(8,128)(2,1)S(1)}, bf16[528,256]{1,0:T(8,128)(2,1)S(1)}, u32[]{:S(2)}, u32[]{:S(2)}) collective-permute-start(bf16[528,256]{1,0:T(8,128)(2,1)S(1)} %get-tuple-element.65), channel_id=1, source_target_pairs={{0,3},{1,2},{2,1},{3,0},{4,7},{5,6},{6,5},{7,4},{8,11},{9,10},{10,... | collective-permute-start | bytes 811016 | tf_op jit(solution)/shard_map/ppermute | solution.py:243
  63.2 0.2 add_convert_fusion.1
  63.4 0.0 copy-start.4
  63.4 0.0 copy-start.6
  63.4 5.1 %shard_map.116 = (f32[1056,1024]{1,0:T(8,128)S(1)}, bf16[1056,1024]{1,0:T(8,128)(2,1)S(1)}) custom-call(s32[2]{0:T(128)S(1)} %pad_add_fusion.place_ref, bf16[256,1024]{1,0:T(8,128)(2,1)} %get-tuple-element.56.context_own, bf16[256,1024]{1,0:T(8,128)(2,1)} %collective-permute-done.3.context_other, bf16[528,256]{1,0:T(8,128)(2,1)S(1)} %get-tuple-element.78.refs_0_, ...), custom_call_target="tpu_custom_call" | custom-call | flops 2214592512 | bytes 6488064 | tf_op jit(solution)/shard_map/pallas_call | solution.py:343
  68.5 1.7 %collective-permute-done.14 = bf16[528,256]{1,0:T(8,128)(2,1)S(1)} collective-permute-done((bf16[528,256]{1,0:T(8,128)(2,1)S(1)}, bf16[528,256]{1,0:T(8,128)(2,1)S(1)}, u32[]{:S(2)}, u32[]{:S(2)}) %collective-permute-start.14) | collective-permute-done | bytes 270368 | tf_op jit(solution)/shard_map/ppermute | solution.py:243
  70.3 3.0 %collective-permute-done.16 = bf16[528,256]{1,0:T(8,128)(2,1)S(1)} collective-permute-done((bf16[528,256]{1,0:T(8,128)(2,1)S(1)}, bf16[528,256]{1,0:T(8,128)(2,1)S(1)}, u32[]{:S(2)}, u32[]{:S(2)}) %collective-permute-start.16) | collective-permute-done | bytes 270368 | tf_op jit(solution)/shard_map/ppermute | solution.py:243
  73.3 0.2 add_convert_fusion
  73.4 0.1 collective-permute-start.23
  73.5 0.7 collective-permute-start.17
  74.3 2.4 %shard_map.117 = (bf16[4,64,1024]{2,1,0:T(8,128)(2,1)}, bf16[4,2,64,128]{3,2,1,0:T(8,128)(2,1)S(1)}) custom-call(f32[256,1024]{1,0:T(8,128)S(1)} %shard_map.114.refs_4_.own_ref, bf16[256,1024]{1,0:T(8,128)(2,1)S(1)} %collective-permute-done.10.got_ref, bf16[4,64,1024]{2,1,0:T(8,128)(2,1)S(1)} %bitcast.20, ...), custom_call_target="tpu_custom_call" | custom-call | flops 234881024 | bytes 4194304 | tf_op jit(solution)/shard_map/pallas_call | solution.py:362
  76.7 2.7 %collective-permute-start.22 = (bf16[512,128]{1,0:T(8,128)(2,1)S(1)}, bf16[512,128]{1,0:T(8,128)(2,1)S(1)}, u32[]{:S(2)}, u32[]{:S(2)}) collective-permute-start(bf16[512,128]{1,0:T(8,128)(2,1)S(1)} %bitcast.23), channel_id=1, source_target_pairs={{0,4},{1,5},{2,6},{3,7},{4,0},{5,1},{6,2},{7,3},{8,12},{9,13},{10,... | collective-permute-start | bytes 393224 | tf_op jit(solution)/shard_map/ppermute | solution.py:243
  79.3 2.6 %collective-permute-start.21 = (bf16[512,128]{1,0:T(8,128)(2,1)S(1)}, bf16[512,128]{1,0:T(8,128)(2,1)S(1)}, u32[]{:S(2)}, u32[]{:S(2)}) collective-permute-start(bf16[512,128]{1,0:T(8,128)(2,1)S(1)} %bitcast.24), channel_id=1, source_target_pairs={{0,3},{1,2},{2,1},{3,0},{4,7},{5,6},{6,5},{7,4},{8,11},{9,10},{10,... | collective-permute-start | bytes 393224 | tf_op jit(solution)/shard_map/ppermute | solution.py:243
  82.0 0.4 collective-permute-done.17
  82.4 1.5 %collective-permute-start.19 = (bf16[512,128]{1,0:T(8,128)(2,1)S(1)}, bf16[512,128]{1,0:T(8,128)(2,1)S(1)}, u32[]{:S(2)}, u32[]{:S(2)}) collective-permute-start(bf16[512,128]{1,0:T(8,128)(2,1)S(1)} %bitcast.26), channel_id=1, source_target_pairs={{0,1},{1,0},{2,3},{3,2},{4,5},{5,4},{6,7},{7,6},{8,9},{9,8},{10,11... | collective-permute-start | bytes 393224 | tf_op jit(solution)/shard_map/ppermute | solution.py:243
  84.0 1.8 %collective-permute-start.18 = (bf16[528,256]{1,0:T(8,128)(2,1)S(1)}, bf16[528,256]{1,0:T(8,128)(2,1)S(1)}, u32[]{:S(2)}, u32[]{:S(2)}) collective-permute-start(bf16[528,256]{1,0:T(8,128)(2,1)S(1)} %get-tuple-element.76), channel_id=1, source_target_pairs={{0,4},{1,5},{2,6},{3,7},{4,0},{5,1},{6,2},{7,3},{8,12},{9,13},{10,... | collective-permute-start | bytes 811016 | tf_op jit(solution)/shard_map/ppermute | solution.py:243
  85.8 2.9 %add_bitcast_fusion = f32[1024,1056]{0,1:T(8,128)} fusion(f32[1056,1024]{1,0:T(8,128)S(1)} %get-tuple-element.72, bf16[1056,1024]{1,0:T(8,128)(2,1)S(1)} %collective-permute-done.23), kind=kLoop, calls=%fused_computation | loop fusion | flops 2162688 | bytes 10813440 | tf_op jit(solution)/shard_map/transpose | solution.py:372
  88.7 2.6 %collective-permute-start.26 = (bf16[512,128]{1,0:T(8,128)(2,1)S(1)}, bf16[512,128]{1,0:T(8,128)(2,1)S(1)}, u32[]{:S(2)}, u32[]{:S(2)}) collective-permute-start(bf16[512,128]{1,0:T(8,128)(2,1)S(1)} %collective-permute-done.22.refs_4_), channel_id=1, source_target_pairs={{0,3},{1,2},{2,1},{3,0},{4,7},{5,6},{6,5},{7,4},{8,11},{9,10},{10,... | collective-permute-start | bytes 393224 | tf_op jit(solution)/shard_map/ppermute | solution.py:243
  91.4 0.7 collective-permute-done.21.refs_3_
  92.0 6.6 %collective-permute-done.18.got_ref = bf16[528,256]{1,0:T(8,128)(2,1)S(1)} collective-permute-done((bf16[528,256]{1,0:T(8,128)(2,1)S(1)}, bf16[528,256]{1,0:T(8,128)(2,1)S(1)}, u32[]{:S(2)}, u32[]{:S(2)}) %collective-permute-start.18) | collective-permute-done | bytes 270368 | tf_op jit(solution)/shard_map/ppermute | solution.py:243
  98.7 0.6 collective-permute-start.24
  99.3 1.0 shard_map.118
  100.3 0.1 collective-permute-done.25.refs_6_
  100.4 3.3 %collective-permute-done.24.refs_5_ = bf16[512,128]{1,0:T(8,128)(2,1)S(1)} collective-permute-done((bf16[512,128]{1,0:T(8,128)(2,1)S(1)}, bf16[512,128]{1,0:T(8,128)(2,1)S(1)}, u32[]{:S(2)}, u32[]{:S(2)}) %collective-permute-start.24) | collective-permute-done | bytes 131104 | tf_op jit(solution)/shard_map/ppermute | solution.py:243
  103.6 1.6 %shard_map.119 = bf16[512,1024]{1,0:T(8,128)(2,1)} custom-call(s32[2]{0:T(128)S(1)} %pad_add_fusion.place_ref, bf16[512,128]{1,0:T(8,128)(2,1)S(1)} %bitcast.27, bf16[512,128]{1,0:T(8,128)(2,1)S(1)} %collective-permute-done.19.refs_1_, bf16[512,128]{1,0:T(8,128)(2,1)S(1)} %collective-permute-done.20.refs_2_, ...), custom_call_target="tpu_custom_call" | custom-call | bytes 1048576 | tf_op jit(solution)/shard_map/pallas_call | solution.py:391
  (27 shorter events, 0.1 us)
Async XLA Ops:
  0.6 7.4 %copy-start = (bf16[1,4,2,64,1024]{4,3,2,1,0:T(8,128)(2,1)S(1)}, bf16[1,4,2,64,1024]{4,3,2,1,0:T(8,128)(2,1)}, u32[]{:S(2)}) copy-start(bf16[1,4,2,64,1024]{4,3,2,1,0:T(8,128)(2,1)} %param.9) | copy-start | bytes 3145732
  0.6 28.6 %collective-permute-start = (bf16[1056,1024]{1,0:T(8,128)(2,1)}, bf16[1056,1024]{1,0:T(8,128)(2,1)S(1)}, u32[]{:S(2)}, u32[]{:S(2)}) collective-permute-start(bf16[1056,1024]{1,0:T(8,128)(2,1)} %bitcast.15), channel_id=1, source_target_pairs={{0,8},{8,0},{16,24},{24,16},{1,9},{9,1},{17,25},{25,17},{2,10},{10... | collective-permute-start | bytes 6488072 | tf_op jit(solution)/shard_map/ppermute | solution.py:249
  1.9 1.0 copy-start.8
  4.3 16.8 %collective-permute-start.1 = (bf16[528,256]{1,0:T(8,128)(2,1)}, bf16[528,256]{1,0:T(8,128)(2,1)}, u32[]{:S(2)}, u32[]{:S(2)}) collective-permute-start(bf16[528,256]{1,0:T(8,128)(2,1)} %shard_map.111), channel_id=1, source_target_pairs={{0,4},{1,5},{2,6},{3,7},{4,0},{5,1},{6,2},{7,3},{8,12},{9,13},{10,... | collective-permute-start | bytes 811016 | tf_op jit(solution)/shard_map/ppermute | solution.py:243
  8.1 1.0 copy-start.3
  9.1 0.7 copy-start.9
  11.7 1.0 copy-start.5
  12.7 15.1 %collective-permute-start.3 = (bf16[256,1024]{1,0:T(8,128)(2,1)}, bf16[256,1024]{1,0:T(8,128)(2,1)}, u32[]{:S(2)}, u32[]{:S(2)}) collective-permute-start(bf16[256,1024]{1,0:T(8,128)(2,1)} %get-tuple-element.56.context_own), channel_id=1, source_target_pairs={{0,16},{8,24},{16,0},{24,8},{1,17},{9,25},{17,1},{25,9},{2,18},{10... | collective-permute-start | bytes 1572872 | tf_op jit(solution)/shard_map/ppermute | solution.py:246
  22.3 13.5 %collective-permute-start.2 = (bf16[528,256]{1,0:T(8,128)(2,1)S(1)}, bf16[528,256]{1,0:T(8,128)(2,1)S(1)}, u32[]{:S(2)}, u32[]{:S(2)}) collective-permute-start(bf16[528,256]{1,0:T(8,128)(2,1)S(1)} %get-tuple-element.79), channel_id=1, source_target_pairs={{0,16},{8,24},{16,0},{24,8},{1,17},{9,25},{17,1},{25,9},{2,18},{10... | collective-permute-start | bytes 811016 | tf_op jit(solution)/shard_map/ppermute | solution.py:246
  24.0 13.9 %collective-permute-start.9 = (bf16[528,256]{1,0:T(8,128)(2,1)S(1)}, bf16[528,256]{1,0:T(8,128)(2,1)S(1)}, u32[]{:S(2)}, u32[]{:S(2)}) collective-permute-start(bf16[528,256]{1,0:T(8,128)(2,1)S(1)} %get-tuple-element.78.refs_0_), channel_id=1, source_target_pairs={{0,3},{1,2},{2,1},{3,0},{4,7},{5,6},{6,5},{7,4},{8,11},{9,10},{10,... | collective-permute-start | bytes 811016 | tf_op jit(solution)/shard_map/ppermute | solution.py:243
  25.6 14.6 %collective-permute-start.8 = (bf16[528,256]{1,0:T(8,128)(2,1)S(1)}, bf16[528,256]{1,0:T(8,128)(2,1)S(1)}, u32[]{:S(2)}, u32[]{:S(2)}) collective-permute-start(bf16[528,256]{1,0:T(8,128)(2,1)S(1)} %get-tuple-element.78.refs_0_), channel_id=1, source_target_pairs={{0,2},{1,3},{2,0},{3,1},{4,6},{5,7},{6,4},{7,5},{8,10},{9,11},{10,... | collective-permute-start | bytes 811016 | tf_op jit(solution)/shard_map/ppermute | solution.py:243
  27.8 14.9 %collective-permute-start.7 = (bf16[528,256]{1,0:T(8,128)(2,1)S(1)}, bf16[528,256]{1,0:T(8,128)(2,1)S(1)}, u32[]{:S(2)}, u32[]{:S(2)}) collective-permute-start(bf16[528,256]{1,0:T(8,128)(2,1)S(1)} %get-tuple-element.78.refs_0_), channel_id=1, source_target_pairs={{0,1},{1,0},{2,3},{3,2},{4,5},{5,4},{6,7},{7,6},{8,9},{9,8},{10,11... | collective-permute-start | bytes 811016 | tf_op jit(solution)/shard_map/ppermute | solution.py:243
  29.3 1.6 %copy-start.1 = (bf16[1024,1056]{0,1:T(8,128)(2,1)S(1)}, bf16[1024,1056]{0,1:T(8,128)(2,1)}, u32[]{:S(2)}) copy-start(bf16[1024,1056]{0,1:T(8,128)(2,1)} %param.13) | copy-start | bytes 6488068
  30.9 16.9 %copy-start.2 = (bf16[1024,1056]{0,1:T(8,128)(2,1)S(1)}, bf16[1024,1056]{0,1:T(8,128)(2,1)}, u32[]{:S(2)}) copy-start(bf16[1024,1056]{0,1:T(8,128)(2,1)} %param.13) | copy-start | bytes 6488068
  35.8 10.4 %collective-permute-start.6 = (bf16[528,256]{1,0:T(8,128)(2,1)S(1)}, bf16[528,256]{1,0:T(8,128)(2,1)S(1)}, u32[]{:S(2)}, u32[]{:S(2)}) collective-permute-start(bf16[528,256]{1,0:T(8,128)(2,1)S(1)} %collective-permute-done.2.refs_0_.refs_4_), channel_id=1, source_target_pairs={{0,3},{1,2},{2,1},{3,0},{4,7},{5,6},{6,5},{7,4},{8,11},{9,10},{10,... | collective-permute-start | bytes 811016 | tf_op jit(solution)/shard_map/ppermute | solution.py:243
  37.4 14.4 %collective-permute-start.5 = (bf16[528,256]{1,0:T(8,128)(2,1)S(1)}, bf16[528,256]{1,0:T(8,128)(2,1)S(1)}, u32[]{:S(2)}, u32[]{:S(2)}) collective-permute-start(bf16[528,256]{1,0:T(8,128)(2,1)S(1)} %collective-permute-done.2.refs_0_.refs_4_), channel_id=1, source_target_pairs={{0,2},{1,3},{2,0},{3,1},{4,6},{5,7},{6,4},{7,5},{8,10},{9,11},{10,... | collective-permute-start | bytes 811016 | tf_op jit(solution)/shard_map/ppermute | solution.py:243
  37.8 14.0 %collective-permute-start.4 = (bf16[528,256]{1,0:T(8,128)(2,1)S(1)}, bf16[528,256]{1,0:T(8,128)(2,1)S(1)}, u32[]{:S(2)}, u32[]{:S(2)}) collective-permute-start(bf16[528,256]{1,0:T(8,128)(2,1)S(1)} %collective-permute-done.2.refs_0_.refs_4_), channel_id=1, source_target_pairs={{0,1},{1,0},{2,3},{3,2},{4,5},{5,4},{6,7},{7,6},{8,9},{9,8},{10,11... | collective-permute-start | bytes 811016 | tf_op jit(solution)/shard_map/ppermute | solution.py:243
  40.2 20.6 %collective-permute-start.11 = (bf16[528,256]{1,0:T(8,128)(2,1)S(1)}, bf16[528,256]{1,0:T(8,128)(2,1)S(1)}, u32[]{:S(2)}, u32[]{:S(2)}) collective-permute-start(bf16[528,256]{1,0:T(8,128)(2,1)S(1)} %get-tuple-element.53), channel_id=1, source_target_pairs={{0,1},{1,0},{2,3},{3,2},{4,5},{5,4},{6,7},{7,6},{8,9},{9,8},{10,11... | collective-permute-start | bytes 811016 | tf_op jit(solution)/shard_map/ppermute | solution.py:243
  42.6 18.2 %collective-permute-start.12 = (bf16[528,256]{1,0:T(8,128)(2,1)S(1)}, bf16[528,256]{1,0:T(8,128)(2,1)S(1)}, u32[]{:S(2)}, u32[]{:S(2)}) collective-permute-start(bf16[528,256]{1,0:T(8,128)(2,1)S(1)} %get-tuple-element.54), channel_id=1, source_target_pairs={{0,2},{1,3},{2,0},{3,1},{4,6},{5,7},{6,4},{7,5},{8,10},{9,11},{10,... | collective-permute-start | bytes 811016 | tf_op jit(solution)/shard_map/ppermute | solution.py:243
  46.2 17.0 %collective-permute-start.13 = (bf16[528,256]{1,0:T(8,128)(2,1)S(1)}, bf16[528,256]{1,0:T(8,128)(2,1)S(1)}, u32[]{:S(2)}, u32[]{:S(2)}) collective-permute-start(bf16[528,256]{1,0:T(8,128)(2,1)S(1)} %get-tuple-element.55), channel_id=1, source_target_pairs={{0,3},{1,2},{2,1},{3,0},{4,7},{5,6},{6,5},{7,4},{8,11},{9,10},{10,... | collective-permute-start | bytes 811016 | tf_op jit(solution)/shard_map/ppermute | solution.py:243
  55.5 18.0 %collective-permute-start.10 = (bf16[256,1024]{1,0:T(8,128)(2,1)S(1)}, bf16[256,1024]{1,0:T(8,128)(2,1)S(1)}, u32[]{:S(2)}, u32[]{:S(2)}) collective-permute-start(bf16[256,1024]{1,0:T(8,128)(2,1)S(1)} %shard_map.115.refs_8_), channel_id=1, source_target_pairs={{0,16},{8,24},{16,0},{24,8},{1,17},{9,25},{17,1},{25,9},{2,18},{10... | collective-permute-start | bytes 1572872 | tf_op jit(solution)/shard_map/ppermute | solution.py:246
  56.7 13.6 %collective-permute-start.14 = (bf16[528,256]{1,0:T(8,128)(2,1)S(1)}, bf16[528,256]{1,0:T(8,128)(2,1)S(1)}, u32[]{:S(2)}, u32[]{:S(2)}) collective-permute-start(bf16[528,256]{1,0:T(8,128)(2,1)S(1)} %get-tuple-element.63), channel_id=1, source_target_pairs={{0,1},{1,0},{2,3},{3,2},{4,5},{5,4},{6,7},{7,6},{8,9},{9,8},{10,11... | collective-permute-start | bytes 811016 | tf_op jit(solution)/shard_map/ppermute | solution.py:243
  60.8 9.4 %collective-permute-start.15 = (bf16[528,256]{1,0:T(8,128)(2,1)S(1)}, bf16[528,256]{1,0:T(8,128)(2,1)S(1)}, u32[]{:S(2)}, u32[]{:S(2)}) collective-permute-start(bf16[528,256]{1,0:T(8,128)(2,1)S(1)} %get-tuple-element.64), channel_id=1, source_target_pairs={{0,2},{1,3},{2,0},{3,1},{4,6},{5,7},{6,4},{7,5},{8,10},{9,11},{10,... | collective-permute-start | bytes 811016 | tf_op jit(solution)/shard_map/ppermute | solution.py:243
  60.8 12.5 %collective-permute-start.16 = (bf16[528,256]{1,0:T(8,128)(2,1)S(1)}, bf16[528,256]{1,0:T(8,128)(2,1)S(1)}, u32[]{:S(2)}, u32[]{:S(2)}) collective-permute-start(bf16[528,256]{1,0:T(8,128)(2,1)S(1)} %get-tuple-element.65), channel_id=1, source_target_pairs={{0,3},{1,2},{2,1},{3,0},{4,7},{5,6},{6,5},{7,4},{8,11},{9,10},{10,... | collective-permute-start | bytes 811016 | tf_op jit(solution)/shard_map/ppermute | solution.py:243
  63.4 10.9 %copy-start.4 = (bf16[1,4,64,1024]{3,2,1,0:T(8,128)(2,1)S(1)}, bf16[1,4,64,1024]{3,2,1,0:T(8,128)(2,1)}, u32[]{:S(2)}) copy-start(bf16[1,4,64,1024]{3,2,1,0:T(8,128)(2,1)} %param.8) | copy-start | bytes 1572868
  63.4 10.9 %copy-start.6 = (f32[4,512,64]{2,1,0:T(8,128)S(1)}, f32[4,512,64]{2,1,0:T(8,128)}, u32[]{:S(2)}) copy-start(f32[4,512,64]{2,1,0:T(8,128)} %copy-done.5) | copy-start | bytes 1572868
  73.4 10.5 %collective-permute-start.23 = (bf16[1056,1024]{1,0:T(8,128)(2,1)S(1)}, bf16[1056,1024]{1,0:T(8,128)(2,1)S(1)}, u32[]{:S(2)}, u32[]{:S(2)}) collective-permute-start(bf16[1056,1024]{1,0:T(8,128)(2,1)S(1)} %get-tuple-element.73), channel_id=1, source_target_pairs={{0,8},{8,0},{16,24},{24,16},{1,9},{9,1},{17,25},{25,17},{2,10},{10... | collective-permute-start | bytes 6488072 | tf_op jit(solution)/shard_map/ppermute | solution.py:249
  73.5 8.9 %collective-permute-start.17 = (bf16[528,256]{1,0:T(8,128)(2,1)S(1)}, bf16[528,256]{1,0:T(8,128)(2,1)S(1)}, u32[]{:S(2)}, u32[]{:S(2)}) collective-permute-start(bf16[528,256]{1,0:T(8,128)(2,1)S(1)} %add_convert_fusion.1), channel_id=1, source_target_pairs={{0,16},{8,24},{16,0},{24,8},{1,17},{9,25},{17,1},{25,9},{2,18},{10... | collective-permute-start | bytes 811016 | tf_op jit(solution)/shard_map/ppermute | solution.py:246
  76.7 12.0 %collective-permute-start.22 = (bf16[512,128]{1,0:T(8,128)(2,1)S(1)}, bf16[512,128]{1,0:T(8,128)(2,1)S(1)}, u32[]{:S(2)}, u32[]{:S(2)}) collective-permute-start(bf16[512,128]{1,0:T(8,128)(2,1)S(1)} %bitcast.23), channel_id=1, source_target_pairs={{0,4},{1,5},{2,6},{3,7},{4,0},{5,1},{6,2},{7,3},{8,12},{9,13},{10,... | collective-permute-start | bytes 393224 | tf_op jit(solution)/shard_map/ppermute | solution.py:243
  79.3 12.7 %collective-permute-start.21 = (bf16[512,128]{1,0:T(8,128)(2,1)S(1)}, bf16[512,128]{1,0:T(8,128)(2,1)S(1)}, u32[]{:S(2)}, u32[]{:S(2)}) collective-permute-start(bf16[512,128]{1,0:T(8,128)(2,1)S(1)} %bitcast.24), channel_id=1, source_target_pairs={{0,3},{1,2},{2,1},{3,0},{4,7},{5,6},{6,5},{7,4},{8,11},{9,10},{10,... | collective-permute-start | bytes 393224 | tf_op jit(solution)/shard_map/ppermute | solution.py:243
  82.0 18.3 %collective-permute-start.20 = (bf16[512,128]{1,0:T(8,128)(2,1)S(1)}, bf16[512,128]{1,0:T(8,128)(2,1)S(1)}, u32[]{:S(2)}, u32[]{:S(2)}) collective-permute-start(bf16[512,128]{1,0:T(8,128)(2,1)S(1)} %bitcast.25), channel_id=1, source_target_pairs={{0,2},{1,3},{2,0},{3,1},{4,6},{5,7},{6,4},{7,5},{8,10},{9,11},{10,... | collective-permute-start | bytes 393224 | tf_op jit(solution)/shard_map/ppermute | solution.py:243
  82.4 17.8 %collective-permute-start.19 = (bf16[512,128]{1,0:T(8,128)(2,1)S(1)}, bf16[512,128]{1,0:T(8,128)(2,1)S(1)}, u32[]{:S(2)}, u32[]{:S(2)}) collective-permute-start(bf16[512,128]{1,0:T(8,128)(2,1)S(1)} %bitcast.26), channel_id=1, source_target_pairs={{0,1},{1,0},{2,3},{3,2},{4,5},{5,4},{6,7},{7,6},{8,9},{9,8},{10,11... | collective-permute-start | bytes 393224 | tf_op jit(solution)/shard_map/ppermute | solution.py:243
  84.0 14.7 %collective-permute-start.18 = (bf16[528,256]{1,0:T(8,128)(2,1)S(1)}, bf16[528,256]{1,0:T(8,128)(2,1)S(1)}, u32[]{:S(2)}, u32[]{:S(2)}) collective-permute-start(bf16[528,256]{1,0:T(8,128)(2,1)S(1)} %get-tuple-element.76), channel_id=1, source_target_pairs={{0,4},{1,5},{2,6},{3,7},{4,0},{5,1},{6,2},{7,3},{8,12},{9,13},{10,... | collective-permute-start | bytes 811016 | tf_op jit(solution)/shard_map/ppermute | solution.py:243
  85.8 13.4 %copy-start.7 = (bf16[1,4,64,528]{3,2,1,0:T(8,128)(2,1)S(1)}, bf16[1,4,64,528]{3,2,1,0:T(8,128)(2,1)}, u32[]{:S(2)}) copy-start(bf16[1,4,64,528]{3,2,1,0:T(8,128)(2,1)} %param.11) | copy-start | bytes 811012
  88.7 11.5 %collective-permute-start.26 = (bf16[512,128]{1,0:T(8,128)(2,1)S(1)}, bf16[512,128]{1,0:T(8,128)(2,1)S(1)}, u32[]{:S(2)}, u32[]{:S(2)}) collective-permute-start(bf16[512,128]{1,0:T(8,128)(2,1)S(1)} %collective-permute-done.22.refs_4_), channel_id=1, source_target_pairs={{0,3},{1,2},{2,1},{3,0},{4,7},{5,6},{6,5},{7,4},{8,11},{9,10},{10,... | collective-permute-start | bytes 393224 | tf_op jit(solution)/shard_map/ppermute | solution.py:243
  92.0 8.4 %collective-permute-start.25 = (bf16[512,128]{1,0:T(8,128)(2,1)S(1)}, bf16[512,128]{1,0:T(8,128)(2,1)S(1)}, u32[]{:S(2)}, u32[]{:S(2)}) collective-permute-start(bf16[512,128]{1,0:T(8,128)(2,1)S(1)} %collective-permute-done.22.refs_4_), channel_id=1, source_target_pairs={{0,2},{1,3},{2,0},{3,1},{4,6},{5,7},{6,4},{7,5},{8,10},{9,11},{10,... | collective-permute-start | bytes 393224 | tf_op jit(solution)/shard_map/ppermute | solution.py:243
  98.7 5.0 %collective-permute-start.24 = (bf16[512,128]{1,0:T(8,128)(2,1)S(1)}, bf16[512,128]{1,0:T(8,128)(2,1)S(1)}, u32[]{:S(2)}, u32[]{:S(2)}) collective-permute-start(bf16[512,128]{1,0:T(8,128)(2,1)S(1)} %collective-permute-done.22.refs_4_), channel_id=1, source_target_pairs={{0,1},{1,0},{2,3},{3,2},{4,5},{5,4},{6,7},{7,6},{8,9},{9,8},{10,11... | collective-permute-start | bytes 393224 | tf_op jit(solution)/shard_map/ppermute | solution.py:243

commit v3 on v2

--- a/solution.py
+++ b/solution.py
@@ -92,19 +92,11 @@
         key_value_grad_ref[m, 1] = dot(probs.astype(BF), grad, TN).astype(BF)
 
 
-def prepare_kernel(info_ref, cot_ref, out_ref, padded):
+def turn_kernel(cot_ref, out_ref, padded):
     slots, length, features = cot_ref.shape
-    replicas = (info_ref.shape[0] - 2) // 2
-    total = 0
-    for r in range(2, 2 + replicas):
-        total += info_ref[r] * info_ref[r + replicas]
-    live = info_ref[2 + info_ref[0]]
-    count = jnp.where(live > 0, info_ref[2 + replicas + info_ref[0]], 0)
-    total = jnp.full((length, features), jnp.maximum(total, 1), jnp.int32).astype(F32)
     padded[:, features:] = jnp.zeros((slots * length, padded.shape[1] - features), F32)
     for m in range(slots):
-        weight = jnp.where(jnp.full((length, features), m < count), 1.0, 0.0) / total
-        padded[m * length : (m + 1) * length, :features] = cot_ref[m].astype(F32) * weight
+        padded[m * length : (m + 1) * length, :features] = cot_ref[m].astype(F32)
     out_ref[...] = padded[...].T[:features].astype(BF)
 
 
@@ -216,6 +208,16 @@
         copy.start()
     for copy in copies:
         copy.wait()
+
+
+def slot_weights(live_mask, micro_counts, slots):
+    replica = lax.axis_index("dp")
+    pick = jnp.arange(live_mask.shape[0]) == replica
+    my_live = jnp.sum(jnp.where(pick, live_mask, 0))
+    my_count = jnp.sum(jnp.where(pick, micro_counts, 0))
+    live_total = jnp.maximum(jnp.sum(live_mask * micro_counts), 1)
+    slot_live = (jnp.arange(slots) < my_count) & (my_live > 0)
+    return slot_live.astype(F32) / live_total.astype(F32)
 
 
 def by_activations(
@@ -236,7 +238,6 @@
     tokens = slots * length
     dp_idx, tensor_idx = lax.axis_index("dp"), lax.axis_index("tensor")
     place = jnp.stack([dp_idx, tensor_idx]).astype(jnp.int32)
-    info = jnp.concatenate([place, live_mask, micro_counts])
     home = (dp_idx // 2) == (tensor_idx // inner)
 
     def swap(array, mask):
@@ -251,15 +252,15 @@
     shape = jax.ShapeDtypeStruct
     wide = (features + 127) // 128 * 128
 
-    scaled = call(
-        prepare_kernel,
+    turned = call(
+        turn_kernel,
         shape((features, tokens), BF),
-        [SMEM, pl.BlockSpec(cotangent.shape[1:])],
+        [pl.BlockSpec(cotangent.shape[1:])],
         0,
         4 * tokens * features,
         [pltpu.VMEM((tokens, wide), F32)],
-    )(info, cotangent[0])
-    across = swap(scaled, inner)
+    )(cotangent[0])
+    across = swap(turned, inner)
 
     weight_own = out_weight.T
     weight_other = swap_core(weight_own)
@@ -280,10 +281,14 @@
     )(queries[0], key_value, segment_ids[0])
     context_other = swap_x(context)
     across, context = lax.optimization_barrier((across, context))
-    cot_own = jnp.where(home, scaled, across)
-    cot_other = swap_x(jnp.where(home, across, scaled))
+    weight = jnp.repeat(slot_weights(live_mask, micro_counts, slots), length)
+    scaled = lambda array: (array.astype(F32) * weight[None, :]).astype(BF)
+    cot_own = scaled(jnp.where(home, turned, across))
+    cot_other = swap_x(scaled(jnp.where(home, across, turned)))
     shards_own = [swap(cot_own, mask) if mask else cot_own for mask in range(inner)]
 
+
+    cot_other, context_other = lax.optimization_barrier((cot_other, context_other))
 
     big = 2 * tokens * width * 2 * own_rows
     whole = lambda *dims: pl.BlockSpec(dims, lambda i: (0,) * len(dims))
@@ -305,7 +310,6 @@
         out_specs=[whole(features, tokens)] * (2 * inner),
         grid=(inner,),
     )(place, weight_own, weight_other, context, context_other)
-    cot_other, partial = lax.optimization_barrier((cot_other, partial))
     shards_other = [swap(cot_other, mask) if mask else cot_other for mask in range(inner)]
     near, far = list(partial[::2]), partial[1::2]
     far = [swap(far[mask], mask) if mask else far[mask] for mask in range(inner)]
@@ -356,8 +360,8 @@
         out_specs=(column(own_rows), column(own_rows)),
         grid=(width // tile,),
     )(place, context_late, context_other, *shards_own, *shards_other, grad_other)
-    grad_got, weight_grad_other, near_sum = lax.optimization_barrier(
-        (grad_got, weight_grad_other, near_sum)
+    grad_got, weight_grad_other, near_sum, far_got = lax.optimization_barrier(
+        (grad_got, weight_grad_other, near_sum, far_got)
     )
     query_gradient, key_value_part = call(
         functools.partial(backward_kernel, heads),
@@ -374,12 +378,12 @@
     rows = slots * 2 * length
     part = key_value_part.reshape(rows, HEAD_SIZE)
     parts = [swap(part, mask) if mask else part for mask in range(inner)]
-    far_got, _ = lax.optimization_barrier((far_got, part))
     part = swap(part, inner)
+    part, weight_grad = lax.optimization_barrier((part, weight_grad))
+    parts += [swap(part, mask) if mask else part for mask in range(inner)]
     kept = jnp.where(home, near_sum, far_got)
     got = swap(jnp.where(home, far_got, near_sum), inner)
-    part, weight_grad = lax.optimization_barrier((part, weight_grad))
-    parts += [swap(part, mask) if mask else part for mask in range(inner)]
+    got, parts[1], parts[2], parts[3] = lax.optimization_barrier((got, parts[1], parts[2], parts[3]))
     block_residual = call(
         finish_kernel,
         shape((slots, length, features), BF),

time: 106 us -> 101 us (0.953)
  waiting for transfers between devices: 33.6 us -> 26.9 us
  between operations: 0.78 us -> 2.19 us
  other arithmetic: 5.13 us -> 6.32 us
    ppermute x21, waiting for transfers between devices: 32.3 us -> 22.7 us  [swap(): lax.ppermute(array, 'tensor', [(t, t ^ mask) for t in range(tensor_size)])]
    ppermute x4, waiting for transfers between devices: 1.27 us -> 4.18 us  [swap_x(): return lax.ppermute(array, 'dp', [(d, d ^ 2) for d in range(4)])]
    reduce_sum x0 -> x1, other arithmetic: none -> 1.38 us  [slot_weights(): my_count = jnp.sum(jnp.where(pick, micro_counts, 0))]
    convert_element_type x0 -> x1, other arithmetic: none -> 1.18 us  [by_activations(): scaled = lambda array: (array.astype(F32) * weight[None, :]).astype(BF)]
    select_n x1 -> x0, other arithmetic: 1.07 us -> none  [by_activations(): cot_own = jnp.where(home, scaled, across)]
  transfers between devices with their start and end apart: 27 -> 27, of which waited for: 14 -> 14; matrix products, arithmetic and copies ran while one was open for 5% -> 6% of each run, Pallas kernels for 23% -> 23%
where the time goes in v3:
time: 101 us; the launch traced here: 100 us
  starting transfers between devices  34.6 us (34%)
  waiting for transfers between devices  26.9 us (27%)
  Pallas kernels  24.9 us (25%)
  other arithmetic  6.32 us (6%)
  local copies, waits for them, and re-layouts  5.49 us (5%)
  between operations  2.19 us (2%)
    ppermute x21, starting transfers between devices, swap(): lax.ppermute(array, 'tensor', [(t, t ^ mask) for t in range(tensor_size)])  29.6 us
    ppermute x21, waiting for transfers between devices, swap(): lax.ppermute(array, 'tensor', [(t, t ^ mask) for t in range(tensor_size)])  22.7 us
    pallas_call x2, Pallas kernels, context_grad(): call(functools.partial(context_grad_kernel, inner), shape((tokens, width)...  7.29 us
    unnamed x20, local copies, waits for them, and re-layouts  5.3 us
    pallas_call x1, Pallas kernels, by_activations(): call(functools.partial(weight_grad_kernel, inner), (shape((own_rows, widt...  4.99 us
    pallas_call x1, Pallas kernels, by_activations(): call(functools.partial(project_kernel, inner), [shape((features, tokens),...  4.88 us
    ppermute x4, starting transfers between devices, swap_x(): return lax.ppermute(array, 'dp', [(d, d ^ 2) for d in range(4)])  4.36 us
    ppermute x4, waiting for transfers between devices, swap_x(): return lax.ppermute(array, 'dp', [(d, d ^ 2) for d in range(4)])  4.18 us
  transfers between devices with their start and end apart: 27, of which 14 were waited for; matrix products, arithmetic and copies ran while one was open for 6% of the time, Pallas kernels for 23%

profile of v3, /device:TPU:0, one launch (start us, length us, event | category | flops | bytes accessed | tf_op | source)
XLA Modules:
  0.0 100.4 jit_solution(672742354361813258)
XLA Ops:
  0.6 0.0 copy-start
  0.6 0.5 collective-permute-start
  1.2 1.0 copy-done.8
  2.1 0.9 shard_map.111
  3.0 3.7 %collective-permute-start.1 = (bf16[528,256]{1,0:T(8,128)(2,1)}, bf16[528,256]{1,0:T(8,128)(2,1)}, u32[]{:S(2)}, u32[]{:S(2)}) collective-permute-start(bf16[528,256]{1,0:T(8,128)(2,1)} %shard_map.111), channel_id=1, source_target_pairs={{0,4},{1,5},{2,6},{3,7},{4,0},{5,1},{6,2},{7,3},{8,12},{9,13},{10,... | collective-permute-start | bytes 811016 | tf_op jit(solution)/shard_map/ppermute | solution.py:244
  6.7 1.0 %copy-done.3 = bf16[1,4,64,1024]{3,2,1,0:T(8,128)(2,1)S(1)} copy-done((bf16[1,4,64,1024]{3,2,1,0:T(8,128)(2,1)S(1)}, bf16[1,4,64,1024]{3,2,1,0:T(8,128)(2,1)}, u32[]{:S(2)}) %copy-start.3) | copy-done | bytes 524312
  7.8 0.7 copy-done.9
  8.5 1.9 %shard_map.112 = (bf16[256,1024]{1,0:T(8,128)(2,1)}, f32[4,512,64]{2,1,0:T(8,128)S(1)}) custom-call(bf16[4,64,1024]{2,1,0:T(8,128)(2,1)S(1)} %bitcast.19, bf16[4,2,64,128]{3,2,1,0:T(8,128)(2,1)S(1)} %dynamic-slice_bitcast_fusion.key_value_ref, s32[4,64]{1,0:T(4,128)S(1)} %bitcast.28), custom_call_target="tpu_custom_call" | custom-call | flops 67108864 | bytes 2097152 | tf_op jit(solution)/shard_map/pallas_call | solution.py:272
  10.4 1.0 copy-done.5
  11.4 1.5 %collective-permute-start.3 = (bf16[256,1024]{1,0:T(8,128)(2,1)}, bf16[256,1024]{1,0:T(8,128)(2,1)}, u32[]{:S(2)}, u32[]{:S(2)}) collective-permute-start(bf16[256,1024]{1,0:T(8,128)(2,1)} %get-tuple-element.46.context_own), channel_id=1, source_target_pairs={{0,16},{8,24},{16,0},{24,8},{1,17},{9,25},{17,1},{25,9},{2,18},{10... | collective-permute-start | bytes 1572872 | tf_op jit(solution)/shard_map/ppermute | solution.py:247
  12.9 1.4 %fusion = (s32[]{:T(128)}, s32[]{:T(128)}, s32[]{:T(128)}) fusion(s32[4]{0:T(128)} %param.15, s32[]{:T(128)} %axis_index.27, s32[4]{0:T(128)} %param.14), kind=kLoop, calls=%fused_computation.11 | loop fusion | flops 25 | bytes 48 | tf_op jit(solution)/shard_map/reduce_sum | solution.py:217
  15.6 0.6 and_select_fusion
  16.2 0.1 broadcast_in_dim.15
  16.2 0.1 mul.24
  16.3 3.5 %collective-permute-done.1 = bf16[528,256]{1,0:T(8,128)(2,1)} collective-permute-done((bf16[528,256]{1,0:T(8,128)(2,1)}, bf16[528,256]{1,0:T(8,128)(2,1)}, u32[]{:S(2)}, u32[]{:S(2)}) %collective-permute-start.1) | collective-permute-done | bytes 270368 | tf_op jit(solution)/shard_map/ppermute | solution.py:244
  19.9 1.2 %multiply_convert_fusion = (bf16[528,256]{1,0:T(8,128)(2,1)S(1)}, bf16[528,256]{1,0:T(8,128)(2,1)S(1)}) fusion(bf16[528,256]{1,0:T(8,128)(2,1)} %shard_map.111, bf16[528,256]{1,0:T(8,128)(2,1)} %collective-permute-done.1, f32[256]{0:T(256)S(1)} %mul.24, pred[]{:T(512)S(6)} %eq.9), kind=kLoop, calls=%fused_computation.3 | loop fusion | flops 1081344 | bytes 1082369 | tf_op jit(solution)/shard_map/convert_element_type | solution.py:285
  21.0 1.6 %collective-permute-start.2 = (bf16[528,256]{1,0:T(8,128)(2,1)S(1)}, bf16[528,256]{1,0:T(8,128)(2,1)S(1)}, u32[]{:S(2)}, u32[]{:S(2)}) collective-permute-start(bf16[528,256]{1,0:T(8,128)(2,1)S(1)} %get-tuple-element.74), channel_id=1, source_target_pairs={{0,16},{8,24},{16,0},{24,8},{1,17},{9,25},{17,1},{25,9},{2,18},{10... | collective-permute-start | bytes 811016 | tf_op jit(solution)/shard_map/ppermute | solution.py:247
  22.7 1.6 %collective-permute-start.9 = (bf16[528,256]{1,0:T(8,128)(2,1)S(1)}, bf16[528,256]{1,0:T(8,128)(2,1)S(1)}, u32[]{:S(2)}, u32[]{:S(2)}) collective-permute-start(bf16[528,256]{1,0:T(8,128)(2,1)S(1)} %get-tuple-element.73.refs_0_), channel_id=1, source_target_pairs={{0,3},{1,2},{2,1},{3,0},{4,7},{5,6},{6,5},{7,4},{8,11},{9,10},{10,... | collective-permute-start | bytes 811016 | tf_op jit(solution)/shard_map/ppermute | solution.py:244
  24.3 1.4 %collective-permute-start.8 = (bf16[528,256]{1,0:T(8,128)(2,1)S(1)}, bf16[528,256]{1,0:T(8,128)(2,1)S(1)}, u32[]{:S(2)}, u32[]{:S(2)}) collective-permute-start(bf16[528,256]{1,0:T(8,128)(2,1)S(1)} %get-tuple-element.73.refs_0_), channel_id=1, source_target_pairs={{0,2},{1,3},{2,0},{3,1},{4,6},{5,7},{6,4},{7,5},{8,10},{9,11},{10,... | collective-permute-start | bytes 811016 | tf_op jit(solution)/shard_map/ppermute | solution.py:244
  25.7 0.8 collective-permute-done.3.context_other
  26.4 1.5 %collective-permute-start.7 = (bf16[528,256]{1,0:T(8,128)(2,1)S(1)}, bf16[528,256]{1,0:T(8,128)(2,1)S(1)}, u32[]{:S(2)}, u32[]{:S(2)}) collective-permute-start(bf16[528,256]{1,0:T(8,128)(2,1)S(1)} %get-tuple-element.73.refs_0_), channel_id=1, source_target_pairs={{0,1},{1,0},{2,3},{3,2},{4,5},{5,4},{6,7},{7,6},{8,9},{9,8},{10,11... | collective-permute-start | bytes 811016 | tf_op jit(solution)/shard_map/ppermute | solution.py:244
  28.0 3.4 %collective-permute-done.2.refs_0_.refs_4_ = bf16[528,256]{1,0:T(8,128)(2,1)S(1)} collective-permute-done((bf16[528,256]{1,0:T(8,128)(2,1)S(1)}, bf16[528,256]{1,0:T(8,128)(2,1)S(1)}, u32[]{:S(2)}, u32[]{:S(2)}) %collective-permute-start.2) | collective-permute-done | bytes 270368 | tf_op jit(solution)/shard_map/ppermute | solution.py:247
  31.4 2.5 %collective-permute-start.6 = (bf16[528,256]{1,0:T(8,128)(2,1)S(1)}, bf16[528,256]{1,0:T(8,128)(2,1)S(1)}, u32[]{:S(2)}, u32[]{:S(2)}) collective-permute-start(bf16[528,256]{1,0:T(8,128)(2,1)S(1)} %collective-permute-done.2.refs_0_.refs_4_), channel_id=1, source_target_pairs={{0,3},{1,2},{2,1},{3,0},{4,7},{5,6},{6,5},{7,4},{8,11},{9,10},{10,... | collective-permute-start | bytes 811016 | tf_op jit(solution)/shard_map/ppermute | solution.py:244
  33.9 0.1 pad_add_fusion.place_ref
  34.0 0.5 collective-permute-start.5
  34.4 0.8 collective-permute-start.4
  35.2 1.6 %copy-done.1 = bf16[1024,1056]{0,1:T(8,128)(2,1)S(1)} copy-done((bf16[1024,1056]{0,1:T(8,128)(2,1)S(1)}, bf16[1024,1056]{0,1:T(8,128)(2,1)}, u32[]{:S(2)}) %copy-start.1) | copy-done | bytes 2162712
  36.8 4.9 %shard_map.115 = (bf16[528,256]{1,0:T(8,128)(2,1)S(1)}, bf16[528,256]{1,0:T(8,128)(2,1)S(1)}, bf16[528,256]{1,0:T(8,128)(2,1)S(1)}, bf16[528,256]{1,0:T(8,128)(2...) custom-call(s32[2]{0:T(128)S(1)} %pad_add_fusion.place_ref, ...), custom_call_target="tpu_custom_call" | custom-call | flops 2214592512 | bytes 4325376 | tf_op jit(solution)/shard_map/pallas_call | solution.py:297
  41.7 1.3 %collective-permute-start.11 = (bf16[528,256]{1,0:T(8,128)(2,1)S(1)}, bf16[528,256]{1,0:T(8,128)(2,1)S(1)}, u32[]{:S(2)}, u32[]{:S(2)}) collective-permute-start(bf16[528,256]{1,0:T(8,128)(2,1)S(1)} %get-tuple-element.43), channel_id=1, source_target_pairs={{0,1},{1,0},{2,3},{3,2},{4,5},{5,4},{6,7},{7,6},{8,9},{9,8},{10,11... | collective-permute-start | bytes 811016 | tf_op jit(solution)/shard_map/ppermute | solution.py:244
  43.0 1.6 %collective-permute-start.12 = (bf16[528,256]{1,0:T(8,128)(2,1)S(1)}, bf16[528,256]{1,0:T(8,128)(2,1)S(1)}, u32[]{:S(2)}, u32[]{:S(2)}) collective-permute-start(bf16[528,256]{1,0:T(8,128)(2,1)S(1)} %get-tuple-element.44), channel_id=1, source_target_pairs={{0,2},{1,3},{2,0},{3,1},{4,6},{5,7},{6,4},{7,5},{8,10},{9,11},{10,... | collective-permute-start | bytes 811016 | tf_op jit(solution)/shard_map/ppermute | solution.py:244
  44.6 0.1 collective-permute-done.6.refs_3_.refs_7_
  44.7 1.6 %collective-permute-start.13 = (bf16[528,256]{1,0:T(8,128)(2,1)S(1)}, bf16[528,256]{1,0:T(8,128)(2,1)S(1)}, u32[]{:S(2)}, u32[]{:S(2)}) collective-permute-start(bf16[528,256]{1,0:T(8,128)(2,1)S(1)} %get-tuple-element.45), channel_id=1, source_target_pairs={{0,3},{1,2},{2,1},{3,0},{4,7},{5,6},{6,5},{7,4},{8,11},{9,10},{10,... | collective-permute-start | bytes 811016 | tf_op jit(solution)/shard_map/ppermute | solution.py:244
  46.2 3.6 %shard_map.113.refs_4_.own_ref = f32[256,1024]{1,0:T(8,128)S(1)} custom-call(s32[2]{0:T(128)S(1)} %pad_add_fusion.place_ref, bf16[1056,1024]{1,0:T(8,128)(2,1)S(1)} %bitcast.17, bf16[1056,1024]{1,0:T(8,128)(2,1)S(1)} %collective-permute-done.other_w, bf16[528,256]{1,0:T(8,128)(2,1)S(1)} %get-tuple-element.73.refs_0_, ...), custom_call_target="tpu_custom_call" | custom-call | flops 1107296256 | bytes 4325376 | tf_op jit(solution)/shard_map/pallas_call | solution.py:321
  49.9 0.6 collective-permute-done.5.refs_2_.refs_6_
  50.5 3.7 %shard_map.114.refs_8_ = bf16[256,1024]{1,0:T(8,128)(2,1)S(1)} custom-call(s32[2]{0:T(128)S(1)} %pad_add_fusion.place_ref, bf16[1056,1024]{1,0:T(8,128)(2,1)S(1)} %bitcast.18, bf16[1056,1024]{1,0:T(8,128)(2,1)S(1)} %collective-permute-done.other_w, bf16[528,256]{1,0:T(8,128)(2,1)S(1)} %collective-permute-done.2.refs_0_.refs_4_, ...), custom_call_target="tpu_custom_call" | custom-call | flops 1107296256 | bytes 4325376 | tf_op jit(solution)/shard_map/pallas_call | solution.py:321
  54.2 0.6 collective-permute-start.10
  54.7 0.7 collective-permute-start.14
  55.4 4.1 %collective-permute-done.11 = bf16[528,256]{1,0:T(8,128)(2,1)S(1)} collective-permute-done((bf16[528,256]{1,0:T(8,128)(2,1)S(1)}, bf16[528,256]{1,0:T(8,128)(2,1)S(1)}, u32[]{:S(2)}, u32[]{:S(2)}) %collective-permute-start.11) | collective-permute-done | bytes 270368 | tf_op jit(solution)/shard_map/ppermute | solution.py:244
  59.5 0.9 collective-permute-start.15
  60.5 1.4 %collective-permute-start.16 = (bf16[528,256]{1,0:T(8,128)(2,1)S(1)}, bf16[528,256]{1,0:T(8,128)(2,1)S(1)}, u32[]{:S(2)}, u32[]{:S(2)}) collective-permute-start(bf16[528,256]{1,0:T(8,128)(2,1)S(1)} %get-tuple-element.55), channel_id=1, source_target_pairs={{0,3},{1,2},{2,1},{3,0},{4,7},{5,6},{6,5},{7,4},{8,11},{9,10},{10,... | collective-permute-start | bytes 811016 | tf_op jit(solution)/shard_map/ppermute | solution.py:244
  61.9 0.2 add_convert_fusion.1
  62.0 0.0 copy-start.6
  62.1 0.7 collective-permute-start.17
  62.7 5.0 %shard_map.116 = (f32[1056,1024]{1,0:T(8,128)S(1)}, bf16[1056,1024]{1,0:T(8,128)(2,1)S(1)}) custom-call(s32[2]{0:T(128)S(1)} %pad_add_fusion.place_ref, bf16[256,1024]{1,0:T(8,128)(2,1)} %get-tuple-element.46.context_own, bf16[256,1024]{1,0:T(8,128)(2,1)} %collective-permute-done.3.context_other, bf16[528,256]{1,0:T(8,128)(2,1)S(1)} %get-tuple-element.73.refs_0_, ...), custom_call_target="tpu_custom_call" | custom-call | flops 2214592512 | bytes 6488064 | tf_op jit(solution)/shard_map/pallas_call | solution.py:347
  67.8 1.2 %collective-permute-done.14 = bf16[528,256]{1,0:T(8,128)(2,1)S(1)} collective-permute-done((bf16[528,256]{1,0:T(8,128)(2,1)S(1)}, bf16[528,256]{1,0:T(8,128)(2,1)S(1)}, u32[]{:S(2)}, u32[]{:S(2)}) %collective-permute-start.14) | collective-permute-done | bytes 270368 | tf_op jit(solution)/shard_map/ppermute | solution.py:244
  69.0 3.0 %collective-permute-done.16 = bf16[528,256]{1,0:T(8,128)(2,1)S(1)} collective-permute-done((bf16[528,256]{1,0:T(8,128)(2,1)S(1)}, bf16[528,256]{1,0:T(8,128)(2,1)S(1)}, u32[]{:S(2)}, u32[]{:S(2)}) %collective-permute-start.16) | collective-permute-done | bytes 270368 | tf_op jit(solution)/shard_map/ppermute | solution.py:244
  72.0 0.2 add_convert_fusion
  72.2 0.1 collective-permute-start.23
  72.3 2.4 %shard_map.117 = (bf16[4,64,1024]{2,1,0:T(8,128)(2,1)}, bf16[4,2,64,128]{3,2,1,0:T(8,128)(2,1)S(1)}) custom-call(f32[256,1024]{1,0:T(8,128)S(1)} %shard_map.113.refs_4_.own_ref, bf16[256,1024]{1,0:T(8,128)(2,1)S(1)} %collective-permute-done.10.got_ref, bf16[4,64,1024]{2,1,0:T(8,128)(2,1)S(1)} %bitcast.20, ...), custom_call_target="tpu_custom_call" | custom-call | flops 234881024 | bytes 4194304 | tf_op jit(solution)/shard_map/pallas_call | solution.py:366
  74.7 2.8 %collective-permute-start.22 = (bf16[512,128]{1,0:T(8,128)(2,1)S(1)}, bf16[512,128]{1,0:T(8,128)(2,1)S(1)}, u32[]{:S(2)}, u32[]{:S(2)}) collective-permute-start(bf16[512,128]{1,0:T(8,128)(2,1)S(1)} %bitcast.23), channel_id=1, source_target_pairs={{0,4},{1,5},{2,6},{3,7},{4,0},{5,1},{6,2},{7,3},{8,12},{9,13},{10,... | collective-permute-start | bytes 393224 | tf_op jit(solution)/shard_map/ppermute | solution.py:244
  77.5 2.6 %collective-permute-start.21 = (bf16[512,128]{1,0:T(8,128)(2,1)S(1)}, bf16[512,128]{1,0:T(8,128)(2,1)S(1)}, u32[]{:S(2)}, u32[]{:S(2)}) collective-permute-start(bf16[512,128]{1,0:T(8,128)(2,1)S(1)} %bitcast.24), channel_id=1, source_target_pairs={{0,3},{1,2},{2,1},{3,0},{4,7},{5,6},{6,5},{7,4},{8,11},{9,10},{10,... | collective-permute-start | bytes 393224 | tf_op jit(solution)/shard_map/ppermute | solution.py:244
  80.1 0.8 collective-permute-start.19
  81.0 0.2 collective-permute-start.18
  81.2 2.8 %add_bitcast_fusion = f32[1024,1056]{0,1:T(8,128)} fusion(f32[1056,1024]{1,0:T(8,128)S(1)} %get-tuple-element.66, bf16[1056,1024]{1,0:T(8,128)(2,1)S(1)} %collective-permute-done.23), kind=kLoop, calls=%fused_computation | loop fusion | flops 2162688 | bytes 10813440 | tf_op jit(solution)/shard_map/transpose | solution.py:376
  84.0 0.8 collective-permute-done.22.refs_4_
  84.8 1.8 %collective-permute-start.26 = (bf16[512,128]{1,0:T(8,128)(2,1)S(1)}, bf16[512,128]{1,0:T(8,128)(2,1)S(1)}, u32[]{:S(2)}, u32[]{:S(2)}) collective-permute-start(bf16[512,128]{1,0:T(8,128)(2,1)S(1)} %collective-permute-done.22.refs_4_), channel_id=1, source_target_pairs={{0,3},{1,2},{2,1},{3,0},{4,7},{5,6},{6,5},{7,4},{8,11},{9,10},{10,... | collective-permute-start | bytes 393224 | tf_op jit(solution)/shard_map/ppermute | solution.py:244
  86.6 3.8 %collective-permute-done.21.refs_3_ = bf16[512,128]{1,0:T(8,128)(2,1)S(1)} collective-permute-done((bf16[512,128]{1,0:T(8,128)(2,1)S(1)}, bf16[512,128]{1,0:T(8,128)(2,1)S(1)}, u32[]{:S(2)}, u32[]{:S(2)}) %collective-permute-start.21) | collective-permute-done | bytes 131104 | tf_op jit(solution)/shard_map/ppermute | solution.py:244
  90.4 1.4 %collective-permute-done.20.refs_2_ = bf16[512,128]{1,0:T(8,128)(2,1)S(1)} collective-permute-done((bf16[512,128]{1,0:T(8,128)(2,1)S(1)}, bf16[512,128]{1,0:T(8,128)(2,1)S(1)}, u32[]{:S(2)}, u32[]{:S(2)}) %collective-permute-start.20) | collective-permute-done | bytes 131104 | tf_op jit(solution)/shard_map/ppermute | solution.py:244
  91.8 1.9 %collective-permute-start.24 = (bf16[512,128]{1,0:T(8,128)(2,1)S(1)}, bf16[512,128]{1,0:T(8,128)(2,1)S(1)}, u32[]{:S(2)}, u32[]{:S(2)}) collective-permute-start(bf16[512,128]{1,0:T(8,128)(2,1)S(1)} %collective-permute-done.22.refs_4_), channel_id=1, source_target_pairs={{0,1},{1,0},{2,3},{3,2},{4,5},{5,4},{6,7},{7,6},{8,9},{9,8},{10,11... | collective-permute-start | bytes 393224 | tf_op jit(solution)/shard_map/ppermute | solution.py:244
  93.8 2.4 %collective-permute-done.18.got_ref = bf16[528,256]{1,0:T(8,128)(2,1)S(1)} collective-permute-done((bf16[528,256]{1,0:T(8,128)(2,1)S(1)}, bf16[528,256]{1,0:T(8,128)(2,1)S(1)}, u32[]{:S(2)}, u32[]{:S(2)}) %collective-permute-start.18) | collective-permute-done | bytes 270368 | tf_op jit(solution)/shard_map/ppermute | solution.py:244
  96.2 1.0 shard_map.118
  97.1 0.4 collective-permute-done.26.refs_7_
  97.6 1.3 %collective-permute-done.25.refs_6_ = bf16[512,128]{1,0:T(8,128)(2,1)S(1)} collective-permute-done((bf16[512,128]{1,0:T(8,128)(2,1)S(1)}, bf16[512,128]{1,0:T(8,128)(2,1)S(1)}, u32[]{:S(2)}, u32[]{:S(2)}) %collective-permute-start.25) | collective-permute-done | bytes 131104 | tf_op jit(solution)/shard_map/ppermute | solution.py:244
  98.8 1.6 %shard_map.119 = bf16[512,1024]{1,0:T(8,128)(2,1)} custom-call(s32[2]{0:T(128)S(1)} %pad_add_fusion.place_ref, bf16[512,128]{1,0:T(8,128)(2,1)S(1)} %bitcast.27, bf16[512,128]{1,0:T(8,128)(2,1)S(1)} %collective-permute-done.19.refs_1_, bf16[512,128]{1,0:T(8,128)(2,1)S(1)} %collective-permute-done.20.refs_2_, ...), custom_call_target="tpu_custom_call" | custom-call | bytes 1048576 | tf_op jit(solution)/shard_map/pallas_call | solution.py:395
  (30 shorter events, 0.1 us)
Async XLA Ops:
  0.6 6.1 %copy-start = (bf16[1,4,2,64,1024]{4,3,2,1,0:T(8,128)(2,1)S(1)}, bf16[1,4,2,64,1024]{4,3,2,1,0:T(8,128)(2,1)}, u32[]{:S(2)}) copy-start(bf16[1,4,2,64,1024]{4,3,2,1,0:T(8,128)(2,1)} %param.9) | copy-start | bytes 3145732
  0.6 33.8 %collective-permute-start = (bf16[1056,1024]{1,0:T(8,128)(2,1)}, bf16[1056,1024]{1,0:T(8,128)(2,1)S(1)}, u32[]{:S(2)}, u32[]{:S(2)}) collective-permute-start(bf16[1056,1024]{1,0:T(8,128)(2,1)} %bitcast.15), channel_id=1, source_target_pairs={{0,8},{8,0},{16,24},{24,16},{1,9},{9,1},{17,25},{25,17},{2,10},{10... | collective-permute-start | bytes 6488072 | tf_op jit(solution)/shard_map/ppermute | solution.py:250
  1.2 1.0 copy-start.8
  3.0 16.8 %collective-permute-start.1 = (bf16[528,256]{1,0:T(8,128)(2,1)}, bf16[528,256]{1,0:T(8,128)(2,1)}, u32[]{:S(2)}, u32[]{:S(2)}) collective-permute-start(bf16[528,256]{1,0:T(8,128)(2,1)} %shard_map.111), channel_id=1, source_target_pairs={{0,4},{1,5},{2,6},{3,7},{4,0},{5,1},{6,2},{7,3},{8,12},{9,13},{10,... | collective-permute-start | bytes 811016 | tf_op jit(solution)/shard_map/ppermute | solution.py:244
  6.7 1.0 %copy-start.3 = (bf16[1,4,64,1024]{3,2,1,0:T(8,128)(2,1)S(1)}, bf16[1,4,64,1024]{3,2,1,0:T(8,128)(2,1)}, u32[]{:S(2)}) copy-start(bf16[1,4,64,1024]{3,2,1,0:T(8,128)(2,1)} %param.8) | copy-start | bytes 1572868
  7.8 0.7 copy-start.9
  10.4 1.0 copy-start.5
  11.4 15.1 %collective-permute-start.3 = (bf16[256,1024]{1,0:T(8,128)(2,1)}, bf16[256,1024]{1,0:T(8,128)(2,1)}, u32[]{:S(2)}, u32[]{:S(2)}) collective-permute-start(bf16[256,1024]{1,0:T(8,128)(2,1)} %get-tuple-element.46.context_own), channel_id=1, source_target_pairs={{0,16},{8,24},{16,0},{24,8},{1,17},{9,25},{17,1},{25,9},{2,18},{10... | collective-permute-start | bytes 1572872 | tf_op jit(solution)/shard_map/ppermute | solution.py:247
  21.0 10.3 %collective-permute-start.2 = (bf16[528,256]{1,0:T(8,128)(2,1)S(1)}, bf16[528,256]{1,0:T(8,128)(2,1)S(1)}, u32[]{:S(2)}, u32[]{:S(2)}) collective-permute-start(bf16[528,256]{1,0:T(8,128)(2,1)S(1)} %get-tuple-element.74), channel_id=1, source_target_pairs={{0,16},{8,24},{16,0},{24,8},{1,17},{9,25},{17,1},{25,9},{2,18},{10... | collective-permute-start | bytes 811016 | tf_op jit(solution)/shard_map/ppermute | solution.py:247
  22.7 11.3 %collective-permute-start.9 = (bf16[528,256]{1,0:T(8,128)(2,1)S(1)}, bf16[528,256]{1,0:T(8,128)(2,1)S(1)}, u32[]{:S(2)}, u32[]{:S(2)}) collective-permute-start(bf16[528,256]{1,0:T(8,128)(2,1)S(1)} %get-tuple-element.73.refs_0_), channel_id=1, source_target_pairs={{0,3},{1,2},{2,1},{3,0},{4,7},{5,6},{6,5},{7,4},{8,11},{9,10},{10,... | collective-permute-start | bytes 811016 | tf_op jit(solution)/shard_map/ppermute | solution.py:244
  24.3 17.4 %collective-permute-start.8 = (bf16[528,256]{1,0:T(8,128)(2,1)S(1)}, bf16[528,256]{1,0:T(8,128)(2,1)S(1)}, u32[]{:S(2)}, u32[]{:S(2)}) collective-permute-start(bf16[528,256]{1,0:T(8,128)(2,1)S(1)} %get-tuple-element.73.refs_0_), channel_id=1, source_target_pairs={{0,2},{1,3},{2,0},{3,1},{4,6},{5,7},{6,4},{7,5},{8,10},{9,11},{10,... | collective-permute-start | bytes 811016 | tf_op jit(solution)/shard_map/ppermute | solution.py:244
  26.4 16.6 %collective-permute-start.7 = (bf16[528,256]{1,0:T(8,128)(2,1)S(1)}, bf16[528,256]{1,0:T(8,128)(2,1)S(1)}, u32[]{:S(2)}, u32[]{:S(2)}) collective-permute-start(bf16[528,256]{1,0:T(8,128)(2,1)S(1)} %get-tuple-element.73.refs_0_), channel_id=1, source_target_pairs={{0,1},{1,0},{2,3},{3,2},{4,5},{5,4},{6,7},{7,6},{8,9},{9,8},{10,11... | collective-permute-start | bytes 811016 | tf_op jit(solution)/shard_map/ppermute | solution.py:244
  31.4 13.3 %collective-permute-start.6 = (bf16[528,256]{1,0:T(8,128)(2,1)S(1)}, bf16[528,256]{1,0:T(8,128)(2,1)S(1)}, u32[]{:S(2)}, u32[]{:S(2)}) collective-permute-start(bf16[528,256]{1,0:T(8,128)(2,1)S(1)} %collective-permute-done.2.refs_0_.refs_4_), channel_id=1, source_target_pairs={{0,3},{1,2},{2,1},{3,0},{4,7},{5,6},{6,5},{7,4},{8,11},{9,10},{10,... | collective-permute-start | bytes 811016 | tf_op jit(solution)/shard_map/ppermute | solution.py:244
  34.0 16.5 %collective-permute-start.5 = (bf16[528,256]{1,0:T(8,128)(2,1)S(1)}, bf16[528,256]{1,0:T(8,128)(2,1)S(1)}, u32[]{:S(2)}, u32[]{:S(2)}) collective-permute-start(bf16[528,256]{1,0:T(8,128)(2,1)S(1)} %collective-permute-done.2.refs_0_.refs_4_), channel_id=1, source_target_pairs={{0,2},{1,3},{2,0},{3,1},{4,6},{5,7},{6,4},{7,5},{8,10},{9,11},{10,... | collective-permute-start | bytes 811016 | tf_op jit(solution)/shard_map/ppermute | solution.py:244
  34.4 16.1 %collective-permute-start.4 = (bf16[528,256]{1,0:T(8,128)(2,1)S(1)}, bf16[528,256]{1,0:T(8,128)(2,1)S(1)}, u32[]{:S(2)}, u32[]{:S(2)}) collective-permute-start(bf16[528,256]{1,0:T(8,128)(2,1)S(1)} %collective-permute-done.2.refs_0_.refs_4_), channel_id=1, source_target_pairs={{0,1},{1,0},{2,3},{3,2},{4,5},{5,4},{6,7},{7,6},{8,9},{9,8},{10,11... | collective-permute-start | bytes 811016 | tf_op jit(solution)/shard_map/ppermute | solution.py:244
  35.2 1.6 %copy-start.1 = (bf16[1024,1056]{0,1:T(8,128)(2,1)S(1)}, bf16[1024,1056]{0,1:T(8,128)(2,1)}, u32[]{:S(2)}) copy-start(bf16[1024,1056]{0,1:T(8,128)(2,1)} %param.13) | copy-start | bytes 6488068
  36.8 9.5 %copy-start.2 = (bf16[1024,1056]{0,1:T(8,128)(2,1)S(1)}, bf16[1024,1056]{0,1:T(8,128)(2,1)}, u32[]{:S(2)}) copy-start(bf16[1024,1056]{0,1:T(8,128)(2,1)} %param.13) | copy-start | bytes 6488068
  41.7 17.8 %collective-permute-start.11 = (bf16[528,256]{1,0:T(8,128)(2,1)S(1)}, bf16[528,256]{1,0:T(8,128)(2,1)S(1)}, u32[]{:S(2)}, u32[]{:S(2)}) collective-permute-start(bf16[528,256]{1,0:T(8,128)(2,1)S(1)} %get-tuple-element.43), channel_id=1, source_target_pairs={{0,1},{1,0},{2,3},{3,2},{4,5},{5,4},{6,7},{7,6},{8,9},{9,8},{10,11... | collective-permute-start | bytes 811016 | tf_op jit(solution)/shard_map/ppermute | solution.py:244
  43.0 17.4 %collective-permute-start.12 = (bf16[528,256]{1,0:T(8,128)(2,1)S(1)}, bf16[528,256]{1,0:T(8,128)(2,1)S(1)}, u32[]{:S(2)}, u32[]{:S(2)}) collective-permute-start(bf16[528,256]{1,0:T(8,128)(2,1)S(1)} %get-tuple-element.44), channel_id=1, source_target_pairs={{0,2},{1,3},{2,0},{3,1},{4,6},{5,7},{6,4},{7,5},{8,10},{9,11},{10,... | collective-permute-start | bytes 811016 | tf_op jit(solution)/shard_map/ppermute | solution.py:244
  44.7 17.2 %collective-permute-start.13 = (bf16[528,256]{1,0:T(8,128)(2,1)S(1)}, bf16[528,256]{1,0:T(8,128)(2,1)S(1)}, u32[]{:S(2)}, u32[]{:S(2)}) collective-permute-start(bf16[528,256]{1,0:T(8,128)(2,1)S(1)} %get-tuple-element.45), channel_id=1, source_target_pairs={{0,3},{1,2},{2,1},{3,0},{4,7},{5,6},{6,5},{7,4},{8,11},{9,10},{10,... | collective-permute-start | bytes 811016 | tf_op jit(solution)/shard_map/ppermute | solution.py:244
  54.2 18.0 %collective-permute-start.10 = (bf16[256,1024]{1,0:T(8,128)(2,1)S(1)}, bf16[256,1024]{1,0:T(8,128)(2,1)S(1)}, u32[]{:S(2)}, u32[]{:S(2)}) collective-permute-start(bf16[256,1024]{1,0:T(8,128)(2,1)S(1)} %shard_map.114.refs_8_), channel_id=1, source_target_pairs={{0,16},{8,24},{16,0},{24,8},{1,17},{9,25},{17,1},{25,9},{2,18},{10... | collective-permute-start | bytes 1572872 | tf_op jit(solution)/shard_map/ppermute | solution.py:247
  54.7 14.2 %collective-permute-start.14 = (bf16[528,256]{1,0:T(8,128)(2,1)S(1)}, bf16[528,256]{1,0:T(8,128)(2,1)S(1)}, u32[]{:S(2)}, u32[]{:S(2)}) collective-permute-start(bf16[528,256]{1,0:T(8,128)(2,1)S(1)} %get-tuple-element.53), channel_id=1, source_target_pairs={{0,1},{1,0},{2,3},{3,2},{4,5},{5,4},{6,7},{7,6},{8,9},{9,8},{10,11... | collective-permute-start | bytes 811016 | tf_op jit(solution)/shard_map/ppermute | solution.py:244
  59.5 9.4 %collective-permute-start.15 = (bf16[528,256]{1,0:T(8,128)(2,1)S(1)}, bf16[528,256]{1,0:T(8,128)(2,1)S(1)}, u32[]{:S(2)}, u32[]{:S(2)}) collective-permute-start(bf16[528,256]{1,0:T(8,128)(2,1)S(1)} %get-tuple-element.54), channel_id=1, source_target_pairs={{0,2},{1,3},{2,0},{3,1},{4,6},{5,7},{6,4},{7,5},{8,10},{9,11},{10,... | collective-permute-start | bytes 811016 | tf_op jit(solution)/shard_map/ppermute | solution.py:244
  60.5 11.5 %collective-permute-start.16 = (bf16[528,256]{1,0:T(8,128)(2,1)S(1)}, bf16[528,256]{1,0:T(8,128)(2,1)S(1)}, u32[]{:S(2)}, u32[]{:S(2)}) collective-permute-start(bf16[528,256]{1,0:T(8,128)(2,1)S(1)} %get-tuple-element.55), channel_id=1, source_target_pairs={{0,3},{1,2},{2,1},{3,0},{4,7},{5,6},{6,5},{7,4},{8,11},{9,10},{10,... | collective-permute-start | bytes 811016 | tf_op jit(solution)/shard_map/ppermute | solution.py:244
  62.0 10.2 %copy-start.4 = (bf16[1,4,64,1024]{3,2,1,0:T(8,128)(2,1)S(1)}, bf16[1,4,64,1024]{3,2,1,0:T(8,128)(2,1)}, u32[]{:S(2)}) copy-start(bf16[1,4,64,1024]{3,2,1,0:T(8,128)(2,1)} %param.8) | copy-start | bytes 1572868
  62.0 10.2 %copy-start.6 = (f32[4,512,64]{2,1,0:T(8,128)S(1)}, f32[4,512,64]{2,1,0:T(8,128)}, u32[]{:S(2)}) copy-start(f32[4,512,64]{2,1,0:T(8,128)} %copy-done.5) | copy-start | bytes 1572868
  62.1 10.1 %collective-permute-start.17 = (bf16[528,256]{1,0:T(8,128)(2,1)S(1)}, bf16[528,256]{1,0:T(8,128)(2,1)S(1)}, u32[]{:S(2)}, u32[]{:S(2)}) collective-permute-start(bf16[528,256]{1,0:T(8,128)(2,1)S(1)} %add_convert_fusion.1), channel_id=1, source_target_pairs={{0,16},{8,24},{16,0},{24,8},{1,17},{9,25},{17,1},{25,9},{2,18},{10... | collective-permute-start | bytes 811016 | tf_op jit(solution)/shard_map/ppermute | solution.py:247
  72.2 8.8 %collective-permute-start.23 = (bf16[1056,1024]{1,0:T(8,128)(2,1)S(1)}, bf16[1056,1024]{1,0:T(8,128)(2,1)S(1)}, u32[]{:S(2)}, u32[]{:S(2)}) collective-permute-start(bf16[1056,1024]{1,0:T(8,128)(2,1)S(1)} %get-tuple-element.67), channel_id=1, source_target_pairs={{0,8},{8,0},{16,24},{24,16},{1,9},{9,1},{17,25},{25,17},{2,10},{10... | collective-permute-start | bytes 6488072 | tf_op jit(solution)/shard_map/ppermute | solution.py:250
  74.7 10.1 %collective-permute-start.22 = (bf16[512,128]{1,0:T(8,128)(2,1)S(1)}, bf16[512,128]{1,0:T(8,128)(2,1)S(1)}, u32[]{:S(2)}, u32[]{:S(2)}) collective-permute-start(bf16[512,128]{1,0:T(8,128)(2,1)S(1)} %bitcast.23), channel_id=1, source_target_pairs={{0,4},{1,5},{2,6},{3,7},{4,0},{5,1},{6,2},{7,3},{8,12},{9,13},{10,... | collective-permute-start | bytes 393224 | tf_op jit(solution)/shard_map/ppermute | solution.py:244
  77.5 12.9 %collective-permute-start.21 = (bf16[512,128]{1,0:T(8,128)(2,1)S(1)}, bf16[512,128]{1,0:T(8,128)(2,1)S(1)}, u32[]{:S(2)}, u32[]{:S(2)}) collective-permute-start(bf16[512,128]{1,0:T(8,128)(2,1)S(1)} %bitcast.24), channel_id=1, source_target_pairs={{0,3},{1,2},{2,1},{3,0},{4,7},{5,6},{6,5},{7,4},{8,11},{9,10},{10,... | collective-permute-start | bytes 393224 | tf_op jit(solution)/shard_map/ppermute | solution.py:244
  80.1 11.7 %collective-permute-start.20 = (bf16[512,128]{1,0:T(8,128)(2,1)S(1)}, bf16[512,128]{1,0:T(8,128)(2,1)S(1)}, u32[]{:S(2)}, u32[]{:S(2)}) collective-permute-start(bf16[512,128]{1,0:T(8,128)(2,1)S(1)} %bitcast.25), channel_id=1, source_target_pairs={{0,2},{1,3},{2,0},{3,1},{4,6},{5,7},{6,4},{7,5},{8,10},{9,11},{10,... | collective-permute-start | bytes 393224 | tf_op jit(solution)/shard_map/ppermute | solution.py:244
  80.1 13.6 %collective-permute-start.19 = (bf16[512,128]{1,0:T(8,128)(2,1)S(1)}, bf16[512,128]{1,0:T(8,128)(2,1)S(1)}, u32[]{:S(2)}, u32[]{:S(2)}) collective-permute-start(bf16[512,128]{1,0:T(8,128)(2,1)S(1)} %bitcast.26), channel_id=1, source_target_pairs={{0,1},{1,0},{2,3},{3,2},{4,5},{5,4},{6,7},{7,6},{8,9},{9,8},{10,11... | collective-permute-start | bytes 393224 | tf_op jit(solution)/shard_map/ppermute | solution.py:244
  81.0 15.1 %collective-permute-start.18 = (bf16[528,256]{1,0:T(8,128)(2,1)S(1)}, bf16[528,256]{1,0:T(8,128)(2,1)S(1)}, u32[]{:S(2)}, u32[]{:S(2)}) collective-permute-start(bf16[528,256]{1,0:T(8,128)(2,1)S(1)} %get-tuple-element.75), channel_id=1, source_target_pairs={{0,4},{1,5},{2,6},{3,7},{4,0},{5,1},{6,2},{7,3},{8,12},{9,13},{10,... | collective-permute-start | bytes 811016 | tf_op jit(solution)/shard_map/ppermute | solution.py:244
  81.2 14.9 %copy-start.7 = (bf16[1,4,64,528]{3,2,1,0:T(8,128)(2,1)S(1)}, bf16[1,4,64,528]{3,2,1,0:T(8,128)(2,1)}, u32[]{:S(2)}) copy-start(bf16[1,4,64,528]{3,2,1,0:T(8,128)(2,1)} %param.11) | copy-start | bytes 811012
  84.8 12.8 %collective-permute-start.26 = (bf16[512,128]{1,0:T(8,128)(2,1)S(1)}, bf16[512,128]{1,0:T(8,128)(2,1)S(1)}, u32[]{:S(2)}, u32[]{:S(2)}) collective-permute-start(bf16[512,128]{1,0:T(8,128)(2,1)S(1)} %collective-permute-done.22.refs_4_), channel_id=1, source_target_pairs={{0,3},{1,2},{2,1},{3,0},{4,7},{5,6},{6,5},{7,4},{8,11},{9,10},{10,... | collective-permute-start | bytes 393224 | tf_op jit(solution)/shard_map/ppermute | solution.py:244
  90.4 8.4 %collective-permute-start.25 = (bf16[512,128]{1,0:T(8,128)(2,1)S(1)}, bf16[512,128]{1,0:T(8,128)(2,1)S(1)}, u32[]{:S(2)}, u32[]{:S(2)}) collective-permute-start(bf16[512,128]{1,0:T(8,128)(2,1)S(1)} %collective-permute-done.22.refs_4_), channel_id=1, source_target_pairs={{0,2},{1,3},{2,0},{3,1},{4,6},{5,7},{6,4},{7,5},{8,10},{9,11},{10,... | collective-permute-start | bytes 393224 | tf_op jit(solution)/shard_map/ppermute | solution.py:244
  91.8 7.0 %collective-permute-start.24 = (bf16[512,128]{1,0:T(8,128)(2,1)S(1)}, bf16[512,128]{1,0:T(8,128)(2,1)S(1)}, u32[]{:S(2)}, u32[]{:S(2)}) collective-permute-start(bf16[512,128]{1,0:T(8,128)(2,1)S(1)} %collective-permute-done.22.refs_4_), channel_id=1, source_target_pairs={{0,1},{1,0},{2,3},{3,2},{4,5},{5,4},{6,7},{7,6},{8,9},{9,8},{10,11... | collective-permute-start | bytes 393224 | tf_op jit(solution)/shard_map/ppermute | solution.py:244

commit v4 on v3

--- a/solution.py
+++ b/solution.py
@@ -283,8 +283,10 @@
     across, context = lax.optimization_barrier((across, context))
     weight = jnp.repeat(slot_weights(live_mask, micro_counts, slots), length)
     scaled = lambda array: (array.astype(F32) * weight[None, :]).astype(BF)
+    sent = scaled(jnp.where(home, across, turned))
+    cot_other = swap_x(sent)
+    across, _ = lax.optimization_barrier((across, sent))
     cot_own = scaled(jnp.where(home, turned, across))
-    cot_other = swap_x(scaled(jnp.where(home, across, turned)))
     shards_own = [swap(cot_own, mask) if mask else cot_own for mask in range(inner)]
 
 
@@ -314,7 +316,7 @@
     near, far = list(partial[::2]), partial[1::2]
     far = [swap(far[mask], mask) if mask else far[mask] for mask in range(inner)]
 
-    tile = min(256, width)
+    tile = min(512, width)
     column = lambda rows: pl.BlockSpec((rows, tile), lambda i: (0, i))
 
     def context_grad(shards, dtype):

time: 101 us -> 101 us (level)
  starting transfers between devices: 34.6 us -> 38.4 us
  Pallas kernels: 24.9 us -> 22.5 us
  waiting for transfers between devices: 26.9 us -> 25.4 us
    ppermute x4, starting transfers between devices: 4.36 us -> 7.29 us  [swap_x(): return lax.ppermute(array, 'dp', [(d, d ^ 2) for d in range(4)])]
    ppermute x21, waiting for transfers between devices: 22.7 us -> 19.9 us  [swap(): lax.ppermute(array, 'tensor', [(t, t ^ mask) for t in range(tensor_size)])]
    ppermute x4, waiting for transfers between devices: 4.18 us -> 5.46 us  [swap_x(): return lax.ppermute(array, 'dp', [(d, d ^ 2) for d in range(4)])]
    pallas_call x2, Pallas kernels: 7.29 us -> 6.08 us  [context_grad(): call(functools.partial(context_grad_kernel, inner), shape((tokens, width)...]
    unnamed x20 -> x24, local copies, waits for them, and re-layouts: 5.3 us -> 5.36 us
  transfers between devices with their start and end apart: 27 -> 27, of which waited for: 14 -> 12; matrix products, arithmetic and copies ran while one was open for 6% -> 7% of each run, Pallas kernels for 23% -> 21%
where the time goes in v4:
time: 101 us
  starting transfers between devices  38.4 us (38%)
  waiting for transfers between devices  25.4 us (25%)
  Pallas kernels  22.5 us (22%)
  other arithmetic  6.52 us (6%)
  local copies, waits for them, and re-layouts  5.55 us (5%)
  between operations  2.18 us (2%)
    ppermute x21, starting transfers between devices, swap(): lax.ppermute(array, 'tensor', [(t, t ^ mask) for t in range(tensor_size)])  30.6 us
    ppermute x21, waiting for transfers between devices, swap(): lax.ppermute(array, 'tensor', [(t, t ^ mask) for t in range(tensor_size)])  19.9 us
    ppermute x4, starting transfers between devices, swap_x(): return lax.ppermute(array, 'dp', [(d, d ^ 2) for d in range(4)])  7.29 us
    pallas_call x2, Pallas kernels, context_grad(): call(functools.partial(context_grad_kernel, inner), shape((tokens, width)...  6.08 us
    ppermute x4, waiting for transfers between devices, swap_x(): return lax.ppermute(array, 'dp', [(d, d ^ 2) for d in range(4)])  5.46 us
    unnamed x24, local copies, waits for them, and re-layouts  5.36 us
    pallas_call x1, Pallas kernels, by_activations(): call(functools.partial(project_kernel, inner), [shape((features, tokens),...  4.88 us
    pallas_call x1, Pallas kernels, by_activations(): call(functools.partial(weight_grad_kernel, inner), (shape((own_rows, widt...  4.47 us
  transfers between devices with their start and end apart: 27, of which 12 were waited for; matrix products, arithmetic and copies ran while one was open for 7% of the time, Pallas kernels for 21%

profile of v4, /device:TPU:0, one launch (start us, length us, event | category | flops | bytes accessed | tf_op | source)
XLA Modules:
  0.0 100.5 jit_solution(7256166286785806909)
XLA Ops:
  0.6 0.0 copy-start
  0.6 0.5 collective-permute-start
  1.2 1.0 copy-done.10
  2.1 0.2 shard_map.111
  2.3 3.7 %collective-permute-start.1 = (bf16[528,256]{1,0:T(8,128)(2,1)S(1)}, bf16[528,256]{1,0:T(8,128)(2,1)}, u32[]{:S(2)}, u32[]{:S(2)}) collective-permute-start(bf16[528,256]{1,0:T(8,128)(2,1)S(1)} %shard_map.111), channel_id=1, source_target_pairs={{0,4},{1,5},{2,6},{3,7},{4,0},{5,1},{6,2},{7,3},{8,12},{9,13},{10,... | collective-permute-start | bytes 811016 | tf_op jit(solution)/shard_map/ppermute | solution.py:244
  6.1 0.0 copy-start.3
  6.1 1.1 %copy-done.3 = bf16[1,4,64,1024]{3,2,1,0:T(8,128)(2,1)S(1)} copy-done((bf16[1,4,64,1024]{3,2,1,0:T(8,128)(2,1)S(1)}, bf16[1,4,64,1024]{3,2,1,0:T(8,128)(2,1)}, u32[]{:S(2)}) %copy-start.3) | copy-done | bytes 524312
  7.2 0.7 copy-done.11
  7.9 1.9 %shard_map.112 = (bf16[256,1024]{1,0:T(8,128)(2,1)}, f32[4,512,64]{2,1,0:T(8,128)S(1)}) custom-call(bf16[4,64,1024]{2,1,0:T(8,128)(2,1)S(1)} %bitcast.19, bf16[4,2,64,128]{3,2,1,0:T(8,128)(2,1)S(1)} %dynamic-slice_bitcast_fusion.key_value_ref, s32[4,64]{1,0:T(4,128)S(1)} %bitcast.28), custom_call_target="tpu_custom_call" | custom-call | flops 67108864 | bytes 2097152 | tf_op jit(solution)/shard_map/pallas_call | solution.py:272
  9.8 1.0 copy-done.7
  10.8 1.5 %collective-permute-start.3 = (bf16[256,1024]{1,0:T(8,128)(2,1)}, bf16[256,1024]{1,0:T(8,128)(2,1)}, u32[]{:S(2)}, u32[]{:S(2)}) collective-permute-start(bf16[256,1024]{1,0:T(8,128)(2,1)} %get-tuple-element.48.context_own), channel_id=1, source_target_pairs={{0,16},{8,24},{16,0},{24,8},{1,17},{9,25},{17,1},{25,9},{2,18},{10... | collective-permute-start | bytes 1572872 | tf_op jit(solution)/shard_map/ppermute | solution.py:247
  12.3 1.4 %fusion = (s32[]{:T(128)}, s32[]{:T(128)}, s32[]{:T(128)}) fusion(s32[4]{0:T(128)} %param.15, s32[]{:T(128)} %axis_index.27, s32[4]{0:T(128)} %param.14), kind=kLoop, calls=%fused_computation.11 | loop fusion | flops 25 | bytes 48 | tf_op jit(solution)/shard_map/reduce_sum | solution.py:217
  15.0 0.7 and_select_fusion
  15.7 0.1 broadcast_in_dim.15
  15.8 0.1 mul.24
  15.8 3.2 %collective-permute-done.1 = bf16[528,256]{1,0:T(8,128)(2,1)} collective-permute-done((bf16[528,256]{1,0:T(8,128)(2,1)S(1)}, bf16[528,256]{1,0:T(8,128)(2,1)}, u32[]{:S(2)}, u32[]{:S(2)}) %collective-permute-start.1) | collective-permute-done | bytes 270368 | tf_op jit(solution)/shard_map/ppermute | solution.py:244
  19.0 1.0 %multiply_convert_fusion.1 = bf16[528,256]{1,0:T(8,128)(2,1)S(1)} fusion(f32[256]{0:T(256)S(1)} %mul.24, bf16[528,256]{1,0:T(8,128)(2,1)} %collective-permute-done.1, bf16[528,256]{1,0:T(8,128)(2,1)S(1)} %shard_map.111, pred[]{:T(512)S(6)} %eq.9), kind=kLoop, calls=%fused_computation.4 | loop fusion | flops 540672 | bytes 812033 | tf_op jit(solution)/shard_map/convert_element_type | solution.py:285
  20.1 0.7 collective-permute-start.2
  20.7 0.1 multiply_convert_fusion.refs_0_
  20.8 1.6 %collective-permute-start.9 = (bf16[528,256]{1,0:T(8,128)(2,1)S(1)}, bf16[528,256]{1,0:T(8,128)(2,1)S(1)}, u32[]{:S(2)}, u32[]{:S(2)}) collective-permute-start(bf16[528,256]{1,0:T(8,128)(2,1)S(1)} %multiply_convert_fusion.refs_0_), channel_id=1, source_target_pairs={{0,3},{1,2},{2,1},{3,0},{4,7},{5,6},{6,5},{7,4},{8,11},{9,10},{10,... | collective-permute-start | bytes 811016 | tf_op jit(solution)/shard_map/ppermute | solution.py:244
  22.4 1.4 %collective-permute-start.8 = (bf16[528,256]{1,0:T(8,128)(2,1)S(1)}, bf16[528,256]{1,0:T(8,128)(2,1)S(1)}, u32[]{:S(2)}, u32[]{:S(2)}) collective-permute-start(bf16[528,256]{1,0:T(8,128)(2,1)S(1)} %multiply_convert_fusion.refs_0_), channel_id=1, source_target_pairs={{0,2},{1,3},{2,0},{3,1},{4,6},{5,7},{6,4},{7,5},{8,10},{9,11},{10,... | collective-permute-start | bytes 811016 | tf_op jit(solution)/shard_map/ppermute | solution.py:244
  23.9 2.0 %collective-permute-done.3.context_other = bf16[256,1024]{1,0:T(8,128)(2,1)} collective-permute-done((bf16[256,1024]{1,0:T(8,128)(2,1)}, bf16[256,1024]{1,0:T(8,128)(2,1)}, u32[]{:S(2)}, u32[]{:S(2)}) %collective-permute-start.3) | collective-permute-done | bytes 524320 | tf_op jit(solution)/shard_map/ppermute | solution.py:247
  25.9 1.5 %collective-permute-start.7 = (bf16[528,256]{1,0:T(8,128)(2,1)S(1)}, bf16[528,256]{1,0:T(8,128)(2,1)S(1)}, u32[]{:S(2)}, u32[]{:S(2)}) collective-permute-start(bf16[528,256]{1,0:T(8,128)(2,1)S(1)} %multiply_convert_fusion.refs_0_), channel_id=1, source_target_pairs={{0,1},{1,0},{2,3},{3,2},{4,5},{5,4},{6,7},{7,6},{8,9},{9,8},{10,11... | collective-permute-start | bytes 811016 | tf_op jit(solution)/shard_map/ppermute | solution.py:244
  27.4 3.4 %collective-permute-done.2.refs_0_.refs_4_ = bf16[528,256]{1,0:T(8,128)(2,1)S(1)} collective-permute-done((bf16[528,256]{1,0:T(8,128)(2,1)S(1)}, bf16[528,256]{1,0:T(8,128)(2,1)S(1)}, u32[]{:S(2)}, u32[]{:S(2)}) %collective-permute-start.2) | collective-permute-done | bytes 270368 | tf_op jit(solution)/shard_map/ppermute | solution.py:247
  30.8 2.5 %collective-permute-start.6 = (bf16[528,256]{1,0:T(8,128)(2,1)S(1)}, bf16[528,256]{1,0:T(8,128)(2,1)S(1)}, u32[]{:S(2)}, u32[]{:S(2)}) collective-permute-start(bf16[528,256]{1,0:T(8,128)(2,1)S(1)} %collective-permute-done.2.refs_0_.refs_4_), channel_id=1, source_target_pairs={{0,3},{1,2},{2,1},{3,0},{4,7},{5,6},{6,5},{7,4},{8,11},{9,10},{10,... | collective-permute-start | bytes 811016 | tf_op jit(solution)/shard_map/ppermute | solution.py:244
  33.3 0.1 pad_add_fusion.place_ref
  33.4 0.5 collective-permute-start.5
  33.8 0.5 collective-permute-start.4
  34.4 1.6 %copy-done.1 = bf16[1024,1056]{0,1:T(8,128)(2,1)S(1)} copy-done((bf16[1024,1056]{0,1:T(8,128)(2,1)S(1)}, bf16[1024,1056]{0,1:T(8,128)(2,1)}, u32[]{:S(2)}) %copy-start.1) | copy-done | bytes 2162712
  36.0 4.9 %shard_map.115 = (bf16[528,256]{1,0:T(8,128)(2,1)S(1)}, bf16[528,256]{1,0:T(8,128)(2,1)S(1)}, bf16[528,256]{1,0:T(8,128)(2,1)S(1)}, bf16[528,256]{1,0:T(8,128)(2...) custom-call(s32[2]{0:T(128)S(1)} %pad_add_fusion.place_ref, ...), custom_call_target="tpu_custom_call" | custom-call | flops 2214592512 | bytes 4325376 | tf_op jit(solution)/shard_map/pallas_call | solution.py:299
  40.9 1.6 %collective-permute-start.11 = (bf16[528,256]{1,0:T(8,128)(2,1)S(1)}, bf16[528,256]{1,0:T(8,128)(2,1)S(1)}, u32[]{:S(2)}, u32[]{:S(2)}) collective-permute-start(bf16[528,256]{1,0:T(8,128)(2,1)S(1)} %get-tuple-element.45), channel_id=1, source_target_pairs={{0,1},{1,0},{2,3},{3,2},{4,5},{5,4},{6,7},{7,6},{8,9},{9,8},{10,11... | collective-permute-start | bytes 811016 | tf_op jit(solution)/shard_map/ppermute | solution.py:244
  42.4 1.6 %collective-permute-start.12 = (bf16[528,256]{1,0:T(8,128)(2,1)S(1)}, bf16[528,256]{1,0:T(8,128)(2,1)S(1)}, u32[]{:S(2)}, u32[]{:S(2)}) collective-permute-start(bf16[528,256]{1,0:T(8,128)(2,1)S(1)} %get-tuple-element.46), channel_id=1, source_target_pairs={{0,2},{1,3},{2,0},{3,1},{4,6},{5,7},{6,4},{7,5},{8,10},{9,11},{10,... | collective-permute-start | bytes 811016 | tf_op jit(solution)/shard_map/ppermute | solution.py:244
  44.0 0.4 collective-permute-start.13
  44.4 3.1 %shard_map.113.refs_4_.own_ref = f32[256,1024]{1,0:T(8,128)S(1)} custom-call(s32[2]{0:T(128)S(1)} %pad_add_fusion.place_ref, bf16[1056,1024]{1,0:T(8,128)(2,1)S(1)} %bitcast.17, bf16[1056,1024]{1,0:T(8,128)(2,1)S(1)} %collective-permute-done.other_w, bf16[528,256]{1,0:T(8,128)(2,1)S(1)} %multiply_convert_fusion.refs_0_, ...), custom_call_target="tpu_custom_call" | custom-call | flops 1107296256 | bytes 4325376 | tf_op jit(solution)/shard_map/pallas_call | solution.py:323
  47.5 1.2 %collective-permute-done.5.refs_2_.refs_6_ = bf16[528,256]{1,0:T(8,128)(2,1)S(1)} collective-permute-done((bf16[528,256]{1,0:T(8,128)(2,1)S(1)}, bf16[528,256]{1,0:T(8,128)(2,1)S(1)}, u32[]{:S(2)}, u32[]{:S(2)}) %collective-permute-start.5) | collective-permute-done | bytes 270368 | tf_op jit(solution)/shard_map/ppermute | solution.py:244
  48.7 3.0 %shard_map.114.refs_8_ = bf16[256,1024]{1,0:T(8,128)(2,1)S(1)} custom-call(s32[2]{0:T(128)S(1)} %pad_add_fusion.place_ref, bf16[1056,1024]{1,0:T(8,128)(2,1)S(1)} %bitcast.18, bf16[1056,1024]{1,0:T(8,128)(2,1)S(1)} %collective-permute-done.other_w, bf16[528,256]{1,0:T(8,128)(2,1)S(1)} %collective-permute-done.2.refs_0_.refs_4_, ...), custom_call_target="tpu_custom_call" | custom-call | flops 1107296256 | bytes 4325376 | tf_op jit(solution)/shard_map/pallas_call | solution.py:323
  51.7 2.5 %collective-permute-start.10 = (bf16[256,1024]{1,0:T(8,128)(2,1)S(1)}, bf16[256,1024]{1,0:T(8,128)(2,1)S(1)}, u32[]{:S(2)}, u32[]{:S(2)}) collective-permute-start(bf16[256,1024]{1,0:T(8,128)(2,1)S(1)} %shard_map.114.refs_8_), channel_id=1, source_target_pairs={{0,16},{8,24},{16,0},{24,8},{1,17},{9,25},{17,1},{25,9},{2,18},{10... | collective-permute-start | bytes 1572872 | tf_op jit(solution)/shard_map/ppermute | solution.py:247
  54.2 0.4 collective-permute-start.14
  54.7 0.7 collective-permute-start.15
  55.4 2.3 %collective-permute-start.16 = (bf16[528,256]{1,0:T(8,128)(2,1)S(1)}, bf16[528,256]{1,0:T(8,128)(2,1)S(1)}, u32[]{:S(2)}, u32[]{:S(2)}) collective-permute-start(bf16[528,256]{1,0:T(8,128)(2,1)S(1)} %get-tuple-element.57), channel_id=1, source_target_pairs={{0,3},{1,2},{2,1},{3,0},{4,7},{5,6},{6,5},{7,4},{8,11},{9,10},{10,... | collective-permute-start | bytes 811016 | tf_op jit(solution)/shard_map/ppermute | solution.py:244
  57.7 2.5 %collective-permute-done.13 = bf16[528,256]{1,0:T(8,128)(2,1)S(1)} collective-permute-done((bf16[528,256]{1,0:T(8,128)(2,1)S(1)}, bf16[528,256]{1,0:T(8,128)(2,1)S(1)}, u32[]{:S(2)}, u32[]{:S(2)}) %collective-permute-start.13) | collective-permute-done | bytes 270368 | tf_op jit(solution)/shard_map/ppermute | solution.py:244
  60.3 0.2 add_convert_fusion.1
  60.4 0.0 copy-start.4
  60.4 2.6 %collective-permute-start.17 = (bf16[528,256]{1,0:T(8,128)(2,1)S(1)}, bf16[528,256]{1,0:T(8,128)(2,1)S(1)}, u32[]{:S(2)}, u32[]{:S(2)}) collective-permute-start(bf16[528,256]{1,0:T(8,128)(2,1)S(1)} %add_convert_fusion.1), channel_id=1, source_target_pairs={{0,16},{8,24},{16,0},{24,8},{1,17},{9,25},{17,1},{25,9},{2,18},{10... | collective-permute-start | bytes 811016 | tf_op jit(solution)/shard_map/ppermute | solution.py:247
  63.0 4.5 %shard_map.116 = (f32[1056,1024]{1,0:T(8,128)S(1)}, bf16[1056,1024]{1,0:T(8,128)(2,1)S(1)}) custom-call(s32[2]{0:T(128)S(1)} %pad_add_fusion.place_ref, bf16[256,1024]{1,0:T(8,128)(2,1)} %get-tuple-element.48.context_own, bf16[256,1024]{1,0:T(8,128)(2,1)} %collective-permute-done.3.context_other, bf16[528,256]{1,0:T(8,128)(2,1)S(1)} %multiply_convert_fusion.refs_0_, ...), custom_call_target="tpu_custom_call" | custom-call | flops 2214592512 | bytes 6488064 | tf_op jit(solution)/shard_map/pallas_call | solution.py:349
  67.5 2.6 %collective-permute-done.16 = bf16[528,256]{1,0:T(8,128)(2,1)S(1)} collective-permute-done((bf16[528,256]{1,0:T(8,128)(2,1)S(1)}, bf16[528,256]{1,0:T(8,128)(2,1)S(1)}, u32[]{:S(2)}, u32[]{:S(2)}) %collective-permute-start.16) | collective-permute-done | bytes 270368 | tf_op jit(solution)/shard_map/ppermute | solution.py:244
  70.2 0.2 add_convert_fusion
  70.3 0.1 collective-permute-done.17
  70.4 0.0 collective-permute-start.23
  70.5 2.4 %shard_map.117 = (bf16[4,64,1024]{2,1,0:T(8,128)(2,1)}, bf16[4,2,64,128]{3,2,1,0:T(8,128)(2,1)S(1)}) custom-call(f32[256,1024]{1,0:T(8,128)S(1)} %shard_map.113.refs_4_.own_ref, bf16[256,1024]{1,0:T(8,128)(2,1)S(1)} %collective-permute-done.10.got_ref, bf16[4,64,1024]{2,1,0:T(8,128)(2,1)S(1)} %bitcast.20, bf16[4,2,64,128]{3,2,1,0:T(8,128)(2,1)S(1)} %copy-done.6, ...), custom_call_target="tpu_custom_call" | custom-call | flops 234881024 | bytes 4194304 | tf_op jit(solution)/shard_map/pallas_call | solution.py:368
  72.9 4.7 %collective-permute-start.22 = (bf16[512,128]{1,0:T(8,128)(2,1)S(1)}, bf16[512,128]{1,0:T(8,128)(2,1)S(1)}, u32[]{:S(2)}, u32[]{:S(2)}) collective-permute-start(bf16[512,128]{1,0:T(8,128)(2,1)S(1)} %bitcast.23), channel_id=1, source_target_pairs={{0,4},{1,5},{2,6},{3,7},{4,0},{5,1},{6,2},{7,3},{8,12},{9,13},{10,... | collective-permute-start | bytes 393224 | tf_op jit(solution)/shard_map/ppermute | solution.py:244
  77.6 2.6 %collective-permute-start.21 = (bf16[512,128]{1,0:T(8,128)(2,1)S(1)}, bf16[512,128]{1,0:T(8,128)(2,1)S(1)}, u32[]{:S(2)}, u32[]{:S(2)}) collective-permute-start(bf16[512,128]{1,0:T(8,128)(2,1)S(1)} %bitcast.24), channel_id=1, source_target_pairs={{0,3},{1,2},{2,1},{3,0},{4,7},{5,6},{6,5},{7,4},{8,11},{9,10},{10,... | collective-permute-start | bytes 393224 | tf_op jit(solution)/shard_map/ppermute | solution.py:244
  80.3 0.8 collective-permute-start.19
  81.2 0.1 collective-permute-start.18
  81.3 2.9 %add_bitcast_fusion = f32[1024,1056]{0,1:T(8,128)} fusion(f32[1056,1024]{1,0:T(8,128)S(1)} %get-tuple-element.68, bf16[1056,1024]{1,0:T(8,128)(2,1)S(1)} %collective-permute-done.23), kind=kLoop, calls=%fused_computation | loop fusion | flops 2162688 | bytes 10813440 | tf_op jit(solution)/shard_map/transpose | solution.py:378
  84.2 0.7 collective-permute-done.22.refs_4_
  84.9 1.9 %collective-permute-start.26 = (bf16[512,128]{1,0:T(8,128)(2,1)S(1)}, bf16[512,128]{1,0:T(8,128)(2,1)S(1)}, u32[]{:S(2)}, u32[]{:S(2)}) collective-permute-start(bf16[512,128]{1,0:T(8,128)(2,1)S(1)} %collective-permute-done.22.refs_4_), channel_id=1, source_target_pairs={{0,3},{1,2},{2,1},{3,0},{4,7},{5,6},{6,5},{7,4},{8,11},{9,10},{10,... | collective-permute-start | bytes 393224 | tf_op jit(solution)/shard_map/ppermute | solution.py:244
  86.8 3.3 %collective-permute-done.21.refs_3_ = bf16[512,128]{1,0:T(8,128)(2,1)S(1)} collective-permute-done((bf16[512,128]{1,0:T(8,128)(2,1)S(1)}, bf16[512,128]{1,0:T(8,128)(2,1)S(1)}, u32[]{:S(2)}, u32[]{:S(2)}) %collective-permute-start.21) | collective-permute-done | bytes 131104 | tf_op jit(solution)/shard_map/ppermute | solution.py:244
  90.1 1.8 %collective-permute-done.20.refs_2_ = bf16[512,128]{1,0:T(8,128)(2,1)S(1)} collective-permute-done((bf16[512,128]{1,0:T(8,128)(2,1)S(1)}, bf16[512,128]{1,0:T(8,128)(2,1)S(1)}, u32[]{:S(2)}, u32[]{:S(2)}) %collective-permute-start.20) | collective-permute-done | bytes 131104 | tf_op jit(solution)/shard_map/ppermute | solution.py:244
  92.0 1.5 %collective-permute-start.24 = (bf16[512,128]{1,0:T(8,128)(2,1)S(1)}, bf16[512,128]{1,0:T(8,128)(2,1)S(1)}, u32[]{:S(2)}, u32[]{:S(2)}) collective-permute-start(bf16[512,128]{1,0:T(8,128)(2,1)S(1)} %collective-permute-done.22.refs_4_), channel_id=1, source_target_pairs={{0,1},{1,0},{2,3},{3,2},{4,5},{5,4},{6,7},{7,6},{8,9},{9,8},{10,11... | collective-permute-start | bytes 393224 | tf_op jit(solution)/shard_map/ppermute | solution.py:244
  93.5 2.8 %collective-permute-done.18.got_ref = bf16[528,256]{1,0:T(8,128)(2,1)S(1)} collective-permute-done((bf16[528,256]{1,0:T(8,128)(2,1)S(1)}, bf16[528,256]{1,0:T(8,128)(2,1)S(1)}, u32[]{:S(2)}, u32[]{:S(2)}) %collective-permute-start.18) | collective-permute-done | bytes 270368 | tf_op jit(solution)/shard_map/ppermute | solution.py:244
  96.3 1.0 shard_map.118
  97.3 1.7 %collective-permute-done.25.refs_6_ = bf16[512,128]{1,0:T(8,128)(2,1)S(1)} collective-permute-done((bf16[512,128]{1,0:T(8,128)(2,1)S(1)}, bf16[512,128]{1,0:T(8,128)(2,1)S(1)}, u32[]{:S(2)}, u32[]{:S(2)}) %collective-permute-start.25) | collective-permute-done | bytes 131104 | tf_op jit(solution)/shard_map/ppermute | solution.py:244
  99.0 1.6 %shard_map.119 = bf16[512,1024]{1,0:T(8,128)(2,1)} custom-call(s32[2]{0:T(128)S(1)} %pad_add_fusion.place_ref, bf16[512,128]{1,0:T(8,128)(2,1)S(1)} %bitcast.27, bf16[512,128]{1,0:T(8,128)(2,1)S(1)} %collective-permute-done.19.refs_1_, bf16[512,128]{1,0:T(8,128)(2,1)S(1)} %collective-permute-done.20.refs_2_, ...), custom_call_target="tpu_custom_call" | custom-call | bytes 1048576 | tf_op jit(solution)/shard_map/pallas_call | solution.py:397
  (35 shorter events, 0.2 us)
Async XLA Ops:
  0.6 5.4 %copy-start = (bf16[1,4,2,64,1024]{4,3,2,1,0:T(8,128)(2,1)S(1)}, bf16[1,4,2,64,1024]{4,3,2,1,0:T(8,128)(2,1)}, u32[]{:S(2)}) copy-start(bf16[1,4,2,64,1024]{4,3,2,1,0:T(8,128)(2,1)} %param.9) | copy-start | bytes 3145732
  0.6 33.2 %collective-permute-start = (bf16[1056,1024]{1,0:T(8,128)(2,1)}, bf16[1056,1024]{1,0:T(8,128)(2,1)S(1)}, u32[]{:S(2)}, u32[]{:S(2)}) collective-permute-start(bf16[1056,1024]{1,0:T(8,128)(2,1)} %bitcast.15), channel_id=1, source_target_pairs={{0,8},{8,0},{16,24},{24,16},{1,9},{9,1},{17,25},{25,17},{2,10},{10... | collective-permute-start | bytes 6488072 | tf_op jit(solution)/shard_map/ppermute | solution.py:250
  1.2 1.0 copy-start.10
  2.3 16.7 %collective-permute-start.1 = (bf16[528,256]{1,0:T(8,128)(2,1)S(1)}, bf16[528,256]{1,0:T(8,128)(2,1)}, u32[]{:S(2)}, u32[]{:S(2)}) collective-permute-start(bf16[528,256]{1,0:T(8,128)(2,1)S(1)} %shard_map.111), channel_id=1, source_target_pairs={{0,4},{1,5},{2,6},{3,7},{4,0},{5,1},{6,2},{7,3},{8,12},{9,13},{10,... | collective-permute-start | bytes 811016 | tf_op jit(solution)/shard_map/ppermute | solution.py:244
  6.1 3.7 %copy-start.5 = (bf16[4,2,64,128]{3,2,1,0:T(8,128)(2,1)}, bf16[4,2,64,128]{3,2,1,0:T(8,128)(2,1)S(1)}, u32[]{:S(2)}) copy-start(bf16[4,2,64,128]{3,2,1,0:T(8,128)(2,1)S(1)} %dynamic-slice_bitcast_fusion.key_value_ref) | copy-start | bytes 393220
  6.1 1.1 %copy-start.3 = (bf16[1,4,64,1024]{3,2,1,0:T(8,128)(2,1)S(1)}, bf16[1,4,64,1024]{3,2,1,0:T(8,128)(2,1)}, u32[]{:S(2)}) copy-start(bf16[1,4,64,1024]{3,2,1,0:T(8,128)(2,1)} %param.8) | copy-start | bytes 1572868
  7.2 0.7 copy-start.11
  9.8 1.0 copy-start.7
  10.8 15.1 %collective-permute-start.3 = (bf16[256,1024]{1,0:T(8,128)(2,1)}, bf16[256,1024]{1,0:T(8,128)(2,1)}, u32[]{:S(2)}, u32[]{:S(2)}) collective-permute-start(bf16[256,1024]{1,0:T(8,128)(2,1)} %get-tuple-element.48.context_own), channel_id=1, source_target_pairs={{0,16},{8,24},{16,0},{24,8},{1,17},{9,25},{17,1},{25,9},{2,18},{10... | collective-permute-start | bytes 1572872 | tf_op jit(solution)/shard_map/ppermute | solution.py:247
  20.1 10.7 %collective-permute-start.2 = (bf16[528,256]{1,0:T(8,128)(2,1)S(1)}, bf16[528,256]{1,0:T(8,128)(2,1)S(1)}, u32[]{:S(2)}, u32[]{:S(2)}) collective-permute-start(bf16[528,256]{1,0:T(8,128)(2,1)S(1)} %multiply_convert_fusion.1), channel_id=1, source_target_pairs={{0,16},{8,24},{16,0},{24,8},{1,17},{9,25},{17,1},{25,9},{2,18},{10... | collective-permute-start | bytes 811016 | tf_op jit(solution)/shard_map/ppermute | solution.py:247
  20.8 12.6 %collective-permute-start.9 = (bf16[528,256]{1,0:T(8,128)(2,1)S(1)}, bf16[528,256]{1,0:T(8,128)(2,1)S(1)}, u32[]{:S(2)}, u32[]{:S(2)}) collective-permute-start(bf16[528,256]{1,0:T(8,128)(2,1)S(1)} %multiply_convert_fusion.refs_0_), channel_id=1, source_target_pairs={{0,3},{1,2},{2,1},{3,0},{4,7},{5,6},{6,5},{7,4},{8,11},{9,10},{10,... | collective-permute-start | bytes 811016 | tf_op jit(solution)/shard_map/ppermute | solution.py:244
  22.4 18.4 %collective-permute-start.8 = (bf16[528,256]{1,0:T(8,128)(2,1)S(1)}, bf16[528,256]{1,0:T(8,128)(2,1)S(1)}, u32[]{:S(2)}, u32[]{:S(2)}) collective-permute-start(bf16[528,256]{1,0:T(8,128)(2,1)S(1)} %multiply_convert_fusion.refs_0_), channel_id=1, source_target_pairs={{0,2},{1,3},{2,0},{3,1},{4,6},{5,7},{6,4},{7,5},{8,10},{9,11},{10,... | collective-permute-start | bytes 811016 | tf_op jit(solution)/shard_map/ppermute | solution.py:244
  25.9 16.6 %collective-permute-start.7 = (bf16[528,256]{1,0:T(8,128)(2,1)S(1)}, bf16[528,256]{1,0:T(8,128)(2,1)S(1)}, u32[]{:S(2)}, u32[]{:S(2)}) collective-permute-start(bf16[528,256]{1,0:T(8,128)(2,1)S(1)} %multiply_convert_fusion.refs_0_), channel_id=1, source_target_pairs={{0,1},{1,0},{2,3},{3,2},{4,5},{5,4},{6,7},{7,6},{8,9},{9,8},{10,11... | collective-permute-start | bytes 811016 | tf_op jit(solution)/shard_map/ppermute | solution.py:244
  30.8 13.2 %collective-permute-start.6 = (bf16[528,256]{1,0:T(8,128)(2,1)S(1)}, bf16[528,256]{1,0:T(8,128)(2,1)S(1)}, u32[]{:S(2)}, u32[]{:S(2)}) collective-permute-start(bf16[528,256]{1,0:T(8,128)(2,1)S(1)} %collective-permute-done.2.refs_0_.refs_4_), channel_id=1, source_target_pairs={{0,3},{1,2},{2,1},{3,0},{4,7},{5,6},{6,5},{7,4},{8,11},{9,10},{10,... | collective-permute-start | bytes 811016 | tf_op jit(solution)/shard_map/ppermute | solution.py:244
  33.4 15.3 %collective-permute-start.5 = (bf16[528,256]{1,0:T(8,128)(2,1)S(1)}, bf16[528,256]{1,0:T(8,128)(2,1)S(1)}, u32[]{:S(2)}, u32[]{:S(2)}) collective-permute-start(bf16[528,256]{1,0:T(8,128)(2,1)S(1)} %collective-permute-done.2.refs_0_.refs_4_), channel_id=1, source_target_pairs={{0,2},{1,3},{2,0},{3,1},{4,6},{5,7},{6,4},{7,5},{8,10},{9,11},{10,... | collective-permute-start | bytes 811016 | tf_op jit(solution)/shard_map/ppermute | solution.py:244
  33.8 14.8 %collective-permute-start.4 = (bf16[528,256]{1,0:T(8,128)(2,1)S(1)}, bf16[528,256]{1,0:T(8,128)(2,1)S(1)}, u32[]{:S(2)}, u32[]{:S(2)}) collective-permute-start(bf16[528,256]{1,0:T(8,128)(2,1)S(1)} %collective-permute-done.2.refs_0_.refs_4_), channel_id=1, source_target_pairs={{0,1},{1,0},{2,3},{3,2},{4,5},{5,4},{6,7},{7,6},{8,9},{9,8},{10,11... | collective-permute-start | bytes 811016 | tf_op jit(solution)/shard_map/ppermute | solution.py:244
  34.3 1.6 %copy-start.1 = (bf16[1024,1056]{0,1:T(8,128)(2,1)S(1)}, bf16[1024,1056]{0,1:T(8,128)(2,1)}, u32[]{:S(2)}) copy-start(bf16[1024,1056]{0,1:T(8,128)(2,1)} %param.13) | copy-start | bytes 6488068
  36.0 8.5 %copy-start.2 = (bf16[1024,1056]{0,1:T(8,128)(2,1)S(1)}, bf16[1024,1056]{0,1:T(8,128)(2,1)}, u32[]{:S(2)}) copy-start(bf16[1024,1056]{0,1:T(8,128)(2,1)} %param.13) | copy-start | bytes 6488068
  40.9 13.8 %collective-permute-start.11 = (bf16[528,256]{1,0:T(8,128)(2,1)S(1)}, bf16[528,256]{1,0:T(8,128)(2,1)S(1)}, u32[]{:S(2)}, u32[]{:S(2)}) collective-permute-start(bf16[528,256]{1,0:T(8,128)(2,1)S(1)} %get-tuple-element.45), channel_id=1, source_target_pairs={{0,1},{1,0},{2,3},{3,2},{4,5},{5,4},{6,7},{7,6},{8,9},{9,8},{10,11... | collective-permute-start | bytes 811016 | tf_op jit(solution)/shard_map/ppermute | solution.py:244
  42.4 13.0 %collective-permute-start.12 = (bf16[528,256]{1,0:T(8,128)(2,1)S(1)}, bf16[528,256]{1,0:T(8,128)(2,1)S(1)}, u32[]{:S(2)}, u32[]{:S(2)}) collective-permute-start(bf16[528,256]{1,0:T(8,128)(2,1)S(1)} %get-tuple-element.46), channel_id=1, source_target_pairs={{0,2},{1,3},{2,0},{3,1},{4,6},{5,7},{6,4},{7,5},{8,10},{9,11},{10,... | collective-permute-start | bytes 811016 | tf_op jit(solution)/shard_map/ppermute | solution.py:244
  44.0 16.2 %collective-permute-start.13 = (bf16[528,256]{1,0:T(8,128)(2,1)S(1)}, bf16[528,256]{1,0:T(8,128)(2,1)S(1)}, u32[]{:S(2)}, u32[]{:S(2)}) collective-permute-start(bf16[528,256]{1,0:T(8,128)(2,1)S(1)} %get-tuple-element.47), channel_id=1, source_target_pairs={{0,3},{1,2},{2,1},{3,0},{4,7},{5,6},{6,5},{7,4},{8,11},{9,10},{10,... | collective-permute-start | bytes 811016 | tf_op jit(solution)/shard_map/ppermute | solution.py:244
  51.7 18.6 %collective-permute-start.10 = (bf16[256,1024]{1,0:T(8,128)(2,1)S(1)}, bf16[256,1024]{1,0:T(8,128)(2,1)S(1)}, u32[]{:S(2)}, u32[]{:S(2)}) collective-permute-start(bf16[256,1024]{1,0:T(8,128)(2,1)S(1)} %shard_map.114.refs_8_), channel_id=1, source_target_pairs={{0,16},{8,24},{16,0},{24,8},{1,17},{9,25},{17,1},{25,9},{2,18},{10... | collective-permute-start | bytes 1572872 | tf_op jit(solution)/shard_map/ppermute | solution.py:247
  54.2 13.3 %collective-permute-start.14 = (bf16[528,256]{1,0:T(8,128)(2,1)S(1)}, bf16[528,256]{1,0:T(8,128)(2,1)S(1)}, u32[]{:S(2)}, u32[]{:S(2)}) collective-permute-start(bf16[528,256]{1,0:T(8,128)(2,1)S(1)} %get-tuple-element.55), channel_id=1, source_target_pairs={{0,1},{1,0},{2,3},{3,2},{4,5},{5,4},{6,7},{7,6},{8,9},{9,8},{10,11... | collective-permute-start | bytes 811016 | tf_op jit(solution)/shard_map/ppermute | solution.py:244
  54.7 12.9 %collective-permute-start.15 = (bf16[528,256]{1,0:T(8,128)(2,1)S(1)}, bf16[528,256]{1,0:T(8,128)(2,1)S(1)}, u32[]{:S(2)}, u32[]{:S(2)}) collective-permute-start(bf16[528,256]{1,0:T(8,128)(2,1)S(1)} %get-tuple-element.56), channel_id=1, source_target_pairs={{0,2},{1,3},{2,0},{3,1},{4,6},{5,7},{6,4},{7,5},{8,10},{9,11},{10,... | collective-permute-start | bytes 811016 | tf_op jit(solution)/shard_map/ppermute | solution.py:244
  55.4 14.8 %collective-permute-start.16 = (bf16[528,256]{1,0:T(8,128)(2,1)S(1)}, bf16[528,256]{1,0:T(8,128)(2,1)S(1)}, u32[]{:S(2)}, u32[]{:S(2)}) collective-permute-start(bf16[528,256]{1,0:T(8,128)(2,1)S(1)} %get-tuple-element.57), channel_id=1, source_target_pairs={{0,3},{1,2},{2,1},{3,0},{4,7},{5,6},{6,5},{7,4},{8,11},{9,10},{10,... | collective-permute-start | bytes 811016 | tf_op jit(solution)/shard_map/ppermute | solution.py:244
  60.4 10.0 %copy-start.4 = (bf16[1,4,64,1024]{3,2,1,0:T(8,128)(2,1)S(1)}, bf16[1,4,64,1024]{3,2,1,0:T(8,128)(2,1)}, u32[]{:S(2)}) copy-start(bf16[1,4,64,1024]{3,2,1,0:T(8,128)(2,1)} %param.8) | copy-start | bytes 1572868
  60.4 10.0 %copy-start.6 = (bf16[4,2,64,128]{3,2,1,0:T(8,128)(2,1)S(1)}, bf16[4,2,64,128]{3,2,1,0:T(8,128)(2,1)}, u32[]{:S(2)}) copy-start(bf16[4,2,64,128]{3,2,1,0:T(8,128)(2,1)} %copy-done.5) | copy-start | bytes 393220
  60.4 10.0 %copy-start.8 = (f32[4,512,64]{2,1,0:T(8,128)S(1)}, f32[4,512,64]{2,1,0:T(8,128)}, u32[]{:S(2)}) copy-start(f32[4,512,64]{2,1,0:T(8,128)} %copy-done.7) | copy-start | bytes 1572868
  60.4 10.0 %collective-permute-start.17 = (bf16[528,256]{1,0:T(8,128)(2,1)S(1)}, bf16[528,256]{1,0:T(8,128)(2,1)S(1)}, u32[]{:S(2)}, u32[]{:S(2)}) collective-permute-start(bf16[528,256]{1,0:T(8,128)(2,1)S(1)} %add_convert_fusion.1), channel_id=1, source_target_pairs={{0,16},{8,24},{16,0},{24,8},{1,17},{9,25},{17,1},{25,9},{2,18},{10... | collective-permute-start | bytes 811016 | tf_op jit(solution)/shard_map/ppermute | solution.py:247
  70.4 10.8 %collective-permute-start.23 = (bf16[1056,1024]{1,0:T(8,128)(2,1)S(1)}, bf16[1056,1024]{1,0:T(8,128)(2,1)S(1)}, u32[]{:S(2)}, u32[]{:S(2)}) collective-permute-start(bf16[1056,1024]{1,0:T(8,128)(2,1)S(1)} %get-tuple-element.69), channel_id=1, source_target_pairs={{0,8},{8,0},{16,24},{24,16},{1,9},{9,1},{17,25},{25,17},{2,10},{10... | collective-permute-start | bytes 6488072 | tf_op jit(solution)/shard_map/ppermute | solution.py:250
  72.9 12.0 %collective-permute-start.22 = (bf16[512,128]{1,0:T(8,128)(2,1)S(1)}, bf16[512,128]{1,0:T(8,128)(2,1)S(1)}, u32[]{:S(2)}, u32[]{:S(2)}) collective-permute-start(bf16[512,128]{1,0:T(8,128)(2,1)S(1)} %bitcast.23), channel_id=1, source_target_pairs={{0,4},{1,5},{2,6},{3,7},{4,0},{5,1},{6,2},{7,3},{8,12},{9,13},{10,... | collective-permute-start | bytes 393224 | tf_op jit(solution)/shard_map/ppermute | solution.py:244
  77.6 12.5 %collective-permute-start.21 = (bf16[512,128]{1,0:T(8,128)(2,1)S(1)}, bf16[512,128]{1,0:T(8,128)(2,1)S(1)}, u32[]{:S(2)}, u32[]{:S(2)}) collective-permute-start(bf16[512,128]{1,0:T(8,128)(2,1)S(1)} %bitcast.24), channel_id=1, source_target_pairs={{0,3},{1,2},{2,1},{3,0},{4,7},{5,6},{6,5},{7,4},{8,11},{9,10},{10,... | collective-permute-start | bytes 393224 | tf_op jit(solution)/shard_map/ppermute | solution.py:244
  80.3 11.7 %collective-permute-start.20 = (bf16[512,128]{1,0:T(8,128)(2,1)S(1)}, bf16[512,128]{1,0:T(8,128)(2,1)S(1)}, u32[]{:S(2)}, u32[]{:S(2)}) collective-permute-start(bf16[512,128]{1,0:T(8,128)(2,1)S(1)} %bitcast.25), channel_id=1, source_target_pairs={{0,2},{1,3},{2,0},{3,1},{4,6},{5,7},{6,4},{7,5},{8,10},{9,11},{10,... | collective-permute-start | bytes 393224 | tf_op jit(solution)/shard_map/ppermute | solution.py:244
  80.3 13.2 %collective-permute-start.19 = (bf16[512,128]{1,0:T(8,128)(2,1)S(1)}, bf16[512,128]{1,0:T(8,128)(2,1)S(1)}, u32[]{:S(2)}, u32[]{:S(2)}) collective-permute-start(bf16[512,128]{1,0:T(8,128)(2,1)S(1)} %bitcast.26), channel_id=1, source_target_pairs={{0,1},{1,0},{2,3},{3,2},{4,5},{5,4},{6,7},{7,6},{8,9},{9,8},{10,11... | collective-permute-start | bytes 393224 | tf_op jit(solution)/shard_map/ppermute | solution.py:244
  81.2 15.1 %collective-permute-start.18 = (bf16[528,256]{1,0:T(8,128)(2,1)S(1)}, bf16[528,256]{1,0:T(8,128)(2,1)S(1)}, u32[]{:S(2)}, u32[]{:S(2)}) collective-permute-start(bf16[528,256]{1,0:T(8,128)(2,1)S(1)} %get-tuple-element.75), channel_id=1, source_target_pairs={{0,4},{1,5},{2,6},{3,7},{4,0},{5,1},{6,2},{7,3},{8,12},{9,13},{10,... | collective-permute-start | bytes 811016 | tf_op jit(solution)/shard_map/ppermute | solution.py:244
  81.2 15.1 %copy-start.9 = (bf16[1,4,64,528]{3,2,1,0:T(8,128)(2,1)S(1)}, bf16[1,4,64,528]{3,2,1,0:T(8,128)(2,1)}, u32[]{:S(2)}) copy-start(bf16[1,4,64,528]{3,2,1,0:T(8,128)(2,1)} %param.11) | copy-start | bytes 811012
  84.9 12.4 %collective-permute-start.26 = (bf16[512,128]{1,0:T(8,128)(2,1)S(1)}, bf16[512,128]{1,0:T(8,128)(2,1)S(1)}, u32[]{:S(2)}, u32[]{:S(2)}) collective-permute-start(bf16[512,128]{1,0:T(8,128)(2,1)S(1)} %collective-permute-done.22.refs_4_), channel_id=1, source_target_pairs={{0,3},{1,2},{2,1},{3,0},{4,7},{5,6},{6,5},{7,4},{8,11},{9,10},{10,... | collective-permute-start | bytes 393224 | tf_op jit(solution)/shard_map/ppermute | solution.py:244
  90.1 8.9 %collective-permute-start.25 = (bf16[512,128]{1,0:T(8,128)(2,1)S(1)}, bf16[512,128]{1,0:T(8,128)(2,1)S(1)}, u32[]{:S(2)}, u32[]{:S(2)}) collective-permute-start(bf16[512,128]{1,0:T(8,128)(2,1)S(1)} %collective-permute-done.22.refs_4_), channel_id=1, source_target_pairs={{0,2},{1,3},{2,0},{3,1},{4,6},{5,7},{6,4},{7,5},{8,10},{9,11},{10,... | collective-permute-start | bytes 393224 | tf_op jit(solution)/shard_map/ppermute | solution.py:244
  92.0 7.0 %collective-permute-start.24 = (bf16[512,128]{1,0:T(8,128)(2,1)S(1)}, bf16[512,128]{1,0:T(8,128)(2,1)S(1)}, u32[]{:S(2)}, u32[]{:S(2)}) collective-permute-start(bf16[512,128]{1,0:T(8,128)(2,1)S(1)} %collective-permute-done.22.refs_4_), channel_id=1, source_target_pairs={{0,1},{1,0},{2,3},{3,2},{4,5},{5,4},{6,7},{7,6},{8,9},{9,8},{10,11... | collective-permute-start | bytes 393224 | tf_op jit(solution)/shard_map/ppermute | solution.py:244

commit v5 on v4

--- a/solution.py
+++ b/solution.py
@@ -316,7 +316,7 @@
     near, far = list(partial[::2]), partial[1::2]
     far = [swap(far[mask], mask) if mask else far[mask] for mask in range(inner)]
 
-    tile = min(512, width)
+    tile = min(1024, width)
     column = lambda rows: pl.BlockSpec((rows, tile), lambda i: (0, i))
 
     def context_grad(shards, dtype):

time: 101 us -> 101 us (level)
  starting transfers between devices: 38.4 us -> 41.1 us
  Pallas kernels: 22.5 us -> 20.6 us
    ppermute x21, starting transfers between devices: 30.6 us -> 33.2 us  [swap(): lax.ppermute(array, 'tensor', [(t, t ^ mask) for t in range(tensor_size)])]
    pallas_call x2, Pallas kernels: 6.08 us -> 4.65 us  [context_grad(): call(functools.partial(context_grad_kernel, inner), shape((tokens, width)...]
  transfers between devices with their start and end apart: 27 -> 27, of which waited for: 12 -> 13; matrix products, arithmetic and copies ran while one was open for 7% -> 7% of each run, Pallas kernels for 21% -> 19%
where the time goes in v5:
time: 101 us
  starting transfers between devices  41.1 us (41%)
  waiting for transfers between devices  24.6 us (24%)
  Pallas kernels  20.6 us (20%)
  other arithmetic  6.51 us (6%)
  local copies, waits for them, and re-layouts  5.55 us (5%)
  between operations  2.33 us (2%)
    ppermute x21, starting transfers between devices, swap(): lax.ppermute(array, 'tensor', [(t, t ^ mask) for t in range(tensor_size)])  33.2 us
    ppermute x21, waiting for transfers between devices, swap(): lax.ppermute(array, 'tensor', [(t, t ^ mask) for t in range(tensor_size)])  19.2 us
    ppermute x4, starting transfers between devices, swap_x(): return lax.ppermute(array, 'dp', [(d, d ^ 2) for d in range(4)])  7.29 us
    ppermute x4, waiting for transfers between devices, swap_x(): return lax.ppermute(array, 'dp', [(d, d ^ 2) for d in range(4)])  5.4 us
    unnamed x24, local copies, waits for them, and re-layouts  5.36 us
    pallas_call x1, Pallas kernels, by_activations(): call(functools.partial(project_kernel, inner), [shape((features, tokens),...  4.88 us
    pallas_call x2, Pallas kernels, context_grad(): call(functools.partial(context_grad_kernel, inner), shape((tokens, width)...  4.65 us
    pallas_call x1, Pallas kernels, by_activations(): call(functools.partial(weight_grad_kernel, inner), (shape((own_rows, widt...  4.01 us
  transfers between devices with their start and end apart: 27, of which 13 were waited for; matrix products, arithmetic and copies ran while one was open for 7% of the time, Pallas kernels for 19%

profile of v5, /device:TPU:0, one launch (start us, length us, event | category | flops | bytes accessed | tf_op | source)
XLA Modules:
  0.0 100.7 jit_solution(8917801599741887845)
XLA Ops:
  0.6 0.0 copy-start
  0.6 0.5 collective-permute-start
  1.2 1.0 copy-done.10
  2.1 0.2 shard_map.111
  2.3 3.7 %collective-permute-start.1 = (bf16[528,256]{1,0:T(8,128)(2,1)S(1)}, bf16[528,256]{1,0:T(8,128)(2,1)}, u32[]{:S(2)}, u32[]{:S(2)}) collective-permute-start(bf16[528,256]{1,0:T(8,128)(2,1)S(1)} %shard_map.111), channel_id=1, source_target_pairs={{0,4},{1,5},{2,6},{3,7},{4,0},{5,1},{6,2},{7,3},{8,12},{9,13},{10,... | collective-permute-start | bytes 811016 | tf_op jit(solution)/shard_map/ppermute | solution.py:244
  6.1 0.0 copy-start.3
  6.1 1.1 %copy-done.3 = bf16[1,4,64,1024]{3,2,1,0:T(8,128)(2,1)S(1)} copy-done((bf16[1,4,64,1024]{3,2,1,0:T(8,128)(2,1)S(1)}, bf16[1,4,64,1024]{3,2,1,0:T(8,128)(2,1)}, u32[]{:S(2)}) %copy-start.3) | copy-done | bytes 524312
  7.2 0.7 copy-done.11
  7.9 1.9 %shard_map.112 = (bf16[256,1024]{1,0:T(8,128)(2,1)}, f32[4,512,64]{2,1,0:T(8,128)S(1)}) custom-call(bf16[4,64,1024]{2,1,0:T(8,128)(2,1)S(1)} %bitcast.19, bf16[4,2,64,128]{3,2,1,0:T(8,128)(2,1)S(1)} %dynamic-slice_bitcast_fusion.key_value_ref, s32[4,64]{1,0:T(4,128)S(1)} %bitcast.28), custom_call_target="tpu_custom_call" | custom-call | flops 67108864 | bytes 2097152 | tf_op jit(solution)/shard_map/pallas_call | solution.py:272
  9.8 1.0 copy-done.7
  10.8 1.5 %collective-permute-start.3 = (bf16[256,1024]{1,0:T(8,128)(2,1)}, bf16[256,1024]{1,0:T(8,128)(2,1)}, u32[]{:S(2)}, u32[]{:S(2)}) collective-permute-start(bf16[256,1024]{1,0:T(8,128)(2,1)} %get-tuple-element.48.context_own), channel_id=1, source_target_pairs={{0,16},{8,24},{16,0},{24,8},{1,17},{9,25},{17,1},{25,9},{2,18},{10... | collective-permute-start | bytes 1572872 | tf_op jit(solution)/shard_map/ppermute | solution.py:247
  12.3 1.4 %fusion = (s32[]{:T(128)}, s32[]{:T(128)}, s32[]{:T(128)}) fusion(s32[4]{0:T(128)} %param.15, s32[]{:T(128)} %axis_index.27, s32[4]{0:T(128)} %param.14), kind=kLoop, calls=%fused_computation.11 | loop fusion | flops 25 | bytes 48 | tf_op jit(solution)/shard_map/reduce_sum | solution.py:217
  15.0 0.7 and_select_fusion
  15.7 0.1 broadcast_in_dim.15
  15.8 0.1 mul.24
  15.8 3.2 %collective-permute-done.1 = bf16[528,256]{1,0:T(8,128)(2,1)} collective-permute-done((bf16[528,256]{1,0:T(8,128)(2,1)S(1)}, bf16[528,256]{1,0:T(8,128)(2,1)}, u32[]{:S(2)}, u32[]{:S(2)}) %collective-permute-start.1) | collective-permute-done | bytes 270368 | tf_op jit(solution)/shard_map/ppermute | solution.py:244
  19.0 1.0 %multiply_convert_fusion.1 = bf16[528,256]{1,0:T(8,128)(2,1)S(1)} fusion(f32[256]{0:T(256)S(1)} %mul.24, bf16[528,256]{1,0:T(8,128)(2,1)} %collective-permute-done.1, bf16[528,256]{1,0:T(8,128)(2,1)S(1)} %shard_map.111, pred[]{:T(512)S(6)} %eq.9), kind=kLoop, calls=%fused_computation.4 | loop fusion | flops 540672 | bytes 812033 | tf_op jit(solution)/shard_map/convert_element_type | solution.py:285
  20.1 0.7 collective-permute-start.2
  20.7 0.1 multiply_convert_fusion.refs_0_
  20.8 1.6 %collective-permute-start.9 = (bf16[528,256]{1,0:T(8,128)(2,1)S(1)}, bf16[528,256]{1,0:T(8,128)(2,1)S(1)}, u32[]{:S(2)}, u32[]{:S(2)}) collective-permute-start(bf16[528,256]{1,0:T(8,128)(2,1)S(1)} %multiply_convert_fusion.refs_0_), channel_id=1, source_target_pairs={{0,3},{1,2},{2,1},{3,0},{4,7},{5,6},{6,5},{7,4},{8,11},{9,10},{10,... | collective-permute-start | bytes 811016 | tf_op jit(solution)/shard_map/ppermute | solution.py:244
  22.4 1.4 %collective-permute-start.8 = (bf16[528,256]{1,0:T(8,128)(2,1)S(1)}, bf16[528,256]{1,0:T(8,128)(2,1)S(1)}, u32[]{:S(2)}, u32[]{:S(2)}) collective-permute-start(bf16[528,256]{1,0:T(8,128)(2,1)S(1)} %multiply_convert_fusion.refs_0_), channel_id=1, source_target_pairs={{0,2},{1,3},{2,0},{3,1},{4,6},{5,7},{6,4},{7,5},{8,10},{9,11},{10,... | collective-permute-start | bytes 811016 | tf_op jit(solution)/shard_map/ppermute | solution.py:244
  23.9 2.0 %collective-permute-done.3.context_other = bf16[256,1024]{1,0:T(8,128)(2,1)} collective-permute-done((bf16[256,1024]{1,0:T(8,128)(2,1)}, bf16[256,1024]{1,0:T(8,128)(2,1)}, u32[]{:S(2)}, u32[]{:S(2)}) %collective-permute-start.3) | collective-permute-done | bytes 524320 | tf_op jit(solution)/shard_map/ppermute | solution.py:247
  25.9 1.5 %collective-permute-start.7 = (bf16[528,256]{1,0:T(8,128)(2,1)S(1)}, bf16[528,256]{1,0:T(8,128)(2,1)S(1)}, u32[]{:S(2)}, u32[]{:S(2)}) collective-permute-start(bf16[528,256]{1,0:T(8,128)(2,1)S(1)} %multiply_convert_fusion.refs_0_), channel_id=1, source_target_pairs={{0,1},{1,0},{2,3},{3,2},{4,5},{5,4},{6,7},{7,6},{8,9},{9,8},{10,11... | collective-permute-start | bytes 811016 | tf_op jit(solution)/shard_map/ppermute | solution.py:244
  27.4 3.4 %collective-permute-done.2.refs_0_.refs_4_ = bf16[528,256]{1,0:T(8,128)(2,1)S(1)} collective-permute-done((bf16[528,256]{1,0:T(8,128)(2,1)S(1)}, bf16[528,256]{1,0:T(8,128)(2,1)S(1)}, u32[]{:S(2)}, u32[]{:S(2)}) %collective-permute-start.2) | collective-permute-done | bytes 270368 | tf_op jit(solution)/shard_map/ppermute | solution.py:247
  30.8 2.5 %collective-permute-start.6 = (bf16[528,256]{1,0:T(8,128)(2,1)S(1)}, bf16[528,256]{1,0:T(8,128)(2,1)S(1)}, u32[]{:S(2)}, u32[]{:S(2)}) collective-permute-start(bf16[528,256]{1,0:T(8,128)(2,1)S(1)} %collective-permute-done.2.refs_0_.refs_4_), channel_id=1, source_target_pairs={{0,3},{1,2},{2,1},{3,0},{4,7},{5,6},{6,5},{7,4},{8,11},{9,10},{10,... | collective-permute-start | bytes 811016 | tf_op jit(solution)/shard_map/ppermute | solution.py:244
  33.3 0.1 pad_add_fusion.place_ref
  33.4 0.5 collective-permute-start.5
  33.8 0.5 collective-permute-start.4
  34.4 1.6 %copy-done.1 = bf16[1024,1056]{0,1:T(8,128)(2,1)S(1)} copy-done((bf16[1024,1056]{0,1:T(8,128)(2,1)S(1)}, bf16[1024,1056]{0,1:T(8,128)(2,1)}, u32[]{:S(2)}) %copy-start.1) | copy-done | bytes 2162712
  36.0 4.9 %shard_map.115 = (bf16[528,256]{1,0:T(8,128)(2,1)S(1)}, bf16[528,256]{1,0:T(8,128)(2,1)S(1)}, bf16[528,256]{1,0:T(8,128)(2,1)S(1)}, bf16[528,256]{1,0:T(8,128)(2...) custom-call(s32[2]{0:T(128)S(1)} %pad_add_fusion.place_ref, ...), custom_call_target="tpu_custom_call" | custom-call | flops 2214592512 | bytes 4325376 | tf_op jit(solution)/shard_map/pallas_call | solution.py:299
  40.9 1.6 %collective-permute-start.11 = (bf16[528,256]{1,0:T(8,128)(2,1)S(1)}, bf16[528,256]{1,0:T(8,128)(2,1)S(1)}, u32[]{:S(2)}, u32[]{:S(2)}) collective-permute-start(bf16[528,256]{1,0:T(8,128)(2,1)S(1)} %get-tuple-element.45), channel_id=1, source_target_pairs={{0,1},{1,0},{2,3},{3,2},{4,5},{5,4},{6,7},{7,6},{8,9},{9,8},{10,11... | collective-permute-start | bytes 811016 | tf_op jit(solution)/shard_map/ppermute | solution.py:244
  42.4 1.6 %collective-permute-start.12 = (bf16[528,256]{1,0:T(8,128)(2,1)S(1)}, bf16[528,256]{1,0:T(8,128)(2,1)S(1)}, u32[]{:S(2)}, u32[]{:S(2)}) collective-permute-start(bf16[528,256]{1,0:T(8,128)(2,1)S(1)} %get-tuple-element.46), channel_id=1, source_target_pairs={{0,2},{1,3},{2,0},{3,1},{4,6},{5,7},{6,4},{7,5},{8,10},{9,11},{10,... | collective-permute-start | bytes 811016 | tf_op jit(solution)/shard_map/ppermute | solution.py:244
  44.0 0.4 collective-permute-start.13
  44.4 2.3 %shard_map.113.refs_4_.own_ref = f32[256,1024]{1,0:T(8,128)S(1)} custom-call(s32[2]{0:T(128)S(1)} %pad_add_fusion.place_ref, bf16[1056,1024]{1,0:T(8,128)(2,1)S(1)} %bitcast.17, bf16[1056,1024]{1,0:T(8,128)(2,1)S(1)} %collective-permute-done.other_w, bf16[528,256]{1,0:T(8,128)(2,1)S(1)} %multiply_convert_fusion.refs_0_, ...), custom_call_target="tpu_custom_call" | custom-call | flops 1107296256 | bytes 4325376 | tf_op jit(solution)/shard_map/pallas_call | solution.py:323
  46.8 1.9 %collective-permute-done.5.refs_2_.refs_6_ = bf16[528,256]{1,0:T(8,128)(2,1)S(1)} collective-permute-done((bf16[528,256]{1,0:T(8,128)(2,1)S(1)}, bf16[528,256]{1,0:T(8,128)(2,1)S(1)}, u32[]{:S(2)}, u32[]{:S(2)}) %collective-permute-start.5) | collective-permute-done | bytes 270368 | tf_op jit(solution)/shard_map/ppermute | solution.py:244
  48.7 2.3 %shard_map.114.refs_8_ = bf16[256,1024]{1,0:T(8,128)(2,1)S(1)} custom-call(s32[2]{0:T(128)S(1)} %pad_add_fusion.place_ref, bf16[1056,1024]{1,0:T(8,128)(2,1)S(1)} %bitcast.18, bf16[1056,1024]{1,0:T(8,128)(2,1)S(1)} %collective-permute-done.other_w, bf16[528,256]{1,0:T(8,128)(2,1)S(1)} %collective-permute-done.2.refs_0_.refs_4_, ...), custom_call_target="tpu_custom_call" | custom-call | flops 1107296256 | bytes 4325376 | tf_op jit(solution)/shard_map/pallas_call | solution.py:323
  51.0 2.5 %collective-permute-start.10 = (bf16[256,1024]{1,0:T(8,128)(2,1)S(1)}, bf16[256,1024]{1,0:T(8,128)(2,1)S(1)}, u32[]{:S(2)}, u32[]{:S(2)}) collective-permute-start(bf16[256,1024]{1,0:T(8,128)(2,1)S(1)} %shard_map.114.refs_8_), channel_id=1, source_target_pairs={{0,16},{8,24},{16,0},{24,8},{1,17},{9,25},{17,1},{25,9},{2,18},{10... | collective-permute-start | bytes 1572872 | tf_op jit(solution)/shard_map/ppermute | solution.py:247
  53.6 0.4 collective-permute-start.14
  54.0 0.4 collective-permute-done.11
  54.4 0.4 collective-permute-start.15
  54.7 5.3 %collective-permute-start.16 = (bf16[528,256]{1,0:T(8,128)(2,1)S(1)}, bf16[528,256]{1,0:T(8,128)(2,1)S(1)}, u32[]{:S(2)}, u32[]{:S(2)}) collective-permute-start(bf16[528,256]{1,0:T(8,128)(2,1)S(1)} %get-tuple-element.57), channel_id=1, source_target_pairs={{0,3},{1,2},{2,1},{3,0},{4,7},{5,6},{6,5},{7,4},{8,11},{9,10},{10,... | collective-permute-start | bytes 811016 | tf_op jit(solution)/shard_map/ppermute | solution.py:244
  60.1 0.2 collective-permute-done.13
  60.3 0.2 add_convert_fusion.1
  60.4 2.6 %collective-permute-start.17 = (bf16[528,256]{1,0:T(8,128)(2,1)S(1)}, bf16[528,256]{1,0:T(8,128)(2,1)S(1)}, u32[]{:S(2)}, u32[]{:S(2)}) collective-permute-start(bf16[528,256]{1,0:T(8,128)(2,1)S(1)} %add_convert_fusion.1), channel_id=1, source_target_pairs={{0,16},{8,24},{16,0},{24,8},{1,17},{9,25},{17,1},{25,9},{2,18},{10... | collective-permute-start | bytes 811016 | tf_op jit(solution)/shard_map/ppermute | solution.py:247
  63.0 4.0 %shard_map.116 = (f32[1056,1024]{1,0:T(8,128)S(1)}, bf16[1056,1024]{1,0:T(8,128)(2,1)S(1)}) custom-call(s32[2]{0:T(128)S(1)} %pad_add_fusion.place_ref, bf16[256,1024]{1,0:T(8,128)(2,1)} %get-tuple-element.48.context_own, bf16[256,1024]{1,0:T(8,128)(2,1)} %collective-permute-done.3.context_other, bf16[528,256]{1,0:T(8,128)(2,1)S(1)} %multiply_convert_fusion.refs_0_, ...), custom_call_target="tpu_custom_call" | custom-call | flops 2214592512 | bytes 6488064 | tf_op jit(solution)/shard_map/pallas_call | solution.py:349
  67.1 0.1 collective-permute-done.14
  67.2 3.0 %collective-permute-done.16 = bf16[528,256]{1,0:T(8,128)(2,1)S(1)} collective-permute-done((bf16[528,256]{1,0:T(8,128)(2,1)S(1)}, bf16[528,256]{1,0:T(8,128)(2,1)S(1)}, u32[]{:S(2)}, u32[]{:S(2)}) %collective-permute-start.16) | collective-permute-done | bytes 270368 | tf_op jit(solution)/shard_map/ppermute | solution.py:244
  70.2 0.2 add_convert_fusion
  70.3 0.1 collective-permute-start.23
  70.5 2.4 %shard_map.117 = (bf16[4,64,1024]{2,1,0:T(8,128)(2,1)}, bf16[4,2,64,128]{3,2,1,0:T(8,128)(2,1)S(1)}) custom-call(f32[256,1024]{1,0:T(8,128)S(1)} %shard_map.113.refs_4_.own_ref, bf16[256,1024]{1,0:T(8,128)(2,1)S(1)} %collective-permute-done.10.got_ref, bf16[4,64,1024]{2,1,0:T(8,128)(2,1)S(1)} %bitcast.20, bf16[4,2,64,128]{3,2,1,0:T(8,128)(2,1)S(1)} %copy-done.6, ...), custom_call_target="tpu_custom_call" | custom-call | flops 234881024 | bytes 4194304 | tf_op jit(solution)/shard_map/pallas_call | solution.py:368
  72.9 4.7 %collective-permute-start.22 = (bf16[512,128]{1,0:T(8,128)(2,1)S(1)}, bf16[512,128]{1,0:T(8,128)(2,1)S(1)}, u32[]{:S(2)}, u32[]{:S(2)}) collective-permute-start(bf16[512,128]{1,0:T(8,128)(2,1)S(1)} %bitcast.23), channel_id=1, source_target_pairs={{0,4},{1,5},{2,6},{3,7},{4,0},{5,1},{6,2},{7,3},{8,12},{9,13},{10,... | collective-permute-start | bytes 393224 | tf_op jit(solution)/shard_map/ppermute | solution.py:244
  77.6 2.6 %collective-permute-start.21 = (bf16[512,128]{1,0:T(8,128)(2,1)S(1)}, bf16[512,128]{1,0:T(8,128)(2,1)S(1)}, u32[]{:S(2)}, u32[]{:S(2)}) collective-permute-start(bf16[512,128]{1,0:T(8,128)(2,1)S(1)} %bitcast.24), channel_id=1, source_target_pairs={{0,3},{1,2},{2,1},{3,0},{4,7},{5,6},{6,5},{7,4},{8,11},{9,10},{10,... | collective-permute-start | bytes 393224 | tf_op jit(solution)/shard_map/ppermute | solution.py:244
  80.3 0.8 collective-permute-start.19
  81.2 0.1 collective-permute-start.18
  81.3 2.9 %add_bitcast_fusion = f32[1024,1056]{0,1:T(8,128)} fusion(f32[1056,1024]{1,0:T(8,128)S(1)} %get-tuple-element.68, bf16[1056,1024]{1,0:T(8,128)(2,1)S(1)} %collective-permute-done.23), kind=kLoop, calls=%fused_computation | loop fusion | flops 2162688 | bytes 10813440 | tf_op jit(solution)/shard_map/transpose | solution.py:378
  84.1 0.7 collective-permute-done.22.refs_4_
  84.9 1.9 %collective-permute-start.26 = (bf16[512,128]{1,0:T(8,128)(2,1)S(1)}, bf16[512,128]{1,0:T(8,128)(2,1)S(1)}, u32[]{:S(2)}, u32[]{:S(2)}) collective-permute-start(bf16[512,128]{1,0:T(8,128)(2,1)S(1)} %collective-permute-done.22.refs_4_), channel_id=1, source_target_pairs={{0,3},{1,2},{2,1},{3,0},{4,7},{5,6},{6,5},{7,4},{8,11},{9,10},{10,... | collective-permute-start | bytes 393224 | tf_op jit(solution)/shard_map/ppermute | solution.py:244
  86.8 3.3 %collective-permute-done.21.refs_3_ = bf16[512,128]{1,0:T(8,128)(2,1)S(1)} collective-permute-done((bf16[512,128]{1,0:T(8,128)(2,1)S(1)}, bf16[512,128]{1,0:T(8,128)(2,1)S(1)}, u32[]{:S(2)}, u32[]{:S(2)}) %collective-permute-start.21) | collective-permute-done | bytes 131104 | tf_op jit(solution)/shard_map/ppermute | solution.py:244
  90.1 1.9 %collective-permute-done.20.refs_2_ = bf16[512,128]{1,0:T(8,128)(2,1)S(1)} collective-permute-done((bf16[512,128]{1,0:T(8,128)(2,1)S(1)}, bf16[512,128]{1,0:T(8,128)(2,1)S(1)}, u32[]{:S(2)}, u32[]{:S(2)}) %collective-permute-start.20) | collective-permute-done | bytes 131104 | tf_op jit(solution)/shard_map/ppermute | solution.py:244
  92.0 1.5 %collective-permute-start.24 = (bf16[512,128]{1,0:T(8,128)(2,1)S(1)}, bf16[512,128]{1,0:T(8,128)(2,1)S(1)}, u32[]{:S(2)}, u32[]{:S(2)}) collective-permute-start(bf16[512,128]{1,0:T(8,128)(2,1)S(1)} %collective-permute-done.22.refs_4_), channel_id=1, source_target_pairs={{0,1},{1,0},{2,3},{3,2},{4,5},{5,4},{6,7},{7,6},{8,9},{9,8},{10,11... | collective-permute-start | bytes 393224 | tf_op jit(solution)/shard_map/ppermute | solution.py:244
  93.5 2.8 %collective-permute-done.18.got_ref = bf16[528,256]{1,0:T(8,128)(2,1)S(1)} collective-permute-done((bf16[528,256]{1,0:T(8,128)(2,1)S(1)}, bf16[528,256]{1,0:T(8,128)(2,1)S(1)}, u32[]{:S(2)}, u32[]{:S(2)}) %collective-permute-start.18) | collective-permute-done | bytes 270368 | tf_op jit(solution)/shard_map/ppermute | solution.py:244
  96.3 1.0 shard_map.118
  97.3 1.7 %collective-permute-done.25.refs_6_ = bf16[512,128]{1,0:T(8,128)(2,1)S(1)} collective-permute-done((bf16[512,128]{1,0:T(8,128)(2,1)S(1)}, bf16[512,128]{1,0:T(8,128)(2,1)S(1)}, u32[]{:S(2)}, u32[]{:S(2)}) %collective-permute-start.25) | collective-permute-done | bytes 131104 | tf_op jit(solution)/shard_map/ppermute | solution.py:244
  99.0 1.6 %shard_map.119 = bf16[512,1024]{1,0:T(8,128)(2,1)} custom-call(s32[2]{0:T(128)S(1)} %pad_add_fusion.place_ref, bf16[512,128]{1,0:T(8,128)(2,1)S(1)} %bitcast.27, bf16[512,128]{1,0:T(8,128)(2,1)S(1)} %collective-permute-done.19.refs_1_, bf16[512,128]{1,0:T(8,128)(2,1)S(1)} %collective-permute-done.20.refs_2_, ...), custom_call_target="tpu_custom_call" | custom-call | bytes 1048576 | tf_op jit(solution)/shard_map/pallas_call | solution.py:397
  (35 shorter events, 0.2 us)
Async XLA Ops:
  0.6 5.4 %copy-start = (bf16[1,4,2,64,1024]{4,3,2,1,0:T(8,128)(2,1)S(1)}, bf16[1,4,2,64,1024]{4,3,2,1,0:T(8,128)(2,1)}, u32[]{:S(2)}) copy-start(bf16[1,4,2,64,1024]{4,3,2,1,0:T(8,128)(2,1)} %param.9) | copy-start | bytes 3145732
  0.6 33.2 %collective-permute-start = (bf16[1056,1024]{1,0:T(8,128)(2,1)}, bf16[1056,1024]{1,0:T(8,128)(2,1)S(1)}, u32[]{:S(2)}, u32[]{:S(2)}) collective-permute-start(bf16[1056,1024]{1,0:T(8,128)(2,1)} %bitcast.15), channel_id=1, source_target_pairs={{0,8},{8,0},{16,24},{24,16},{1,9},{9,1},{17,25},{25,17},{2,10},{10... | collective-permute-start | bytes 6488072 | tf_op jit(solution)/shard_map/ppermute | solution.py:250
  1.2 1.0 copy-start.10
  2.3 16.7 %collective-permute-start.1 = (bf16[528,256]{1,0:T(8,128)(2,1)S(1)}, bf16[528,256]{1,0:T(8,128)(2,1)}, u32[]{:S(2)}, u32[]{:S(2)}) collective-permute-start(bf16[528,256]{1,0:T(8,128)(2,1)S(1)} %shard_map.111), channel_id=1, source_target_pairs={{0,4},{1,5},{2,6},{3,7},{4,0},{5,1},{6,2},{7,3},{8,12},{9,13},{10,... | collective-permute-start | bytes 811016 | tf_op jit(solution)/shard_map/ppermute | solution.py:244
  6.1 3.7 %copy-start.5 = (bf16[4,2,64,128]{3,2,1,0:T(8,128)(2,1)}, bf16[4,2,64,128]{3,2,1,0:T(8,128)(2,1)S(1)}, u32[]{:S(2)}) copy-start(bf16[4,2,64,128]{3,2,1,0:T(8,128)(2,1)S(1)} %dynamic-slice_bitcast_fusion.key_value_ref) | copy-start | bytes 393220
  6.1 1.1 %copy-start.3 = (bf16[1,4,64,1024]{3,2,1,0:T(8,128)(2,1)S(1)}, bf16[1,4,64,1024]{3,2,1,0:T(8,128)(2,1)}, u32[]{:S(2)}) copy-start(bf16[1,4,64,1024]{3,2,1,0:T(8,128)(2,1)} %param.8) | copy-start | bytes 1572868
  7.2 0.7 copy-start.11
  9.8 1.0 copy-start.7
  10.8 15.1 %collective-permute-start.3 = (bf16[256,1024]{1,0:T(8,128)(2,1)}, bf16[256,1024]{1,0:T(8,128)(2,1)}, u32[]{:S(2)}, u32[]{:S(2)}) collective-permute-start(bf16[256,1024]{1,0:T(8,128)(2,1)} %get-tuple-element.48.context_own), channel_id=1, source_target_pairs={{0,16},{8,24},{16,0},{24,8},{1,17},{9,25},{17,1},{25,9},{2,18},{10... | collective-permute-start | bytes 1572872 | tf_op jit(solution)/shard_map/ppermute | solution.py:247
  20.1 10.7 %collective-permute-start.2 = (bf16[528,256]{1,0:T(8,128)(2,1)S(1)}, bf16[528,256]{1,0:T(8,128)(2,1)S(1)}, u32[]{:S(2)}, u32[]{:S(2)}) collective-permute-start(bf16[528,256]{1,0:T(8,128)(2,1)S(1)} %multiply_convert_fusion.1), channel_id=1, source_target_pairs={{0,16},{8,24},{16,0},{24,8},{1,17},{9,25},{17,1},{25,9},{2,18},{10... | collective-permute-start | bytes 811016 | tf_op jit(solution)/shard_map/ppermute | solution.py:247
  20.8 12.6 %collective-permute-start.9 = (bf16[528,256]{1,0:T(8,128)(2,1)S(1)}, bf16[528,256]{1,0:T(8,128)(2,1)S(1)}, u32[]{:S(2)}, u32[]{:S(2)}) collective-permute-start(bf16[528,256]{1,0:T(8,128)(2,1)S(1)} %multiply_convert_fusion.refs_0_), channel_id=1, source_target_pairs={{0,3},{1,2},{2,1},{3,0},{4,7},{5,6},{6,5},{7,4},{8,11},{9,10},{10,... | collective-permute-start | bytes 811016 | tf_op jit(solution)/shard_map/ppermute | solution.py:244
  22.4 18.4 %collective-permute-start.8 = (bf16[528,256]{1,0:T(8,128)(2,1)S(1)}, bf16[528,256]{1,0:T(8,128)(2,1)S(1)}, u32[]{:S(2)}, u32[]{:S(2)}) collective-permute-start(bf16[528,256]{1,0:T(8,128)(2,1)S(1)} %multiply_convert_fusion.refs_0_), channel_id=1, source_target_pairs={{0,2},{1,3},{2,0},{3,1},{4,6},{5,7},{6,4},{7,5},{8,10},{9,11},{10,... | collective-permute-start | bytes 811016 | tf_op jit(solution)/shard_map/ppermute | solution.py:244
  25.9 16.6 %collective-permute-start.7 = (bf16[528,256]{1,0:T(8,128)(2,1)S(1)}, bf16[528,256]{1,0:T(8,128)(2,1)S(1)}, u32[]{:S(2)}, u32[]{:S(2)}) collective-permute-start(bf16[528,256]{1,0:T(8,128)(2,1)S(1)} %multiply_convert_fusion.refs_0_), channel_id=1, source_target_pairs={{0,1},{1,0},{2,3},{3,2},{4,5},{5,4},{6,7},{7,6},{8,9},{9,8},{10,11... | collective-permute-start | bytes 811016 | tf_op jit(solution)/shard_map/ppermute | solution.py:244
  30.8 13.2 %collective-permute-start.6 = (bf16[528,256]{1,0:T(8,128)(2,1)S(1)}, bf16[528,256]{1,0:T(8,128)(2,1)S(1)}, u32[]{:S(2)}, u32[]{:S(2)}) collective-permute-start(bf16[528,256]{1,0:T(8,128)(2,1)S(1)} %collective-permute-done.2.refs_0_.refs_4_), channel_id=1, source_target_pairs={{0,3},{1,2},{2,1},{3,0},{4,7},{5,6},{6,5},{7,4},{8,11},{9,10},{10,... | collective-permute-start | bytes 811016 | tf_op jit(solution)/shard_map/ppermute | solution.py:244
  33.4 15.3 %collective-permute-start.5 = (bf16[528,256]{1,0:T(8,128)(2,1)S(1)}, bf16[528,256]{1,0:T(8,128)(2,1)S(1)}, u32[]{:S(2)}, u32[]{:S(2)}) collective-permute-start(bf16[528,256]{1,0:T(8,128)(2,1)S(1)} %collective-permute-done.2.refs_0_.refs_4_), channel_id=1, source_target_pairs={{0,2},{1,3},{2,0},{3,1},{4,6},{5,7},{6,4},{7,5},{8,10},{9,11},{10,... | collective-permute-start | bytes 811016 | tf_op jit(solution)/shard_map/ppermute | solution.py:244
  33.8 14.8 %collective-permute-start.4 = (bf16[528,256]{1,0:T(8,128)(2,1)S(1)}, bf16[528,256]{1,0:T(8,128)(2,1)S(1)}, u32[]{:S(2)}, u32[]{:S(2)}) collective-permute-start(bf16[528,256]{1,0:T(8,128)(2,1)S(1)} %collective-permute-done.2.refs_0_.refs_4_), channel_id=1, source_target_pairs={{0,1},{1,0},{2,3},{3,2},{4,5},{5,4},{6,7},{7,6},{8,9},{9,8},{10,11... | collective-permute-start | bytes 811016 | tf_op jit(solution)/shard_map/ppermute | solution.py:244
  34.3 1.6 %copy-start.1 = (bf16[1024,1056]{0,1:T(8,128)(2,1)S(1)}, bf16[1024,1056]{0,1:T(8,128)(2,1)}, u32[]{:S(2)}) copy-start(bf16[1024,1056]{0,1:T(8,128)(2,1)} %param.13) | copy-start | bytes 6488068
  36.0 8.5 %copy-start.2 = (bf16[1024,1056]{0,1:T(8,128)(2,1)S(1)}, bf16[1024,1056]{0,1:T(8,128)(2,1)}, u32[]{:S(2)}) copy-start(bf16[1024,1056]{0,1:T(8,128)(2,1)} %param.13) | copy-start | bytes 6488068
  40.9 13.5 %collective-permute-start.11 = (bf16[528,256]{1,0:T(8,128)(2,1)S(1)}, bf16[528,256]{1,0:T(8,128)(2,1)S(1)}, u32[]{:S(2)}, u32[]{:S(2)}) collective-permute-start(bf16[528,256]{1,0:T(8,128)(2,1)S(1)} %get-tuple-element.45), channel_id=1, source_target_pairs={{0,1},{1,0},{2,3},{3,2},{4,5},{5,4},{6,7},{7,6},{8,9},{9,8},{10,11... | collective-permute-start | bytes 811016 | tf_op jit(solution)/shard_map/ppermute | solution.py:244
  42.4 12.3 %collective-permute-start.12 = (bf16[528,256]{1,0:T(8,128)(2,1)S(1)}, bf16[528,256]{1,0:T(8,128)(2,1)S(1)}, u32[]{:S(2)}, u32[]{:S(2)}) collective-permute-start(bf16[528,256]{1,0:T(8,128)(2,1)S(1)} %get-tuple-element.46), channel_id=1, source_target_pairs={{0,2},{1,3},{2,0},{3,1},{4,6},{5,7},{6,4},{7,5},{8,10},{9,11},{10,... | collective-permute-start | bytes 811016 | tf_op jit(solution)/shard_map/ppermute | solution.py:244
  44.0 16.2 %collective-permute-start.13 = (bf16[528,256]{1,0:T(8,128)(2,1)S(1)}, bf16[528,256]{1,0:T(8,128)(2,1)S(1)}, u32[]{:S(2)}, u32[]{:S(2)}) collective-permute-start(bf16[528,256]{1,0:T(8,128)(2,1)S(1)} %get-tuple-element.47), channel_id=1, source_target_pairs={{0,3},{1,2},{2,1},{3,0},{4,7},{5,6},{6,5},{7,4},{8,11},{9,10},{10,... | collective-permute-start | bytes 811016 | tf_op jit(solution)/shard_map/ppermute | solution.py:244
  51.0 19.3 %collective-permute-start.10 = (bf16[256,1024]{1,0:T(8,128)(2,1)S(1)}, bf16[256,1024]{1,0:T(8,128)(2,1)S(1)}, u32[]{:S(2)}, u32[]{:S(2)}) collective-permute-start(bf16[256,1024]{1,0:T(8,128)(2,1)S(1)} %shard_map.114.refs_8_), channel_id=1, source_target_pairs={{0,16},{8,24},{16,0},{24,8},{1,17},{9,25},{17,1},{25,9},{2,18},{10... | collective-permute-start | bytes 1572872 | tf_op jit(solution)/shard_map/ppermute | solution.py:247
  53.6 13.6 %collective-permute-start.14 = (bf16[528,256]{1,0:T(8,128)(2,1)S(1)}, bf16[528,256]{1,0:T(8,128)(2,1)S(1)}, u32[]{:S(2)}, u32[]{:S(2)}) collective-permute-start(bf16[528,256]{1,0:T(8,128)(2,1)S(1)} %get-tuple-element.55), channel_id=1, source_target_pairs={{0,1},{1,0},{2,3},{3,2},{4,5},{5,4},{6,7},{7,6},{8,9},{9,8},{10,11... | collective-permute-start | bytes 811016 | tf_op jit(solution)/shard_map/ppermute | solution.py:244
  54.4 12.8 %collective-permute-start.15 = (bf16[528,256]{1,0:T(8,128)(2,1)S(1)}, bf16[528,256]{1,0:T(8,128)(2,1)S(1)}, u32[]{:S(2)}, u32[]{:S(2)}) collective-permute-start(bf16[528,256]{1,0:T(8,128)(2,1)S(1)} %get-tuple-element.56), channel_id=1, source_target_pairs={{0,2},{1,3},{2,0},{3,1},{4,6},{5,7},{6,4},{7,5},{8,10},{9,11},{10,... | collective-permute-start | bytes 811016 | tf_op jit(solution)/shard_map/ppermute | solution.py:244
  54.7 15.4 %collective-permute-start.16 = (bf16[528,256]{1,0:T(8,128)(2,1)S(1)}, bf16[528,256]{1,0:T(8,128)(2,1)S(1)}, u32[]{:S(2)}, u32[]{:S(2)}) collective-permute-start(bf16[528,256]{1,0:T(8,128)(2,1)S(1)} %get-tuple-element.57), channel_id=1, source_target_pairs={{0,3},{1,2},{2,1},{3,0},{4,7},{5,6},{6,5},{7,4},{8,11},{9,10},{10,... | collective-permute-start | bytes 811016 | tf_op jit(solution)/shard_map/ppermute | solution.py:244
  60.4 10.0 %copy-start.4 = (bf16[1,4,64,1024]{3,2,1,0:T(8,128)(2,1)S(1)}, bf16[1,4,64,1024]{3,2,1,0:T(8,128)(2,1)}, u32[]{:S(2)}) copy-start(bf16[1,4,64,1024]{3,2,1,0:T(8,128)(2,1)} %param.8) | copy-start | bytes 1572868
  60.4 10.0 %copy-start.6 = (bf16[4,2,64,128]{3,2,1,0:T(8,128)(2,1)S(1)}, bf16[4,2,64,128]{3,2,1,0:T(8,128)(2,1)}, u32[]{:S(2)}) copy-start(bf16[4,2,64,128]{3,2,1,0:T(8,128)(2,1)} %copy-done.5) | copy-start | bytes 393220
  60.4 10.0 %copy-start.8 = (f32[4,512,64]{2,1,0:T(8,128)S(1)}, f32[4,512,64]{2,1,0:T(8,128)}, u32[]{:S(2)}) copy-start(f32[4,512,64]{2,1,0:T(8,128)} %copy-done.7) | copy-start | bytes 1572868
  60.4 9.9 %collective-permute-start.17 = (bf16[528,256]{1,0:T(8,128)(2,1)S(1)}, bf16[528,256]{1,0:T(8,128)(2,1)S(1)}, u32[]{:S(2)}, u32[]{:S(2)}) collective-permute-start(bf16[528,256]{1,0:T(8,128)(2,1)S(1)} %add_convert_fusion.1), channel_id=1, source_target_pairs={{0,16},{8,24},{16,0},{24,8},{1,17},{9,25},{17,1},{25,9},{2,18},{10... | collective-permute-start | bytes 811016 | tf_op jit(solution)/shard_map/ppermute | solution.py:247
  70.3 10.8 %collective-permute-start.23 = (bf16[1056,1024]{1,0:T(8,128)(2,1)S(1)}, bf16[1056,1024]{1,0:T(8,128)(2,1)S(1)}, u32[]{:S(2)}, u32[]{:S(2)}) collective-permute-start(bf16[1056,1024]{1,0:T(8,128)(2,1)S(1)} %get-tuple-element.69), channel_id=1, source_target_pairs={{0,8},{8,0},{16,24},{24,16},{1,9},{9,1},{17,25},{25,17},{2,10},{10... | collective-permute-start | bytes 6488072 | tf_op jit(solution)/shard_map/ppermute | solution.py:250
  72.9 12.0 %collective-permute-start.22 = (bf16[512,128]{1,0:T(8,128)(2,1)S(1)}, bf16[512,128]{1,0:T(8,128)(2,1)S(1)}, u32[]{:S(2)}, u32[]{:S(2)}) collective-permute-start(bf16[512,128]{1,0:T(8,128)(2,1)S(1)} %bitcast.23), channel_id=1, source_target_pairs={{0,4},{1,5},{2,6},{3,7},{4,0},{5,1},{6,2},{7,3},{8,12},{9,13},{10,... | collective-permute-start | bytes 393224 | tf_op jit(solution)/shard_map/ppermute | solution.py:244
  77.6 12.5 %collective-permute-start.21 = (bf16[512,128]{1,0:T(8,128)(2,1)S(1)}, bf16[512,128]{1,0:T(8,128)(2,1)S(1)}, u32[]{:S(2)}, u32[]{:S(2)}) collective-permute-start(bf16[512,128]{1,0:T(8,128)(2,1)S(1)} %bitcast.24), channel_id=1, source_target_pairs={{0,3},{1,2},{2,1},{3,0},{4,7},{5,6},{6,5},{7,4},{8,11},{9,10},{10,... | collective-permute-start | bytes 393224 | tf_op jit(solution)/shard_map/ppermute | solution.py:244
  80.3 11.7 %collective-permute-start.20 = (bf16[512,128]{1,0:T(8,128)(2,1)S(1)}, bf16[512,128]{1,0:T(8,128)(2,1)S(1)}, u32[]{:S(2)}, u32[]{:S(2)}) collective-permute-start(bf16[512,128]{1,0:T(8,128)(2,1)S(1)} %bitcast.25), channel_id=1, source_target_pairs={{0,2},{1,3},{2,0},{3,1},{4,6},{5,7},{6,4},{7,5},{8,10},{9,11},{10,... | collective-permute-start | bytes 393224 | tf_op jit(solution)/shard_map/ppermute | solution.py:244
  80.3 13.2 %collective-permute-start.19 = (bf16[512,128]{1,0:T(8,128)(2,1)S(1)}, bf16[512,128]{1,0:T(8,128)(2,1)S(1)}, u32[]{:S(2)}, u32[]{:S(2)}) collective-permute-start(bf16[512,128]{1,0:T(8,128)(2,1)S(1)} %bitcast.26), channel_id=1, source_target_pairs={{0,1},{1,0},{2,3},{3,2},{4,5},{5,4},{6,7},{7,6},{8,9},{9,8},{10,11... | collective-permute-start | bytes 393224 | tf_op jit(solution)/shard_map/ppermute | solution.py:244
  81.2 15.1 %collective-permute-start.18 = (bf16[528,256]{1,0:T(8,128)(2,1)S(1)}, bf16[528,256]{1,0:T(8,128)(2,1)S(1)}, u32[]{:S(2)}, u32[]{:S(2)}) collective-permute-start(bf16[528,256]{1,0:T(8,128)(2,1)S(1)} %get-tuple-element.75), channel_id=1, source_target_pairs={{0,4},{1,5},{2,6},{3,7},{4,0},{5,1},{6,2},{7,3},{8,12},{9,13},{10,... | collective-permute-start | bytes 811016 | tf_op jit(solution)/shard_map/ppermute | solution.py:244
  81.2 15.1 %copy-start.9 = (bf16[1,4,64,528]{3,2,1,0:T(8,128)(2,1)S(1)}, bf16[1,4,64,528]{3,2,1,0:T(8,128)(2,1)}, u32[]{:S(2)}) copy-start(bf16[1,4,64,528]{3,2,1,0:T(8,128)(2,1)} %param.11) | copy-start | bytes 811012
  84.9 12.4 %collective-permute-start.26 = (bf16[512,128]{1,0:T(8,128)(2,1)S(1)}, bf16[512,128]{1,0:T(8,128)(2,1)S(1)}, u32[]{:S(2)}, u32[]{:S(2)}) collective-permute-start(bf16[512,128]{1,0:T(8,128)(2,1)S(1)} %collective-permute-done.22.refs_4_), channel_id=1, source_target_pairs={{0,3},{1,2},{2,1},{3,0},{4,7},{5,6},{6,5},{7,4},{8,11},{9,10},{10,... | collective-permute-start | bytes 393224 | tf_op jit(solution)/shard_map/ppermute | solution.py:244
  90.1 8.9 %collective-permute-start.25 = (bf16[512,128]{1,0:T(8,128)(2,1)S(1)}, bf16[512,128]{1,0:T(8,128)(2,1)S(1)}, u32[]{:S(2)}, u32[]{:S(2)}) collective-permute-start(bf16[512,128]{1,0:T(8,128)(2,1)S(1)} %collective-permute-done.22.refs_4_), channel_id=1, source_target_pairs={{0,2},{1,3},{2,0},{3,1},{4,6},{5,7},{6,4},{7,5},{8,10},{9,11},{10,... | collective-permute-start | bytes 393224 | tf_op jit(solution)/shard_map/ppermute | solution.py:244
  92.0 7.0 %collective-permute-start.24 = (bf16[512,128]{1,0:T(8,128)(2,1)S(1)}, bf16[512,128]{1,0:T(8,128)(2,1)S(1)}, u32[]{:S(2)}, u32[]{:S(2)}) collective-permute-start(bf16[512,128]{1,0:T(8,128)(2,1)S(1)} %collective-permute-done.22.refs_4_), channel_id=1, source_target_pairs={{0,1},{1,0},{2,3},{3,2},{4,5},{5,4},{6,7},{7,6},{8,9},{9,8},{10,11... | collective-permute-start | bytes 393224 | tf_op jit(solution)/shard_map/ppermute | solution.py:244
